TPU v7x, 32 devices: a whole 2x2x4 slice. The times are simulated.
32 devices in a mesh: dp: 8 (over y, x, core), tensor: 4 (over z).
Axes of the slice: x: 2, y: 2, z: 4, core: 2. Of those that a mesh axis runs over, the one named last changes fastest.
Arguments:
- tokens: bfloat16 [8192, 2048], P('dp', 'tensor'), may hold values from -6 to 6
- lengths: int32 [8], P('dp'), may hold values from 256 to 1024, as said below
- cotangent: bfloat16 [8192, 2048], P('dp', 'tensor'), may hold values from -6 to 6
- first_gain: float32 [2048], replicated, may hold values from 0.25 to 1.75
- query_weight: bfloat16 [2048, 2048], P(None, 'tensor'), may hold values from -0.125 to 0.125
- key_weight: bfloat16 [2048, 1024], P(None, 'tensor'), may hold values from -0.125 to 0.125
- value_weight: bfloat16 [2048, 1024], P(None, 'tensor'), may hold values from -0.125 to 0.125
- query_gain: float32 [128], replicated, may hold values from 0.25 to 1.75
- key_gain: float32 [128], replicated, may hold values from 0.25 to 1.75
- out_weight: bfloat16 [2048, 2048], P('tensor'), may hold values from -1.5 to 1.5
- second_gain: float32 [2048], replicated, may hold values from 0.25 to 1.75
- gate_weight: bfloat16 [2048, 6144], P(None, 'tensor'), may hold values from -0.125 to 0.125
- up_weight: bfloat16 [2048, 6144], P(None, 'tensor'), may hold values from -0.125 to 0.125
- down_weight: bfloat16 [6144, 2048], P('tensor'), may hold values from -0.078125 to 0.078125
Outputs:
- block_out: bfloat16 [8192, 2048], P('dp', 'tensor')
- token_grad: bfloat16 [8192, 2048], P('dp', 'tensor')
- first_gain_grad: float32 [2048], P('tensor')
- query_weight_grad: float32 [2048, 2048], P(None, 'tensor')
- key_weight_grad: float32 [2048, 1024], P(None, 'tensor')
- value_weight_grad: float32 [2048, 1024], P(None, 'tensor')
- query_gain_grad: float32 [128], replicated
- key_gain_grad: float32 [128], replicated
- out_weight_grad: float32 [2048, 2048], P('tensor')
- second_gain_grad: float32 [2048], P('tensor')
- gate_weight_grad: float32 [2048, 6144], P(None, 'tensor')
- up_weight_grad: float32 [2048, 6144], P(None, 'tensor')
- down_weight_grad: float32 [6144, 2048], P('tensor')
Inputs may be any that keep to these rules, and one draw needn't show every extreme that they name: `lengths`: each sequence's number of valid tokens, all at its start; in every draw some sequence has exactly 1024.
All inputs are finite; a program needn't handle non-finite values.
Results may differ from a plain program's by a relative error of at most 0.024.
Values may be sent and summed in bfloat16 or wider, within the bound.
No kernel may reach another device: no remote copies, remote signals or barrier semaphores. Data moves between devices by JAX's collectives and lax.ppermute only.
A program may use at most 192 MiB of HBM per device.

v0:
```python
from functools import partial

import jax
import jax.numpy as jnp
from jax import lax
from jax.sharding import PartitionSpec as P

EPSILON = 1e-06
ROPE_BASE = 1000000.0


def norm_rows(values, gain):
    factor = lax.rsqrt(jnp.mean(values * values, axis=-1, keepdims=True) + EPSILON)
    return values * factor * gain


def rope_tables(seq_len, head_dim):
    half_dim = head_dim // 2
    frequency = ROPE_BASE ** (-(jnp.arange(half_dim, dtype=jnp.float32) * 2.0 / head_dim))
    angles = jnp.arange(seq_len, dtype=jnp.float32)[:, None] * frequency[None, :]
    angles = jnp.concatenate([angles, angles], axis=1)
    return (jnp.cos(angles)[:, None, :], jnp.sin(angles)[:, None, :])


def rotate(values, cosine_table, sine_table):
    half_dim = values.shape[-1] // 2
    turned = jnp.concatenate([-values[..., half_dim:], values[..., :half_dim]], axis=-1)
    return values * cosine_table + turned * sine_table


def head_post(raw_heads, gain, cosine_table, sine_table):
    return rotate(norm_rows(raw_heads, gain), cosine_table, sine_table)


def mask_table(row_start, block_rows, seq_len, length):
    positions = jnp.arange(seq_len, dtype=jnp.int32)
    row_index = row_start + jnp.arange(block_rows, dtype=jnp.int32)
    return (positions[None, :] <= row_index[:, None]) & (positions[None, :] < length)


def local(
    tokens,
    lengths,
    cotangent,
    first_gain,
    query_weight,
    key_weight,
    value_weight,
    query_gain,
    key_gain,
    out_weight,
    second_gain,
    gate_weight,
    up_weight,
    down_weight,
):
    tensor_rank = lax.axis_index("tensor")
    seq_len = tokens.shape[0]
    share_width = tokens.shape[1]
    model_width = first_gain.shape[0]
    head_dim = query_gain.shape[0]
    local_heads = query_weight.shape[1] // head_dim
    local_groups = key_weight.shape[1] // head_dim
    group_size = local_heads // local_groups
    block_rows = min(512, seq_len)
    block_count = seq_len // block_rows
    score_scale = head_dim ** (-0.5)
    length = lengths[0]
    valid_rows = (jnp.arange(seq_len, dtype=jnp.int32) < length).astype(jnp.float32)[:, None]
    own_start = tensor_rank * share_width
    first_own = lax.dynamic_slice_in_dim(first_gain, own_start, share_width, 0)
    second_own = lax.dynamic_slice_in_dim(second_gain, own_start, share_width, 0)
    full_tokens, full_cot = (
        lax.all_gather(tokens, "tensor", axis=1, tiled=True),
        lax.all_gather(cotangent, "tensor", axis=1, tiled=True),
    )
    token_rows = full_tokens.astype(jnp.float32)
    token_own = tokens.astype(jnp.float32)
    first_root = lax.rsqrt(jnp.mean(token_rows * token_rows, axis=1, keepdims=True) + EPSILON)
    normed = (token_rows * first_root * first_gain).astype(jnp.bfloat16)
    query_raw = jnp.dot(normed, query_weight, preferred_element_type=jnp.float32).reshape(
        seq_len, local_heads, head_dim
    )
    key_raw = jnp.dot(normed, key_weight, preferred_element_type=jnp.float32).reshape(
        seq_len, local_groups, head_dim
    )
    value_rows = (
        jnp.dot(normed, value_weight, preferred_element_type=jnp.float32)
        .astype(jnp.bfloat16)
        .reshape(seq_len, local_groups, head_dim)
    )
    cosine_table, sine_table = rope_tables(seq_len, head_dim)
    rotated = partial(head_post, cosine_table=cosine_table, sine_table=sine_table)
    query_rot, query_pull = jax.vjp(rotated, query_raw, query_gain)
    key_rot, key_pull = jax.vjp(rotated, key_raw, key_gain)
    query_rows = query_rot.astype(jnp.bfloat16).reshape(seq_len, local_groups, group_size, head_dim)
    key_rows = key_rot.astype(jnp.bfloat16)

    def block_scores(row_start):
        query_block = lax.dynamic_slice_in_dim(query_rows, row_start, block_rows, 0)
        scores = (
            jnp.einsum("qcgd,kcd->cgqk", query_block, key_rows, preferred_element_type=jnp.float32)
            * score_scale
        )
        allowed = mask_table(row_start, block_rows, seq_len, length)
        return (query_block, jnp.where(allowed[None, None], scores, -1e30))

    def attend(row_start):
        query_block, scores = block_scores(row_start)
        highest = jnp.max(scores, axis=-1, keepdims=True)
        raised = jnp.exp(scores - highest)
        row_total = jnp.sum(raised, axis=-1, keepdims=True)
        weights = (raised / row_total).astype(jnp.bfloat16)
        block_out = jnp.einsum(
            "cgqk,kcd->qcgd", weights, value_rows, preferred_element_type=jnp.float32
        )
        return (block_out, highest + jnp.log(row_total))

    starts = jnp.arange(block_count, dtype=jnp.int32) * block_rows
    attended, log_totals = lax.map(attend, starts)
    attended = attended.reshape(seq_len, local_heads * head_dim).astype(jnp.bfloat16)
    branch = jnp.dot(attended, out_weight, preferred_element_type=jnp.float32)
    hidden_rows = token_rows + lax.psum(branch.astype(jnp.bfloat16), "tensor").astype(jnp.float32)
    hidden_own = lax.dynamic_slice_in_dim(hidden_rows, own_start, share_width, 1)
    second_root = lax.rsqrt(jnp.mean(hidden_rows * hidden_rows, axis=1, keepdims=True) + EPSILON)
    mixed_rows = (hidden_rows * second_root * second_gain).astype(jnp.bfloat16)
    gate_value = jnp.dot(mixed_rows, gate_weight, preferred_element_type=jnp.float32)
    up_value = jnp.dot(mixed_rows, up_weight, preferred_element_type=jnp.float32)
    sigmoid_gate = jax.nn.sigmoid(gate_value)
    activated = gate_value * sigmoid_gate
    product = (activated * up_value).astype(jnp.bfloat16)
    down_part = jnp.dot(product, down_weight, preferred_element_type=jnp.float32)
    down_own = lax.psum_scatter(
        down_part.astype(jnp.bfloat16), "tensor", scatter_dimension=1, tiled=True
    ).astype(jnp.float32)
    layer_out = (hidden_own + down_own).astype(jnp.bfloat16)
    grad_full = (full_cot.astype(jnp.float32) * valid_rows).astype(jnp.bfloat16)
    grad_own = cotangent.astype(jnp.float32) * valid_rows
    grad_down = jnp.einsum("sf,sd->fd", product, grad_full, preferred_element_type=jnp.float32)
    grad_product = jnp.einsum(
        "sd,fd->sf", grad_full, down_weight, preferred_element_type=jnp.float32
    )
    silu_slope = sigmoid_gate * (1.0 + gate_value * (1.0 - sigmoid_gate))
    grad_gate_value = (grad_product * up_value * silu_slope).astype(jnp.bfloat16)
    grad_up_value = (grad_product * activated).astype(jnp.bfloat16)
    grad_gate = jnp.einsum(
        "sd,sf->df", mixed_rows, grad_gate_value, preferred_element_type=jnp.float32
    )
    grad_up = jnp.einsum("sd,sf->df", mixed_rows, grad_up_value, preferred_element_type=jnp.float32)
    mixed_grad = jnp.einsum(
        "sf,df->sd", grad_gate_value, gate_weight, preferred_element_type=jnp.float32
    ) + jnp.einsum("sf,df->sd", grad_up_value, up_weight, preferred_element_type=jnp.float32)
    mixed_full_grad = lax.psum(mixed_grad.astype(jnp.bfloat16), "tensor").astype(jnp.float32)
    mid_term = jnp.sum(mixed_full_grad * second_gain * hidden_rows, axis=1, keepdims=True)
    mixed_own_grad = lax.dynamic_slice_in_dim(mixed_full_grad, own_start, share_width, 1)
    second_gain_grad = jnp.sum(mixed_own_grad * hidden_own * second_root, axis=0)
    hidden_grad = (
        grad_own
        + mixed_own_grad * second_own * second_root
        - hidden_own * second_root**3 / model_width * mid_term
    )
    hidden_grad_rows = lax.all_gather(
        hidden_grad.astype(jnp.bfloat16), "tensor", axis=1, tiled=True
    )
    grad_out = jnp.einsum(
        "sh,sd->hd", attended, hidden_grad_rows, preferred_element_type=jnp.float32
    )
    attended_grad = (
        jnp.einsum("sd,hd->sh", hidden_grad_rows, out_weight, preferred_element_type=jnp.float32)
        .astype(jnp.bfloat16)
        .reshape(seq_len, local_groups, group_size, head_dim)
    )

    def attend_back(running, row_start):
        key_sum, value_sum = running
        query_block, scores = block_scores(row_start)
        block_index = row_start // block_rows
        weights = jnp.exp(scores - log_totals[block_index])
        grad_block = lax.dynamic_slice_in_dim(attended_grad, row_start, block_rows, 0)
        weight_grad = jnp.einsum(
            "qcgd,kcd->cgqk", grad_block, value_rows, preferred_element_type=jnp.float32
        )
        centre = jnp.sum(weights * weight_grad, axis=-1, keepdims=True)
        score_grad = (weights * (weight_grad - centre)).astype(jnp.bfloat16)
        value_sum = value_sum + jnp.einsum(
            "cgqk,qcgd->kcd",
            weights.astype(jnp.bfloat16),
            grad_block,
            preferred_element_type=jnp.float32,
        )
        key_sum = (
            key_sum
            + jnp.einsum(
                "cgqk,qcgd->kcd", score_grad, query_block, preferred_element_type=jnp.float32
            )
            * score_scale
        )
        query_grad = (
            jnp.einsum("cgqk,kcd->qcgd", score_grad, key_rows, preferred_element_type=jnp.float32)
            * score_scale
        )
        return ((key_sum, value_sum), query_grad)

    empty_groups = jnp.zeros((seq_len, local_groups, head_dim), jnp.float32)
    (key_grad_rot, value_grad), query_blocks = lax.scan(
        attend_back, (empty_groups, empty_groups), starts
    )
    query_grad_rot = query_blocks.reshape(seq_len, local_heads, head_dim)
    query_raw_grad, query_gain_grad = query_pull(query_grad_rot)
    key_raw_grad, key_gain_grad = key_pull(key_grad_rot)
    query_raw_grad = query_raw_grad.reshape(seq_len, local_heads * head_dim).astype(jnp.bfloat16)
    key_raw_grad = key_raw_grad.reshape(seq_len, local_groups * head_dim).astype(jnp.bfloat16)
    value_raw_grad = value_grad.reshape(seq_len, local_groups * head_dim).astype(jnp.bfloat16)
    grad_query = jnp.einsum("sd,sh->dh", normed, query_raw_grad, preferred_element_type=jnp.float32)
    grad_key = jnp.einsum("sd,sh->dh", normed, key_raw_grad, preferred_element_type=jnp.float32)
    grad_value = jnp.einsum("sd,sh->dh", normed, value_raw_grad, preferred_element_type=jnp.float32)
    normed_grad = jnp.einsum(
        "sh,dh->sd", query_raw_grad, query_weight, preferred_element_type=jnp.float32
    )
    normed_grad = normed_grad + jnp.einsum(
        "sh,dh->sd", key_raw_grad, key_weight, preferred_element_type=jnp.float32
    )
    normed_grad = normed_grad + jnp.einsum(
        "sh,dh->sd", value_raw_grad, value_weight, preferred_element_type=jnp.float32
    )
    normed_own_grad = lax.psum_scatter(
        normed_grad.astype(jnp.bfloat16), "tensor", scatter_dimension=1, tiled=True
    ).astype(jnp.float32)
    first_term, query_gain_grad, key_gain_grad = lax.psum(
        (
            jnp.sum(normed_own_grad * first_own * token_own, axis=1, keepdims=True),
            query_gain_grad,
            key_gain_grad,
        ),
        "tensor",
    )
    first_gain_grad = jnp.sum(normed_own_grad * token_own * first_root, axis=0)
    token_grad = (
        hidden_grad
        + normed_own_grad * first_own * first_root
        - token_own * first_root**3 / model_width * first_term
    ).astype(jnp.bfloat16)
    (
        grad_query,
        grad_key,
        grad_value,
        grad_out,
        grad_gate,
        grad_up,
        grad_down,
        first_gain_grad,
        second_gain_grad,
        query_gain_grad,
        key_gain_grad,
    ) = (
        lax.psum(grad_query.astype(jnp.bfloat16), "dp").astype(jnp.float32),
        lax.psum(grad_key.astype(jnp.bfloat16), "dp").astype(jnp.float32),
        lax.psum(grad_value.astype(jnp.bfloat16), "dp").astype(jnp.float32),
        lax.psum(grad_out.astype(jnp.bfloat16), "dp").astype(jnp.float32),
        lax.psum(grad_gate.astype(jnp.bfloat16), "dp").astype(jnp.float32),
        lax.psum(grad_up.astype(jnp.bfloat16), "dp").astype(jnp.float32),
        lax.psum(grad_down.astype(jnp.bfloat16), "dp").astype(jnp.float32),
        lax.psum(first_gain_grad.astype(jnp.bfloat16), "dp").astype(jnp.float32),
        lax.psum(second_gain_grad.astype(jnp.bfloat16), "dp").astype(jnp.float32),
        lax.psum(query_gain_grad.astype(jnp.bfloat16), "dp").astype(jnp.float32),
        lax.psum(key_gain_grad.astype(jnp.bfloat16), "dp").astype(jnp.float32),
    )
    return (
        layer_out,
        token_grad,
        first_gain_grad,
        grad_query,
        grad_key,
        grad_value,
        query_gain_grad,
        key_gain_grad,
        grad_out,
        second_gain_grad,
        grad_gate,
        grad_up,
        grad_down,
    )


def solution(mesh):
    in_specs = (
        P("dp", "tensor"),
        P("dp"),
        P("dp", "tensor"),
        P(),
        P(None, "tensor"),
        P(None, "tensor"),
        P(None, "tensor"),
        P(),
        P(),
        P("tensor", None),
        P(),
        P(None, "tensor"),
        P(None, "tensor"),
        P("tensor", None),
    )
    out_specs = (
        P("dp", "tensor"),
        P("dp", "tensor"),
        P("tensor"),
        P(None, "tensor"),
        P(None, "tensor"),
        P(None, "tensor"),
        P(),
        P(),
        P("tensor", None),
        P("tensor"),
        P(None, "tensor"),
        P(None, "tensor"),
        P("tensor", None),
    )
    return jax.shard_map(local, mesh=mesh, in_specs=in_specs, out_specs=out_specs, check_vma=False)
```

profile of v0, /device:TPU:0, one launch (start us, length us, event | category | flops | bytes accessed | tf_op | source)
XLA Modules:
  0.0 1266.7 jit_solution(3216866973546808250)
XLA Ops:
  12.5 80.6 %all-gather.4.cloned.1.call-done = bf16[1024,2048]{1,0:T(8,128)(2,1)} async-done(((bf16[1024,512]{1,0:T(8,128)(2,1)}), bf16[1024,2048]{1,0:T(8,128)(2,1)}) %all-gather.4.cloned.1.call-update) | async-done | bytes 4194320 | tf_op jit(solution)/shard_map/all_gather | solution.py:74
  109.6 5.9 multiply_reduce_fusion.5
  127.8 28.9 %while.29 = (s32[]{:T(128)}, bf16[2,512,2,2,128]{4,1,3,2,0:T(8,128)(2,1)}, f32[2,2,2,512,1]{3,2,1,4,0:T(2,128)S(1)}, s32[2]{0:T(128)S(1)}, s32[]{:T(128)}, /*ind...) while((s32[]{:T(128)}, ...), condition=%wide.region_6.7_spmd, body=%wide.region_3.6_spmd.sunk | while | flops 1099955712 | bytes 38344944 | solution.py:120
  162.6 6.3 convolution_convert_fusion.4
  170.4 152.2 %all-reduce.11.cloned.1.call-done = bf16[1024,2048]{1,0:T(8,128)(2,1)} async-done(((bf16[1024,2048]{1,0:T(8,128)(2,1)}), bf16[1024,2048]{1,0:T(8,128)(2,1)}) %all-reduce.11.cloned.1.call-update) | async-done | bytes 4194320 | tf_op jit(solution)/shard_map/psum | solution.py:123
  322.6 5.0 multiply_reduce_fusion.1
  331.4 12.0 fusion.76
  343.4 8.5 fusion.75
  351.9 52.1 %all-gather.6.cloned.1.call-done = bf16[1024,2048]{1,0:T(8,128)(2,1)} async-done(((bf16[1024,512]{1,0:T(8,128)(2,1)}), bf16[1024,2048]{1,0:T(8,128)(2,1)}) %all-gather.6.cloned.1.call-update) | async-done | bytes 4194320 | tf_op jit(solution)/shard_map/all_gather | solution.py:75
  404.1 17.0 %multiply_convert_fusion.2 = (bf16[1024,1536]{1,0:T(8,128)(2,1)}, bf16[1024,1536]{1,0:T(8,128)(2,1)S(1)}, bf16[1024,1536]{1,0:T(8,128)(2,1)}) fusion(f32[1024,1536]{1,0:T(8,128)} %fusion.75, f32[1024,1536]{1,0:T(8,128)} %fusion.76, bf16[1536,2048]{1,0:T(8,128)(2,1)} %param.31, bf16[1024,2048]{1,0:T(8,128)(2,1)} %all-gather.6.cloned.1.call-done, ...), kind=kOutput, calls=%fused_computation.75 | convolution fusion | flops 6472335360 | bytes 32509952 | tf_op jit(solution)/shard_map/sd,fd->sf/dot_general | solution.py:140
  421.1 10.3 fusion.77
  431.4 11.1 add_convert_fusion.1
  442.6 11.0 convolution_convert_fusion.3
  453.8 142.4 %all-reduce.13.cloned.1.call-done = bf16[1024,2048]{1,0:T(8,128)(2,1)} async-done(((bf16[1024,2048]{1,0:T(8,128)(2,1)}), bf16[1024,2048]{1,0:T(8,128)(2,1)}) %all-reduce.13.cloned.1.call-update) | async-done | bytes 4194320 | tf_op jit(solution)/shard_map/psum | solution.py:153
  596.2 7.7 convert_element_type.209
  605.4 4.3 multiply_reduce_fusion
  609.8 65.0 %reduce-scatter.3.cloned.1.call-done = bf16[1024,512]{1,0:T(8,128)(2,1)} async-done(((bf16[1024,2048]{1,0:T(8,128)(2,1)}), bf16[1024,512]{1,0:T(8,128)(2,1)}) %reduce-scatter.3.cloned.1.call-update) | async-done | bytes 1048592 | tf_op jit(solution)/shard_map/reduce_scatter | solution.py:133
  674.8 5.0 fusion.72
  679.9 81.3 %all-gather.8.cloned.1.call-done = bf16[1024,2048]{1,0:T(8,128)(2,1)} async-done(((bf16[1024,512]{1,0:T(8,128)(2,1)}), bf16[1024,2048]{1,0:T(8,128)(2,1)}) %all-gather.8.cloned.1.call-update) | async-done | bytes 4194320 | tf_op jit(solution)/shard_map/all_gather | solution.py:162
  761.2 6.2 convolution_convert_fusion.9
  767.4 44.8 %while.30 = (s32[]{:T(128)}, f32[1024,2,128]{0,2,1:T(8,128)S(1)}, f32[1024,2,128]{0,2,1:T(8,128)}, f32[2,512,2,2,128]{4,1,0,3,2:T(8,128)}, s32[2]{0:T(128)S(1)},...) while((s32[]{:T(128)}, f32[1024,2,128]{0,2,1:T(8,128)S(1)}, ...), condition=%wide.region_14.15_spmd.clone, body=%wide.region_12.14_spmd.clone.sunk | while | flops 2718432768 | bytes 111737504 | solution.py:205
  833.3 12.0 convolution_convert_fusion.1
  845.3 8.8 convolution_convert_fusion.2
  854.2 9.3 convolution_convert_fusion
  876.8 31.9 %reduce-scatter.5.cloned.1.call-done = bf16[1024,512]{1,0:T(8,128)(2,1)} async-done(((bf16[1024,2048]{1,0:T(8,128)(2,1)}), bf16[1024,512]{1,0:T(8,128)(2,1)}) %reduce-scatter.5.cloned.1.call-update) | async-done | bytes 1048592 | tf_op jit(solution)/shard_map/reduce_scatter | solution.py:226
  910.8 17.9 %all-reduce.4 = (f32[1024,1]{0,1:T(1,128)S(1)}, bf16[128]{0:T(256)(128)(2,1)S(1)}, bf16[128]{0:T(256)(128)(2,1)S(1)}) all-reduce(f32[1024,1]{0,1:T(1,128)S(1)} %bitcast.237, f32[128]{0:T(128)S(1)} %get-tuple-element.294, f32[128]{0:T(128)S(1)} %get-tuple-element.298), channel_id=1, replica_groups=mesh['dp'=8,'tensor'=4] {'tensor'}, use_global_device_ids=true, to_apply=%region_19.20 | all-reduce | flops 1280 | bytes 9728 | tf_op jit(solution)/shard_map/psum | solution.py:229
  928.8 13.1 %all-reduce.5 = (bf16[512]{0:T(512)(128)(2,1)S(1)}, bf16[128]{0:T(256)(128)(2,1)S(1)}, bf16[128]{0:T(256)(128)(2,1)S(1)}, bf16[512]{0:T(512)(128)(2,1)S(1)}) all-reduce(bf16[512]{0:T(512)(128)(2,1)S(1)} %get-tuple-element.296, bf16[128]{0:T(256)(128)(2,1)S(1)} %get-tuple-element.339, ...), channel_id=1, replica_groups=mesh['dp'=8,'tensor'=4] {'dp'}, use_global_device_ids=true, to_apply=%region_21.22 | all-reduce | flops 1280 | bytes 5120 | tf_op jit(solution)/shard_map/psum | solution.py:263
  947.6 279.5 %all-reduce.15.cloned.1.call-done = (bf16[2048,512]{1,0:T(8,128)(2,1)}, bf16[2048,256]{1,0:T(8,128)(2,1)}, bf16[2048,256]{1,0:T(8,128)(2,1)}, bf16[512,2048]{1,0...) async-done(((bf16[2048,512]{1,0:T(8,128)(2,1)}, bf16[2048,256]{1,0:T(8,128)(2,1)}, bf16[2048,256]{1,0:T(8,128)(2,1)}, ...) | async-done | bytes 25165840 | tf_op jit(solution)/shard_map/psum | solution.py:256
  1227.1 4.3 convert_element_type.225
  1237.0 9.5 convert_element_type.239
  1246.5 6.6 convert_element_type.241
  1253.1 6.3 convert_element_type.243
  (307 shorter events, 154.2 us)
Async XLA Ops:
  7.2 102.4 %copy-start = (bf16[2048,512]{1,0:T(8,128)(2,1)S(1)}, bf16[2048,512]{1,0:T(8,128)(2,1)}, u32[]{:S(2)}) copy-start(bf16[2048,512]{1,0:T(8,128)(2,1)} %param.22) | copy-start | bytes 6291460
  7.2 85.9 %all-gather.4.cloned.1.call-start = ((), (), s32[]{:S(2)}) async-start(), calls=%async_computation.2 | async-start | bytes 5242880 | tf_op jit(solution)/shard_map/all_gather | solution.py:74
  7.9 314.7 %all-reduce.11.cloned.1.call-start = ((), (), s32[]{:S(2)}) async-start(), calls=%async_computation.3 | async-start | bytes 8388608 | tf_op jit(solution)/shard_map/psum | solution.py:123
  8.0 88.9 %copy-start.64 = (f32[2048]{0:T(1024)S(1)}, f32[2048]{0:T(1024)}, u32[]{:S(2)}) copy-start(f32[2048]{0:T(1024)} %param.21) | copy-start | bytes 24580
  10.4 87.6 %copy-start.17 = (f32[1024,128]{1,0:T(8,128)}, f32[1024,128]{1,0:T(8,128)S(1)}, u32[]{:S(2)}) copy-start(f32[1024,128]{1,0:T(8,128)S(1)} %get-tuple-element.375) | copy-start | bytes 1572868
  10.4 87.6 %copy-start.20 = (f32[1024,128]{1,0:T(8,128)}, f32[1024,128]{1,0:T(8,128)S(1)}, u32[]{:S(2)}) copy-start(f32[1024,128]{1,0:T(8,128)S(1)} %get-tuple-element.376) | copy-start | bytes 1572868
  156.7 12.2 copy-start.4
  156.7 12.2 copy-start.13
  168.9 235.1 %all-gather.6.cloned.1.call-start = ((), (), s32[]{:S(2)}) async-start(), calls=%async_computation.5 | async-start | bytes 5242880 | tf_op jit(solution)/shard_map/all_gather | solution.py:75
  169.7 426.6 %all-reduce.13.cloned.1.call-start = ((), (), s32[]{:S(2)}) async-start(), calls=%async_computation.6 | async-start | bytes 8388608 | tf_op jit(solution)/shard_map/psum | solution.py:153
  170.4 504.4 %copy-start.61 = (f32[1024]{0:T(1024)}, f32[1024]{0:T(1024)S(1)}, u32[]{:S(2)}) copy-start(f32[1024]{0:T(1024)S(1)} %fusion.71) | copy-start | bytes 12292
  170.4 157.3 %copy-start.58 = (f32[2048]{0:T(1024)S(1)}, f32[2048]{0:T(1024)}, u32[]{:S(2)}) copy-start(f32[2048]{0:T(1024)} %param.28) | copy-start | bytes 24580
  328.5 14.9 %slice-start.4 = ((s8[6291456]{0:T(1024)(128)(4,1)}), s8[2097152]{0:T(1024)(128)(4,1)S(1)}, s32[]{:S(2)}) async-start(s8[6291456]{0:T(1024)(128)(4,1)} %bitcast.239), calls=%async_computation.14 | async-start | bytes 4194304
  331.4 12.0 copy-start.31
  331.4 12.0 slice-start.5
  421.1 10.3 copy-start.72
  421.1 10.3 copy-start.75
  442.5 232.2 %reduce-scatter.3.cloned.1.call-start = ((), (), s32[]{:S(2)}) async-start(), calls=%async_computation.4 | async-start | bytes 5242880 | tf_op jit(solution)/shard_map/reduce_scatter | solution.py:133
  453.6 307.6 %all-gather.8.cloned.1.call-start = ((), (), s32[]{:S(2)}) async-start(), calls=%async_computation.7 | async-start | bytes 5242880 | tf_op jit(solution)/shard_map/all_gather | solution.py:162
  605.4 69.3 %copy-start.33 = (bf16[1024,512]{1,0:T(8,128)(2,1)S(1)}, bf16[1024,512]{1,0:T(8,128)(2,1)}, u32[]{:S(2)}) copy-start(bf16[1024,512]{1,0:T(8,128)(2,1)} %param.20) | copy-start | bytes 3145732
  679.8 228.9 %reduce-scatter.5.cloned.1.call-start = ((), (), s32[]{:S(2)}) async-start(), calls=%async_computation.8 | async-start | bytes 5242880 | tf_op jit(solution)/shard_map/reduce_scatter | solution.py:226
  833.2 393.9 %all-reduce.15.cloned.1.call-start = ((), (), s32[]{:S(2)}) async-start(), calls=%async_computation.9 | async-start | bytes 50331648 | tf_op jit(solution)/shard_map/psum | solution.py:256
  833.2 12.0 copy-start.32
  833.3 12.0 copy-start.73
  854.1 9.3 copy-start.36
  875.9 32.8 %copy-start.16 = (bf16[1024,512]{1,0:T(8,128)(2,1)S(1)}, bf16[1024,512]{1,0:T(8,128)(2,1)}, u32[]{:S(2)}) copy-start(bf16[1024,512]{1,0:T(8,128)(2,1)} %param.18) | copy-start | bytes 3145732
  875.9 32.8 %copy-start.57 = (f32[1024]{0:T(1024)S(1)}, f32[1024]{0:T(1024)}, u32[]{:S(2)}) copy-start(f32[1024]{0:T(1024)} %copy-done.56) | copy-start | bytes 12292
  875.9 52.9 %copy-start.69 = (bf16[512]{0:T(512)(128)(2,1)S(1)}, bf16[512]{0:T(512)(128)(2,1)}, u32[]{:S(2)}) copy-start(bf16[512]{0:T(512)(128)(2,1)} %get-tuple-element.360) | copy-start | bytes 3076
  875.9 68.2 %copy-start.63 = (f32[1024]{0:T(1024)S(1)}, f32[1024]{0:T(1024)}, u32[]{:S(2)}) copy-start(f32[1024]{0:T(1024)} %get-tuple-element.377) | copy-start | bytes 12292
  1234.4 12.2 slice-start.2
  1237.0 9.5 slice-start.3
  1237.0 16.1 %slice-start = ((s8[6291456]{0:T(1024)(128)(4,1)}), s8[4194304]{0:T(1024)(128)(4,1)S(1)}, s32[]{:S(2)}) async-start(s8[6291456]{0:T(1024)(128)(4,1)} %bitcast.226), calls=%async_computation.10 | async-start | bytes 8388608
  (68 other events, 215.3 us)
Sparse Core Ops, SparseCore 0:
  9.6 83.4 all-gather.3
  169.0 153.4 all-reduce.10
  324.2 79.7 all-gather.5
  442.7 153.5 all-reduce.12
  598.9 75.7 reduce-scatter.2
  679.9 81.2 all-gather.7
  833.3 75.2 reduce-scatter.4
  914.8 312.1 all-reduce.14
where the time goes:
time: 1280 us; the launch traced here: 1270 us
  waiting for transfers between devices  886 us (69%)
  matrix products  181 us (14%)
  other arithmetic  104 us (8%)
  local copies, waits for them, and re-layouts  34.4 us (3%)
  blocking collectives  31 us (2%)
  between operations  16.1 us (1%)
  loops' own time  13.2 us (1%)
    psum x1, waiting for transfers between devices, local(): lax.psum(grad_query.astype(jnp.bfloat16), 'dp').astype(jnp.float32)  279 us
    psum x1, waiting for transfers between devices, local(): lax.psum(branch.astype(jnp.bfloat16), 'tensor').astype(jnp.float32)  152 us
    psum x1, waiting for transfers between devices, local(): lax.psum(mixed_grad.astype(jnp.bfloat16), 'tensor').astype(jnp.float32)  142 us
    all_gather x1, waiting for transfers between devices, local(): lax.all_gather(hidden_grad.astype(jnp.bfloat16), 'tensor', axis=1, tiled=...  81.3 us
    all_gather x1, waiting for transfers between devices, local(): lax.all_gather(tokens, 'tensor', axis=1, tiled=True)  80.6 us
    reduce_scatter x1, waiting for transfers between devices, local(): lax.psum_scatter(down_part.astype(jnp.bfloat16), 'tensor', scatter_dimens...  65 us
    all_gather x1, waiting for transfers between devices, local(): lax.all_gather(cotangent, 'tensor', axis=1, tiled=True)  52.1 us
    reduce_scatter x1, waiting for transfers between devices, local(): lax.psum_scatter(normed_grad.astype(jnp.bfloat16), 'tensor', scatter_dime...  31.9 us
  transfers between devices with their start and end apart: 8, of which 8 were waited for; matrix products, arithmetic and copies ran while one was open for 8% of the time, Pallas kernels for 0%

commit v1 on v0

v1 whole, which is shorter than its diff:
```python
from functools import partial

import jax
import jax.numpy as jnp
from jax import lax
from jax.sharding import PartitionSpec as P

EPSILON = 1e-06
ROPE_BASE = 1000000.0


def norm_rows(values, gain):
    factor = lax.rsqrt(jnp.mean(values * values, axis=-1, keepdims=True) + EPSILON)
    return values * factor * gain


def rope_tables(seq_len, head_dim):
    half_dim = head_dim // 2
    frequency = ROPE_BASE ** (-(jnp.arange(half_dim, dtype=jnp.float32) * 2.0 / head_dim))
    angles = jnp.arange(seq_len, dtype=jnp.float32)[:, None] * frequency[None, :]
    angles = jnp.concatenate([angles, angles], axis=1)
    return (jnp.cos(angles)[:, None, :], jnp.sin(angles)[:, None, :])


def rotate(values, cosine_table, sine_table):
    half_dim = values.shape[-1] // 2
    turned = jnp.concatenate([-values[..., half_dim:], values[..., :half_dim]], axis=-1)
    return values * cosine_table + turned * sine_table


def head_post(raw_heads, gain, cosine_table, sine_table):
    return rotate(norm_rows(raw_heads, gain), cosine_table, sine_table)


def mask_table(row_start, block_rows, seq_len, length):
    positions = jnp.arange(seq_len, dtype=jnp.int32)
    row_index = row_start + jnp.arange(block_rows, dtype=jnp.int32)
    return (positions[None, :] <= row_index[:, None]) & (positions[None, :] < length)


def small_sum(values, axis, size):
    total = values
    for shift in range(1, size):
        pairs = [(i, (i + shift) % size) for i in range(size)]
        total = total + lax.ppermute(values, axis, pairs)
    return total


def after(value, *others):
    return lax.optimization_barrier((value, others))[0]


def dot(left, right, contract):
    return lax.dot_general(left, right, (contract, ((), ())), preferred_element_type=jnp.float32)


def pair_sum(left, right, core, pairs):
    half = left.shape[1] // 2

    def rows(which):
        part = lax.dynamic_slice_in_dim(left, which * half, half, 1)
        return dot(part, right, ((0,), (0,)))

    received = lax.ppermute(rows(1 - core).astype(jnp.bfloat16), "dp", pairs)
    return (rows(core) + received.astype(jnp.float32)).astype(jnp.bfloat16)


def both_halves(mine, core, pairs):
    other = lax.ppermute(mine, "dp", pairs)
    parts = (jnp.where(core == 0, mine, other), jnp.where(core == 0, other, mine))
    return jnp.concatenate(parts, axis=0).astype(jnp.float32)


def local(
    tensor_size,
    dp_size,
    tokens,
    lengths,
    cotangent,
    first_gain,
    query_weight,
    key_weight,
    value_weight,
    query_gain,
    key_gain,
    out_weight,
    second_gain,
    gate_weight,
    up_weight,
    down_weight,
):
    bf16 = jnp.bfloat16
    tensor_rank = lax.axis_index("tensor")
    dp_rank = lax.axis_index("dp")
    seq_len = tokens.shape[0]
    share_width = tokens.shape[1]
    model_width = first_gain.shape[0]
    head_dim = query_gain.shape[0]
    local_heads = query_weight.shape[1] // head_dim
    local_groups = key_weight.shape[1] // head_dim
    group_size = local_heads // local_groups
    block_rows = min(512, seq_len)
    block_count = seq_len // block_rows
    score_scale = head_dim ** (-0.5)
    length = lengths[0]
    valid_rows = (jnp.arange(seq_len, dtype=jnp.int32) < length).astype(jnp.float32)[:, None]
    own_start = tensor_rank * share_width
    first_own = lax.dynamic_slice_in_dim(first_gain, own_start, share_width, 0)
    second_own = lax.dynamic_slice_in_dim(second_gain, own_start, share_width, 0)
    full_tokens = lax.all_gather(tokens, "tensor", axis=1, tiled=True)
    full_cot = lax.all_gather(after(cotangent, full_tokens), "tensor", axis=1, tiled=True)
    out_cols = model_width // dp_size
    out_rows = out_weight.shape[0]
    out_part = lax.dynamic_slice_in_dim(out_weight, dp_rank * out_cols, out_cols, 1)
    out_full = jnp.zeros((out_rows * tensor_size, model_width), bf16)
    for shift in range(tensor_size):
        pairs = [(i, (i + shift) % tensor_size) for i in range(tensor_size)]
        source = lax.rem(tensor_rank + tensor_size - shift, tensor_size)
        piece = lax.ppermute(out_part, "tensor", pairs) if shift else out_part
        out_full = lax.dynamic_update_slice(
            out_full, piece, (source * out_rows, dp_rank * out_cols)
        )
    rotated_order = [[(i + 1) % dp_size for i in range(dp_size)]]
    out_full = lax.psum(out_full, "dp", axis_index_groups=rotated_order)

    token_own = tokens.astype(jnp.float32)
    token_rows = full_tokens.astype(jnp.float32)
    first_root = lax.rsqrt(jnp.mean(token_rows * token_rows, axis=1, keepdims=True) + EPSILON)
    normed = (token_rows * first_root * first_gain).astype(bf16)
    query_raw = dot(normed, query_weight, ((1,), (0,))).reshape(seq_len, local_heads, head_dim)
    key_raw = dot(normed, key_weight, ((1,), (0,))).reshape(seq_len, local_groups, head_dim)
    value_rows = dot(normed, value_weight, ((1,), (0,))).astype(bf16).reshape(seq_len, local_groups, head_dim)
    cosine_table, sine_table = rope_tables(seq_len, head_dim)
    rotated = partial(head_post, cosine_table=cosine_table, sine_table=sine_table)
    query_rot, query_pull = jax.vjp(rotated, query_raw, query_gain)
    key_rot, key_pull = jax.vjp(rotated, key_raw, key_gain)
    query_rows = query_rot.astype(bf16).reshape(seq_len, local_groups, group_size, head_dim)
    key_rows = key_rot.astype(bf16)

    def block_scores(row_start):
        query_block = lax.dynamic_slice_in_dim(query_rows, row_start, block_rows, 0)
        scores = (
            jnp.einsum("qcgd,kcd->cgqk", query_block, key_rows, preferred_element_type=jnp.float32)
            * score_scale
        )
        allowed = mask_table(row_start, block_rows, seq_len, length)
        return (query_block, jnp.where(allowed[None, None], scores, -1e30))

    def attend(row_start):
        query_block, scores = block_scores(row_start)
        highest = jnp.max(scores, axis=-1, keepdims=True)
        raised = jnp.exp(scores - highest)
        row_total = jnp.sum(raised, axis=-1, keepdims=True)
        weights = (raised / row_total).astype(bf16)
        block_out = jnp.einsum(
            "cgqk,kcd->qcgd", weights, value_rows, preferred_element_type=jnp.float32
        )
        return (block_out, highest + jnp.log(row_total))

    starts = jnp.arange(block_count, dtype=jnp.int32) * block_rows
    attended, log_totals = lax.map(attend, starts)
    attended = attended.reshape(seq_len, local_heads * head_dim).astype(bf16)

    out_full = after(out_full, attended)
    attended = after(attended, full_cot)
    grad_full = (full_cot.astype(jnp.float32) * valid_rows).astype(bf16)
    grad_own = cotangent.astype(jnp.float32) * valid_rows

    half = seq_len // 2
    grad_parts, product_parts, mixed_parts = [], [], []
    gate_grad_parts, up_grad_parts, mid_parts, root_parts, hidden_parts = [], [], [], [], []
    halves = (slice(0, half), slice(half, seq_len))
    heads_in = (attended[:half], after(attended[half:], out_full))
    heads_parts = [lax.all_gather(part, "tensor", axis=1, tiled=True) for part in heads_in]
    product_grads = [dot(grad_full[rows], down_weight, ((1,), (1,))) for rows in halves]
    earlier = product_grads
    for part, rows in enumerate(halves):
        heads_full = after(heads_parts[part], *earlier)
        grad_product = product_grads[part]
        hidden = token_rows[rows] + dot(heads_full, out_full, ((1,), (0,)))
        root = lax.rsqrt(jnp.mean(hidden * hidden, axis=1, keepdims=True) + EPSILON)
        mixed = (hidden * root * second_gain).astype(bf16)
        gate_value = dot(mixed, gate_weight, ((1,), (0,)))
        up_value = dot(mixed, up_weight, ((1,), (0,)))
        sigmoid_gate = jax.nn.sigmoid(gate_value)
        activated = gate_value * sigmoid_gate
        product = (activated * up_value).astype(bf16)
        slope = sigmoid_gate * (1.0 + gate_value * (1.0 - sigmoid_gate))
        gate_grad = (grad_product * up_value * slope).astype(bf16)
        up_grad = (grad_product * activated).astype(bf16)
        mid = jnp.sum(
            gate_grad.astype(jnp.float32) * gate_value + up_grad.astype(jnp.float32) * up_value,
            axis=1,
        )
        mid_parts.append(small_sum(mid, "tensor", tensor_size)[:, None])
        mixed_grad = dot(gate_grad, gate_weight, ((1,), (1,))) + dot(
            up_grad, up_weight, ((1,), (1,))
        )
        mixed_grad = mixed_grad.astype(bf16)
        earlier = [mixed_grad]
        grad_parts.append(lax.psum_scatter(mixed_grad, "tensor", scatter_dimension=1, tiled=True))
        hidden_parts.append(lax.dynamic_slice_in_dim(hidden, own_start, share_width, 1))
        root_parts.append(root)
        product_parts.append(product)
        mixed_parts.append(mixed)
        gate_grad_parts.append(gate_grad)
        up_grad_parts.append(up_grad)
    hidden_own, second_root, product, mixed_rows, gate_grads, up_grads = (
        jnp.concatenate(parts, axis=0)
        for parts in (
            hidden_parts,
            root_parts,
            product_parts,
            mixed_parts,
            gate_grad_parts,
            up_grad_parts,
        )
    )
    down_part = dot(product, down_weight, ((1,), (0,))).astype(bf16)
    core = lax.rem(dp_rank, 2)
    pairs = [(i, i ^ 1) for i in range(dp_size)]
    chips = [[i for i in range(dp_size) if i % 2 == side] for side in (0, 1)]
    early = (
        pair_sum(product, grad_full, core, pairs),
        pair_sum(mixed_rows, gate_grads, core, pairs),
        pair_sum(mixed_rows, up_grads, core, pairs),
    )
    grad_parts, mid_parts = after((grad_parts, mid_parts), *early, down_part)
    mixed_own_grad = jnp.concatenate(grad_parts, axis=0).astype(jnp.float32)
    mid_total = jnp.concatenate(mid_parts, axis=0)
    early = lax.psum(early, "dp", axis_index_groups=chips)

    second_gain_grad = jnp.sum(mixed_own_grad * hidden_own * second_root, axis=0)
    hidden_grad = (
        grad_own
        + mixed_own_grad * second_own * second_root
        - hidden_own * second_root**2 / model_width * mid_total
    )
    hidden_grad_rows = lax.all_gather(hidden_grad.astype(bf16), "tensor", axis=1, tiled=True)
    down_part, hidden_grad_rows = lax.optimization_barrier((down_part, hidden_grad_rows))
    down_own = lax.psum_scatter(down_part, "tensor", scatter_dimension=1, tiled=True)
    grad_out = pair_sum(attended, hidden_grad_rows, core, pairs)
    attended_grad = (
        dot(hidden_grad_rows, out_weight, ((1,), (1,)))
        .astype(bf16)
        .reshape(seq_len, local_groups, group_size, head_dim)
    )

    def attend_back(running, row_start):
        key_sum, value_sum = running
        query_block, scores = block_scores(row_start)
        block_index = row_start // block_rows
        weights = jnp.exp(scores - log_totals[block_index])
        grad_block = lax.dynamic_slice_in_dim(attended_grad, row_start, block_rows, 0)
        weight_grad = jnp.einsum(
            "qcgd,kcd->cgqk", grad_block, value_rows, preferred_element_type=jnp.float32
        )
        centre = jnp.sum(weights * weight_grad, axis=-1, keepdims=True)
        score_grad = (weights * (weight_grad - centre)).astype(bf16)
        value_sum = value_sum + jnp.einsum(
            "cgqk,qcgd->kcd",
            weights.astype(bf16),
            grad_block,
            preferred_element_type=jnp.float32,
        )
        key_sum = (
            key_sum
            + jnp.einsum(
                "cgqk,qcgd->kcd", score_grad, query_block, preferred_element_type=jnp.float32
            )
            * score_scale
        )
        query_grad = (
            jnp.einsum("cgqk,kcd->qcgd", score_grad, key_rows, preferred_element_type=jnp.float32)
            * score_scale
        )
        return ((key_sum, value_sum), query_grad)

    empty_groups = jnp.zeros((seq_len, local_groups, head_dim), jnp.float32)
    (key_grad_rot, value_grad), query_blocks = lax.scan(
        attend_back, (empty_groups, empty_groups), starts
    )
    query_grad_rot = query_blocks.reshape(seq_len, local_heads, head_dim)
    query_raw_grad, query_gain_grad = query_pull(query_grad_rot)
    key_raw_grad, key_gain_grad = key_pull(key_grad_rot)
    query_raw_grad = query_raw_grad.reshape(seq_len, local_heads * head_dim).astype(bf16)
    key_raw_grad = key_raw_grad.reshape(seq_len, local_groups * head_dim).astype(bf16)
    value_raw_grad = value_grad.reshape(seq_len, local_groups * head_dim).astype(bf16)
    normed_grad = (
        dot(query_raw_grad, query_weight, ((1,), (1,)))
        + dot(key_raw_grad, key_weight, ((1,), (1,)))
        + dot(value_raw_grad, value_weight, ((1,), (1,)))
    )
    normed_grad = normed_grad.astype(bf16)
    normed_own_grad = lax.psum_scatter(normed_grad, "tensor", scatter_dimension=1, tiled=True)
    late = (
        grad_out,
        pair_sum(normed, query_raw_grad, core, pairs),
        pair_sum(normed, key_raw_grad, core, pairs),
        pair_sum(normed, value_raw_grad, core, pairs),
    )
    down_own = after(down_own, normed_grad, *late)
    layer_out = (hidden_own + down_own.astype(jnp.float32)).astype(bf16)
    normed_own_grad = after(normed_own_grad, layer_out, *early).astype(jnp.float32)
    backwards = [group[::-1] for group in chips]
    late = lax.psum(after(late, normed_grad, *early), "dp", axis_index_groups=backwards)
    grad_down, grad_gate, grad_up = (both_halves(part, core, pairs) for part in early)
    grad_out, grad_query, grad_key, grad_value = (both_halves(part, core, pairs) for part in late)
    first_term, query_gain_grad, key_gain_grad = lax.psum(
        (
            jnp.sum(normed_own_grad * first_own * token_own, axis=1, keepdims=True),
            query_gain_grad,
            key_gain_grad,
        ),
        "tensor",
    )
    first_gain_grad = jnp.sum(normed_own_grad * token_own * first_root, axis=0)
    token_grad = (
        hidden_grad
        + normed_own_grad * first_own * first_root
        - token_own * first_root**3 / model_width * first_term
    ).astype(bf16)
    gains = jnp.concatenate([first_gain_grad, second_gain_grad, query_gain_grad, key_gain_grad])
    gains = lax.psum(gains, "dp")
    first_gain_grad, second_gain_grad, query_gain_grad, key_gain_grad = (
        gains[:share_width],
        gains[share_width : 2 * share_width],
        gains[2 * share_width : 2 * share_width + head_dim],
        gains[2 * share_width + head_dim :],
    )
    return (
        layer_out,
        token_grad,
        first_gain_grad,
        grad_query,
        grad_key,
        grad_value,
        query_gain_grad,
        key_gain_grad,
        grad_out,
        second_gain_grad,
        grad_gate,
        grad_up,
        grad_down,
    )


def solution(mesh):
    in_specs = (
        P("dp", "tensor"),
        P("dp"),
        P("dp", "tensor"),
        P(),
        P(None, "tensor"),
        P(None, "tensor"),
        P(None, "tensor"),
        P(),
        P(),
        P("tensor", None),
        P(),
        P(None, "tensor"),
        P(None, "tensor"),
        P("tensor", None),
    )
    out_specs = (
        P("dp", "tensor"),
        P("dp", "tensor"),
        P("tensor"),
        P(None, "tensor"),
        P(None, "tensor"),
        P(None, "tensor"),
        P(),
        P(),
        P("tensor", None),
        P("tensor"),
        P(None, "tensor"),
        P(None, "tensor"),
        P("tensor", None),
    )
    return jax.shard_map(
        partial(local, mesh.shape["tensor"], mesh.shape["dp"]), mesh=mesh, in_specs=in_specs, out_specs=out_specs, check_vma=False)
```

time: 1280 us -> 822 us (0.64)
  waiting for transfers between devices: 886 us -> 319 us
  matrix products: 181 us -> 244 us
  local copies, waits for them, and re-layouts: 34.4 us -> 64 us
  starting transfers between devices: 0.32 us -> 17.3 us
  other arithmetic: 104 us -> 117 us
    psum x3, waiting for transfers between devices: 574 us -> 111 us  [the longest x1 63 us: local(): out_full = lax.psum(out_full, 'dp', axis_index_groups=rotated_order)]
    reduce_scatter x2 -> x4, waiting for transfers between devices: 96.8 us -> 1.62 us  [the longest x1 1.61 us: local(): lax.psum_scatter(normed_grad, 'tensor', scatter_dimension=1, tiled=True)]
    dot_general x23 -> x36, matrix products: 151 us -> 192 us  [the longest x34 181 us: dot(): lax.dot_general(left, right, (contract, ((), ())), preferred_element_type...]
    all_gather x3 -> x5, waiting for transfers between devices: 214 us -> 176 us  [the longest x1 85.1 us: local(): full_tokens = lax.all_gather(tokens, 'tensor', axis=1, tiled=True)]
    ppermute x0 -> x23, waiting for transfers between devices: none -> 28.4 us  [the longest x3 21.2 us: local(): piece = lax.ppermute(out_part, 'tensor', pairs) if shift else out_part]
    ppermute x0 -> x23, starting transfers between devices: none -> 15.6 us  [the longest x6 8.33 us: small_sum(): total = total + lax.ppermute(values, axis, pairs)]
    select_n x0 -> x7, other arithmetic: none -> 14.8 us  [both_halves(): jnp.where(core == 0, mine, other)]
    dynamic_update_slice x0 -> x3, local copies, waits for them, and re-layouts: none -> 13.1 us  [local(): lax.dynamic_update_slice(out_full, piece, (source * out_rows, dp_rank * o...]
  transfers between devices with their start and end apart: 8 -> 35, of which waited for: 8 -> 13; matrix products, arithmetic and copies ran while one was open for 8% -> 49% of each run, Pallas kernels for 0% -> 0%
where the time goes in v1:
time: 822 us; the launch traced here: 814 us
  waiting for transfers between devices  319 us (39%)
  matrix products  244 us (30%)
  other arithmetic  117 us (14%)
  local copies, waits for them, and re-layouts  64 us (8%)
  blocking collectives  23.5 us (3%)
  between operations  17.6 us (2%)
  starting transfers between devices  17.3 us (2%)
  loops' own time  12.5 us (2%)
    dot_general x34, matrix products, dot(): lax.dot_general(left, right, (contract, ((), ())), preferred_element_type...  181 us
    all_gather x1, waiting for transfers between devices, local(): full_tokens = lax.all_gather(tokens, 'tensor', axis=1, tiled=True)  85.1 us
    all_gather x1, waiting for transfers between devices, local(): lax.all_gather(hidden_grad.astype(bf16), 'tensor', axis=1, tiled=True)  79.1 us
    psum x1, waiting for transfers between devices, local(): out_full = lax.psum(out_full, 'dp', axis_index_groups=rotated_order)  63 us
    psum x1, waiting for transfers between devices, local(): lax.psum(after(late, normed_grad, *early), 'dp', axis_index_groups=backwa...  38.1 us
    convert_element_type x7, other arithmetic, both_halves(): return jnp.concatenate(parts, axis=0).astype(jnp.float32)  29.9 us
    ppermute x3, waiting for transfers between devices, local(): piece = lax.ppermute(out_part, 'tensor', pairs) if shift else out_part  21.2 us
    dot_general x4, matrix products, block_scores(): jnp.einsum('qcgd,kcd->cgqk', query_block, key_rows, preferred_element_typ...  17.5 us
  transfers between devices with their start and end apart: 35, of which 13 were waited for; matrix products, arithmetic and copies ran while one was open for 49% of the time, Pallas kernels for 0%

profile of v1, /device:TPU:0, one launch (start us, length us, event | category | flops | bytes accessed | tf_op | source)
XLA Modules:
  0.0 814.4 jit_solution(2130991675308638191)
XLA Ops:
  8.8 85.1 %all-gather.6.cloned.1.call-done = bf16[1024,2048]{1,0:T(8,128)(2,1)} async-done(((bf16[1024,512]{1,0:T(8,128)(2,1)}), bf16[1024,2048]{1,0:T(8,128)(2,1)}) %all-gather.6.cloned.1.call-update) | async-done | bytes 4194320 | tf_op jit(solution)/shard_map/all_gather | solution.py:110
  119.2 16.3 %collective-permute-done.1 = bf16[512,256]{1,0:T(8,128)(2,1)} collective-permute-done((bf16[512,256]{1,0:T(8,128)(2,1)S(1)}, bf16[512,256]{1,0:T(8,128)(2,1)}, u32[]{:S(2)}, u32[]{:S(2)}) %collective-permute-start.1) | collective-permute-done | bytes 262176 | tf_op jit(solution)/shard_map/ppermute | solution.py:119
  184.7 28.4 %while.29 = (s32[]{:T(128)}, bf16[2,512,2,2,128]{4,1,3,2,0:T(8,128)(2,1)}, f32[2,2,2,512,1]{3,2,1,4,0:T(2,128)S(1)}, s32[2]{0:T(128)S(1)}, s32[]{:T(128)}, /*ind...) while((s32[]{:T(128)}, ...), condition=%wide.region_6.7_spmd, body=%wide.region_3.6_spmd.sunk | while | flops 1099955712 | bytes 40442120 | solution.py:161
  223.0 63.0 %all-reduce.11.cloned.1.call-done = bf16[2048,2048]{1,0:T(8,128)(2,1)} async-done(((bf16[2048,2048]{1,0:T(8,128)(2,1)}), bf16[2048,2048]{1,0:T(8,128)(2,1)}) %all-reduce.11.cloned.1.call-update) | async-done | bytes 8388624 | tf_op jit(solution)/shard_map/psum | solution.py:124
  286.0 6.7 convert_element_type.227
  295.8 9.5 %fusion.68 = f32[512,1536]{1,0:T(8,128)} fusion(bf16[1536,2048]{1,0:T(8,128)(2,1)} %param.31, bf16[1024,2048]{1,0:T(8,128)(2,1)S(1)} %multiply_convert_fusion), kind=kOutput, calls=%fused_computation.138 | convolution fusion | flops 3221225472 | bytes 11534336 | tf_op jit(solution)/shard_map/dot_general | solution.py:54
  310.8 9.9 %multiply_reduce_fusion.2 = (f32[512]{0:T(512)S(1)}, f32[512,2048]{1,0:T(8,128)S(1)}) fusion(bf16[512,2048]{1,0:T(8,128)(2,1)} %all-gather.10.cloned.1.call-done, bf16[2048,2048]{1,0:T(8,128)(2,1)} %all-reduce.11.cloned.1.call-done, f32[1024,2048]{1,0:T(8,128)} %convert_element_type.227), kind=kOutput, calls=%fused_computation.81 | convolution fusion | flops 4298112512 | bytes 18876416 | tf_op jit(solution)/shard_map/dot_general | solution.py:54
  322.9 7.0 fusion.150
  329.9 6.0 add_reduce_fusion.1
  344.6 12.1 %all-gather.12.cloned.1.call-done = bf16[512,2048]{1,0:T(8,128)(2,1)} async-done(((bf16[512,512]{1,0:T(8,128)(2,1)}), bf16[512,2048]{1,0:T(8,128)(2,1)}) %all-gather.12.cloned.1.call-update) | async-done | bytes 2097168 | tf_op jit(solution)/shard_map/all_gather | solution.py:174
  356.8 9.8 %multiply_reduce_fusion.1 = (f32[512]{0:T(512)S(1)}, f32[512,2048]{1,0:T(8,128)S(1)}) fusion(bf16[512,2048]{1,0:T(8,128)(2,1)} %all-gather.12.cloned.1.call-done, bf16[2048,2048]{1,0:T(8,128)(2,1)} %all-reduce.11.cloned.1.call-done, f32[1024,2048]{1,0:T(8,128)} %convert_element_type.227), kind=kOutput, calls=%fused_computation.78 | convolution fusion | flops 4298112512 | bytes 18876416 | tf_op jit(solution)/shard_map/dot_general | solution.py:54
  368.7 9.3 %fusion.152 = f32[512,1536]{1,0:T(8,128)} fusion(bf16[512,2048]{1,0:T(8,128)(2,1)S(1)} %multiply_convert_fusion.2, bf16[2048,1536]{1,0:T(8,128)(2,1)} %param.29), kind=kOutput, calls=%fused_computation.261 | convolution fusion | flops 3221225472 | bytes 11534336 | tf_op jit(solution)/shard_map/dot_general | solution.py:54
  378.0 7.1 add_reduce_fusion
  400.7 6.3 add_convert_fusion.4
  407.0 7.7 convolution_convert_fusion.1
  414.8 11.2 %convolution_convert_fusion = bf16[1024,2048]{1,0:T(8,128)(2,1)} fusion(bf16[1536,2048]{1,0:T(8,128)(2,1)} %param.31, bf16[512,1536]{1,0:T(8,128)(2,1)} %copy-done.87, bf16[512,1536]{1,0:T(8,128)(2,1)} %get-tuple-element.405), kind=kOutput, calls=%fused_computation.87 | convolution fusion | flops 6450839552 | bytes 13631488 | tf_op jit(solution)/shard_map/dot_general | solution.py:54
  443.2 7.4 add_convert_fusion.2
  450.7 6.6 add_convert_fusion.1
  457.4 6.4 add_convert_fusion.3
  469.4 79.1 %all-gather.14.cloned.1.call-done = bf16[1024,2048]{1,0:T(8,128)(2,1)} async-done(((bf16[1024,512]{1,0:T(8,128)(2,1)}), bf16[1024,2048]{1,0:T(8,128)(2,1)}) %all-gather.14.cloned.1.call-update) | async-done | bytes 4194320 | tf_op jit(solution)/shard_map/all_gather | solution.py:239
  548.5 6.4 convolution_convert_fusion.5
  556.1 73.9 %while.30 = (s32[]{:T(128)}, f32[1024,2,128]{0,2,1:T(8,128)}, f32[1024,2,128]{0,2,1:T(8,128)}, f32[2,512,2,2,128]{4,1,0,3,2:T(8,128)}, s32[2]{0:T(128)S(1)}, /*i...) while((s32[]{:T(128)}, f32[1024,2,128]{0,2,1:T(8,128)}, ...), condition=%wide.region_17.18_spmd.clone, body=%wide.region_15.17_spmd.clone.sunk | while | flops 2718432768 | bytes 145291936 | solution.py:280
  568.6 7.5 fusion.238
  604.8 7.9 fusion.238
  652.7 9.7 %all-reduce.13.cloned.1.call-done = (bf16[768,2048]{1,0:T(8,128)(2,1)}, bf16[1024,1536]{1,0:T(8,128)(2,1)}, bf16[1024,1536]{1,0:T(8,128)(2,1)}) async-done(((bf16[768,2048]{1,0:T(8,128)(2,1)}, bf16[1024,1536]{1,0:T(8,128)(2,1)}, bf16[1024,1536]{1,0:T(8,128)(2,1)}), (bf16[768,2048]{1,0:T(8,128)(2,1)}, bf16[1024,1536]{1,0:T(8,128)(2,1)}, bf16[1024,1536]{1,0:T(8,128)(2,1)})) %all-reduce.13.cloned.1.call-update) | async-done | bytes 9437200 | tf_op jit(solution)/shard_map/psum | solution.py:231
  691.4 6.6 maximum_convert_fusion
  698.0 6.0 broadcast_select_fusion.3
  709.4 6.6 maximum_convert_fusion.1
  715.9 8.7 %maximum_convert_fusion.2 = f32[1536,2048]{1,0:T(8,128)} fusion(bf16[768,2048]{1,0:T(8,128)(2,1)} %get-tuple-element.399, bf16[768,2048]{1,0:T(8,128)(2,1)S(1)} %get-tuple-element.398), kind=kLoop, calls=%fused_computation.66 | loop fusion | flops 12582912 | bytes 18874368 | tf_op jit(solution)/shard_map/convert_element_type | solution.py:71
  729.8 11.1 %all-reduce.4 = (f32[1024,1]{0,1:T(1,128)S(1)}, f32[128]{0:T(128)S(1)}, f32[128]{0:T(128)S(1)}) all-reduce(f32[1024,1]{0,1:T(1,128)S(1)} %bitcast.253, f32[128]{0:T(128)S(1)} %get-tuple-element.334, f32[128]{0:T(128)S(1)} %get-tuple-element.330), channel_id=1, replica_groups=mesh['dp'=8,'tensor'=4] {'tensor'}, use_global_device_ids=true, to_apply=%region_25.26 | all-reduce | flops 1280 | bytes 10240 | tf_op jit(solution)/shard_map/psum | solution.py:309
  740.9 12.4 %psum.91 = f32[1280]{0:T(1024)S(1)} all-reduce(f32[1280]{0:T(1024)S(1)} %pad_maximum_fusion.15), channel_id=1, replica_groups=mesh['dp'=8,'tensor'=4] {'dp'}, use_global_device_ids=true, to_apply=%region_32.33 | all-reduce | flops 1280 | bytes 10240 | tf_op jit(solution)/shard_map/psum | solution.py:324
  753.9 38.1 %all-reduce.15.cloned.1.call-done = (bf16[1024,512]{1,0:T(8,128)(2,1)}, bf16[1024,256]{1,0:T(8,128)(2,1)}, bf16[1024,256]{1,0:T(8,128)(2,1)}, bf16[256,2048]{1,0:T(8,128)(2,1)}) async-done(((bf16[1024,512]{1,0:T(8,128)(2,1)}, bf16[1024,256]{1,0:T(8,128)(2,1)}, bf16[1024,256]{1,0:T(8,128)(2,1)}, bf16[256,2048]{1,0:T(8,128)(2,1)}), (bf16[1024,512]{1,0:T(8,128)(2,1)}, bf16[1024,256]{1,0:T(8,128)(2,1)}, ...) | async-done | bytes 3145744 | tf_op jit(solution)/shard_map/psum | solution.py:306
  (457 shorter events, 296.9 us)
Async XLA Ops:
  8.0 85.9 %all-gather.6.cloned.1.call-start = ((), (), s32[]{:S(2)}) async-start(), calls=%async_computation.4 | async-start | bytes 5242880 | tf_op jit(solution)/shard_map/all_gather | solution.py:110
  8.8 210.2 %all-gather.8.cloned.1.call-start = ((), (), s32[]{:S(2)}) async-start(), calls=%async_computation.5 | async-start | bytes 5242880 | tf_op jit(solution)/shard_map/all_gather | solution.py:111
  94.0 192.1 %all-reduce.11.cloned.1.call-start = ((), (), s32[]{:S(2)}) async-start(), calls=%async_computation.7 | async-start | bytes 16777216 | tf_op jit(solution)/shard_map/psum | solution.py:124
  100.2 15.3 %collective-permute-start = (bf16[512,256]{1,0:T(8,128)(2,1)S(1)}, bf16[512,256]{1,0:T(8,128)(2,1)}, u32[]{:S(2)}, u32[]{:S(2)}) collective-permute-start(bf16[512,256]{1,0:T(8,128)(2,1)S(1)} %get-tuple-element.413), channel_id=1, source_target_pairs={{0,1},{1,2},{2,3},{3,0},{4,5},{5,6},{6,7},{7,4},{8,9},{9,10},{10,1... | collective-permute-start | bytes 786440 | tf_op jit(solution)/shard_map/ppermute | solution.py:119
  100.2 35.4 %collective-permute-start.1 = (bf16[512,256]{1,0:T(8,128)(2,1)S(1)}, bf16[512,256]{1,0:T(8,128)(2,1)}, u32[]{:S(2)}, u32[]{:S(2)}) collective-permute-start(bf16[512,256]{1,0:T(8,128)(2,1)S(1)} %get-tuple-element.413), channel_id=1, source_target_pairs={{0,2},{1,3},{2,0},{3,1},{4,6},{5,7},{6,4},{7,5},{8,10},{9,11},{10,... | collective-permute-start | bytes 786440 | tf_op jit(solution)/shard_map/ppermute | solution.py:119
  101.3 38.9 %collective-permute-start.2 = (bf16[512,256]{1,0:T(8,128)(2,1)S(1)}, bf16[512,256]{1,0:T(8,128)(2,1)}, u32[]{:S(2)}, u32[]{:S(2)}) collective-permute-start(bf16[512,256]{1,0:T(8,128)(2,1)S(1)} %get-tuple-element.413), channel_id=1, source_target_pairs={{0,3},{1,0},{2,1},{3,2},{4,7},{5,4},{6,5},{7,6},{8,11},{9,8},{10,9... | collective-permute-start | bytes 786440 | tf_op jit(solution)/shard_map/ppermute | solution.py:119
  144.9 165.9 %all-gather.10.cloned.1.call-start = ((), (), s32[]{:S(2)}) async-start(), calls=%async_computation.6 | async-start | bytes 2621440 | tf_op jit(solution)/shard_map/all_gather | solution.py:174
  221.2 135.6 %all-gather.12.cloned.1.call-start = ((), (), s32[]{:S(2)}) async-start(), calls=%async_computation.8 | async-start | bytes 2621440 | tf_op jit(solution)/shard_map/all_gather | solution.py:174
  310.6 153.1 %reduce-scatter.5.cloned.1.call-start = ((), (), s32[]{:S(2)}) async-start(), calls=%async_computation.9 | async-start | bytes 2621440 | tf_op jit(solution)/shard_map/reduce_scatter | solution.py:201
  344.2 119.5 %reduce-scatter.7.cloned.1.call-start = ((), (), s32[]{:S(2)}) async-start(), calls=%async_computation.10 | async-start | bytes 2621440 | tf_op jit(solution)/shard_map/reduce_scatter | solution.py:201
  390.2 67.1 %collective-permute-start.9 = (bf16[768,2048]{1,0:T(8,128)(2,1)}, bf16[768,2048]{1,0:T(8,128)(2,1)}, u32[]{:S(2)}, u32[]{:S(2)}) collective-permute-start(bf16[768,2048]{1,0:T(8,128)(2,1)} %convolution_convert_fusion.3), channel_id=1, source_target_pairs={{0,4},{4,0},{8,12},{12,8},{16,20},{20,16},{24,28},{28,24},{1,5},{5... | collective-permute-start | bytes 9437192 | tf_op jit(solution)/shard_map/ppermute | solution.py:64
  395.3 47.9 %collective-permute-start.10 = (bf16[1024,1536]{1,0:T(8,128)(2,1)}, bf16[1024,1536]{1,0:T(8,128)(2,1)}, u32[]{:S(2)}, u32[]{:S(2)}) collective-permute-start(bf16[1024,1536]{1,0:T(8,128)(2,1)} %convolution_convert_fusion.2), channel_id=1, source_target_pairs={{0,4},{4,0},{8,12},{12,8},{16,20},{20,16},{24,28},{28,24},{1,5},{5... | collective-permute-start | bytes 9437192 | tf_op jit(solution)/shard_map/ppermute | solution.py:64
  414.7 35.9 %collective-permute-start.11 = (bf16[1024,1536]{1,0:T(8,128)(2,1)}, bf16[1024,1536]{1,0:T(8,128)(2,1)}, u32[]{:S(2)}, u32[]{:S(2)}) collective-permute-start(bf16[1024,1536]{1,0:T(8,128)(2,1)} %convolution_convert_fusion.1), channel_id=1, source_target_pairs={{0,4},{4,0},{8,12},{12,8},{16,20},{20,16},{24,28},{28,24},{1,5},{5... | collective-permute-start | bytes 9437192 | tf_op jit(solution)/shard_map/ppermute | solution.py:64
  414.8 133.8 %all-gather.14.cloned.1.call-start = ((), (), s32[]{:S(2)}) async-start(), calls=%async_computation.11 | async-start | bytes 5242880 | tf_op jit(solution)/shard_map/all_gather | solution.py:239
  430.0 5.7 collective-permute-start.3
  431.8 5.8 collective-permute-start.8
  435.7 4.7 collective-permute-start.7
  437.5 5.6 collective-permute-start.6
  468.7 193.7 %all-reduce.13.cloned.1.call-start = ((), (), s32[]{:S(2)}) async-start(), calls=%async_computation.14 | async-start | bytes 18874368 | tf_op jit(solution)/shard_map/psum | solution.py:231
  469.3 234.6 %reduce-scatter.9.cloned.1.call-start = ((), (), s32[]{:S(2)}) async-start(), calls=%async_computation.12 | async-start | bytes 5242880 | tf_op jit(solution)/shard_map/reduce_scatter | solution.py:241
  555.0 172.6 %reduce-scatter.11.cloned.1.call-start = ((), (), s32[]{:S(2)}) async-start(), calls=%async_computation.13 | async-start | bytes 5242880 | tf_op jit(solution)/shard_map/reduce_scatter | solution.py:295
  652.5 139.4 %all-reduce.15.cloned.1.call-start = ((), (), s32[]{:S(2)}) async-start(), calls=%async_computation.15 | async-start | bytes 6291456 | tf_op jit(solution)/shard_map/psum | solution.py:306
  662.4 25.7 %collective-permute-start.20 = (bf16[1024,1536]{1,0:T(8,128)(2,1)}, bf16[1024,1536]{1,0:T(8,128)(2,1)}, u32[]{:S(2)}, u32[]{:S(2)}) collective-permute-start(bf16[1024,1536]{1,0:T(8,128)(2,1)} %get-tuple-element.378), channel_id=1, source_target_pairs={{0,4},{4,0},{8,12},{12,8},{16,20},{20,16},{24,28},{28,24},{1,5},{5... | collective-permute-start | bytes 9437192 | tf_op jit(solution)/shard_map/ppermute | solution.py:69
  665.0 8.4 %collective-permute-start.14 = (bf16[1024,256]{1,0:T(8,128)(2,1)S(1)}, bf16[1024,256]{1,0:T(8,128)(2,1)}, u32[]{:S(2)}, u32[]{:S(2)}) collective-permute-start(bf16[1024,256]{1,0:T(8,128)(2,1)S(1)} %fusion.98), channel_id=1, source_target_pairs={{0,4},{4,0},{8,12},{12,8},{16,20},{20,16},{24,28},{28,24},{1,5},{5... | collective-permute-start | bytes 1572872 | tf_op jit(solution)/shard_map/ppermute | solution.py:64
  669.4 11.5 %collective-permute-start.13 = (bf16[1024,512]{1,0:T(8,128)(2,1)}, bf16[1024,512]{1,0:T(8,128)(2,1)}, u32[]{:S(2)}, u32[]{:S(2)}) collective-permute-start(bf16[1024,512]{1,0:T(8,128)(2,1)} %fusion.93), channel_id=1, source_target_pairs={{0,4},{4,0},{8,12},{12,8},{16,20},{20,16},{24,28},{28,24},{1,5},{5... | collective-permute-start | bytes 3145736 | tf_op jit(solution)/shard_map/ppermute | solution.py:64
  669.9 7.7 collective-permute-start.15
  672.8 11.9 %collective-permute-start.12 = (bf16[256,2048]{1,0:T(8,128)(2,1)}, bf16[256,2048]{1,0:T(8,128)(2,1)}, u32[]{:S(2)}, u32[]{:S(2)}) collective-permute-start(bf16[256,2048]{1,0:T(8,128)(2,1)} %convolution_convert_fusion.4), channel_id=1, source_target_pairs={{0,4},{4,0},{8,12},{12,8},{16,20},{20,16},{24,28},{28,24},{1,5},{5... | collective-permute-start | bytes 3145736 | tf_op jit(solution)/shard_map/ppermute | solution.py:64
  673.3 24.7 %collective-permute-start.21 = (bf16[1024,1536]{1,0:T(8,128)(2,1)}, bf16[1024,1536]{1,0:T(8,128)(2,1)}, u32[]{:S(2)}, u32[]{:S(2)}) collective-permute-start(bf16[1024,1536]{1,0:T(8,128)(2,1)} %get-tuple-element.379), channel_id=1, source_target_pairs={{0,4},{4,0},{8,12},{12,8},{16,20},{20,16},{24,28},{28,24},{1,5},{5... | collective-permute-start | bytes 9437192 | tf_op jit(solution)/shard_map/ppermute | solution.py:69
  680.4 23.6 %collective-permute-start.22 = (bf16[768,2048]{1,0:T(8,128)(2,1)}, bf16[768,2048]{1,0:T(8,128)(2,1)}, u32[]{:S(2)}, u32[]{:S(2)}) collective-permute-start(bf16[768,2048]{1,0:T(8,128)(2,1)} %get-tuple-element.377), channel_id=1, source_target_pairs={{0,4},{4,0},{8,12},{12,8},{16,20},{20,16},{24,28},{28,24},{1,5},{5... | collective-permute-start | bytes 9437192 | tf_op jit(solution)/shard_map/ppermute | solution.py:69
  791.9 5.1 collective-permute-start.17
  796.3 5.0 collective-permute-start.16
  796.8 7.3 collective-permute-start.19
  (123 other events, 1078.8 us)
Sparse Core Ops, SparseCore 0:
  10.4 83.4 all-gather.5
  95.5 98.3 all-gather.7
  221.3 60.6 all-gather.9
  310.7 45.9 all-gather.11
  359.0 42.5 reduce-scatter.4
  414.9 42.7 reduce-scatter.6
  468.8 79.6 all-gather.13
  555.1 75.4 reduce-scatter.8
  652.6 74.9 reduce-scatter.10
Sparse Core Ops, SparseCore 1:
  145.0 140.9 all-reduce.10
  474.2 188.2 all-reduce.12
  704.1 87.8 all-reduce.14

commit v2 on v1

v2 whole, which is shorter than its diff:
```python
import math
from functools import partial

import jax
import jax.numpy as jnp
from jax import lax
from jax.experimental import pallas as pl
from jax.experimental.pallas import tpu as pltpu
from jax.sharding import PartitionSpec as P

EPSILON = 1e-06
ROPE_BASE = 1000000.0


def rope_tables(seq_len, head_dim):
    half_dim = head_dim // 2
    frequency = ROPE_BASE ** (-(jnp.arange(half_dim, dtype=jnp.float32) * 2.0 / head_dim))
    angles = jnp.arange(seq_len, dtype=jnp.float32)[:, None] * frequency[None, :]
    angles = jnp.concatenate([angles, angles], axis=1)
    return (jnp.cos(angles)[:, None, :], jnp.sin(angles)[:, None, :])


def rope_rows(seq_len, head_dim):
    cosine, sine = rope_tables(seq_len, head_dim)
    signs = jnp.where(jnp.arange(head_dim) < head_dim // 2, -1.0, 1.0)
    return cosine[:, 0, :], sine[:, 0, :] * signs[None, :]


def head_factor(raw):
    return lax.rsqrt(jnp.mean(raw * raw, axis=-1, keepdims=True) + EPSILON)


def turn(values):
    return pltpu.roll(values, values.shape[-1] // 2, 1)


def dot(left, right, contract):
    return lax.dot_general(left, right, (contract, ((), ())), preferred_element_type=jnp.float32)


def attention_kernel(
    group_size,
    block,
    length_ref,
    query_ref,
    key_ref,
    value_ref,
    query_gain_ref,
    key_gain_ref,
    cosine_ref,
    sine_ref,
    out_ref,
    query_out_ref,
    key_out_ref,
):
    seq_len, head_dim = query_ref.shape
    scale = head_dim ** (-0.5)
    length = length_ref[0]

    def post(raw, gain):
        normed = raw * head_factor(raw) * gain
        return (normed * cosine_ref[...] + turn(normed) * sine_ref[...]).astype(jnp.bfloat16)

    @pl.when(lax.rem(pl.program_id(0), group_size) == 0)
    def _():
        key_out_ref[...] = post(key_ref[...], key_gain_ref[...])

    query_out_ref[...] = post(query_ref[...], query_gain_ref[...])
    below = lax.broadcasted_iota(jnp.int32, (block, block), 0) >= lax.broadcasted_iota(
        jnp.int32, (block, block), 1
    )
    for start in range(0, seq_len, block):
        queries = query_out_ref[start : start + block, :]
        parts = []
        for first, count in ((0, start), (start, block)):
            if not count:
                continue
            scores = dot(queries, key_out_ref[first : first + count, :], ((1,), (1,))) * scale
            place = first + lax.broadcasted_iota(jnp.int32, (1, count), 1)
            scores = scores + jnp.where(place < length, 0.0, -1e30)
            if first == start:
                scores = jnp.where(below, scores, -1e30)
            parts.append((first, count, scores))
        highest = parts[0][2].max(axis=1, keepdims=True)
        for _, _, scores in parts[1:]:
            highest = jnp.maximum(highest, scores.max(axis=1, keepdims=True))
        total, result = 0.0, 0.0
        for first, count, scores in parts:
            raised = jnp.exp(scores - highest)
            total = total + raised.sum(axis=1, keepdims=True)
            values = value_ref[first : first + count, :]
            result = result + dot(raised.astype(jnp.bfloat16), values, ((1,), (0,)))
        out_ref[start : start + block, :] = (result / total).astype(jnp.bfloat16)


def attention_back_kernel(
    group_size,
    block,
    length_ref,
    query_ref,
    key_ref,
    value_ref,
    query_raw_ref,
    key_raw_ref,
    grad_ref,
    query_gain_ref,
    key_gain_ref,
    cosine_ref,
    sine_ref,
    query_grad_ref,
    key_grad_ref,
    value_grad_ref,
    query_gain_grad_ref,
    key_gain_grad_ref,
    query_sum,
    key_sum,
    value_sum,
):
    seq_len, head_dim = query_ref.shape
    scale = head_dim ** (-0.5)
    length = length_ref[0]
    head = pl.program_id(0)
    place_in_group = lax.rem(head, group_size)

    @pl.when(head == 0)
    def _():
        query_gain_grad_ref[...] = jnp.zeros_like(query_gain_grad_ref)
        key_gain_grad_ref[...] = jnp.zeros_like(key_gain_grad_ref)

    @pl.when(place_in_group == 0)
    def _():
        key_sum[...] = jnp.zeros_like(key_sum)
        value_sum[...] = jnp.zeros_like(value_sum)

    above = lax.broadcasted_iota(jnp.int32, (block, block), 0) <= lax.broadcasted_iota(
        jnp.int32, (block, block), 1
    )
    for start in range(0, seq_len, block):
        rows = slice(start, start + block)
        queries, grads = query_ref[rows, :], grad_ref[rows, :]
        parts = []
        for first, count in ((0, start), (start, block)):
            if not count:
                continue
            scores = dot(key_ref[first : first + count, :], queries, ((1,), (1,))) * scale
            place = first + lax.broadcasted_iota(jnp.int32, (count, 1), 0)
            scores = jnp.where(place < length, scores, -1e30)
            if first == start:
                scores = jnp.where(above, scores, -1e30)
            parts.append((slice(first, first + count), scores))
        highest = parts[0][1].max(axis=0, keepdims=True)
        for _, scores in parts[1:]:
            highest = jnp.maximum(highest, scores.max(axis=0, keepdims=True))
        parts = [(keys, jnp.exp(scores - highest)) for keys, scores in parts]
        total = sum(raised.sum(axis=0, keepdims=True) for _, raised in parts)
        inverse = 1.0 / total
        centre, weighted = 0.0, []
        for keys, raised in parts:
            weights = raised * inverse
            weight_grad = dot(value_ref[keys, :], grads, ((1,), (1,)))
            centre = centre + (weights * weight_grad).sum(axis=0, keepdims=True)
            value_sum[keys, :] += dot(weights.astype(jnp.bfloat16), grads, ((1,), (0,)))
            weighted.append((keys, weights, weight_grad))
        query_grad = 0.0
        for keys, weights, weight_grad in weighted:
            score_grad = (weights * (weight_grad - centre)).astype(jnp.bfloat16)
            key_sum[keys, :] += dot(score_grad, queries, ((1,), (0,)))
            query_grad = query_grad + dot(score_grad, key_ref[keys, :], ((0,), (0,)))
        query_sum[rows, :] = query_grad

    def back(total, raw, gain):
        grad = total * scale
        grad = grad * cosine_ref[...] - turn(grad) * sine_ref[...]
        factor = head_factor(raw)
        gain_grad = (grad * raw * factor).sum(axis=0, keepdims=True)
        grad = grad * gain
        shift = (grad * raw).sum(axis=1, keepdims=True) * (factor * factor * factor / head_dim)
        return (grad * factor - raw * shift).astype(jnp.bfloat16), gain_grad

    query_grad_ref[...], gain_grad = back(query_sum[...], query_raw_ref[...], query_gain_ref[...])
    query_gain_grad_ref[...] += gain_grad

    @pl.when(place_in_group == group_size - 1)
    def _():
        key_grad_ref[...], gain_grad = back(key_sum[...], key_raw_ref[...], key_gain_ref[...])
        key_gain_grad_ref[...] += gain_grad
        value_grad_ref[...] = value_sum[...].astype(jnp.bfloat16)


def attention_specs(seq_len, head_dim, group_size):
    query = pl.BlockSpec((seq_len, head_dim), lambda head: (0, head))
    key = pl.BlockSpec((seq_len, head_dim), lambda head: (0, head // group_size))
    gain = pl.BlockSpec((1, head_dim), lambda head: (0, 0))
    table = pl.BlockSpec((seq_len, head_dim), lambda head: (0, 0))
    length = pl.BlockSpec(memory_space=pltpu.SMEM)
    return length, query, key, gain, table


def attention(length, query_raw, key_raw, values, query_gain, key_gain, cosine, sine, group_size):
    seq_len, head_dim = cosine.shape
    heads = query_raw.shape[1] // head_dim
    block = math.gcd(256, seq_len)
    count, query, key, gain, table = attention_specs(seq_len, head_dim, group_size)
    pairs = heads * seq_len * (seq_len + block) // 2
    return pl.pallas_call(
        partial(attention_kernel, group_size, block),
        grid=(heads,),
        in_specs=[count, query, key, key, gain, gain, table, table],
        out_specs=[query, query, key],
        out_shape=[
            jax.ShapeDtypeStruct(query_raw.shape, jnp.bfloat16),
            jax.ShapeDtypeStruct(query_raw.shape, jnp.bfloat16),
            jax.ShapeDtypeStruct(key_raw.shape, jnp.bfloat16),
        ],
        compiler_params=pltpu.CompilerParams(vmem_limit_bytes=40 * 1024 * 1024),
        cost_estimate=pl.CostEstimate(
            flops=4 * pairs * head_dim, bytes_accessed=8 * query_raw.size, transcendentals=pairs
        ),
        name="attention",
    )(length, query_raw, key_raw, values, query_gain, key_gain, cosine, sine)


def attention_back(
    length,
    queries,
    keys,
    values,
    query_raw,
    key_raw,
    grads,
    query_gain,
    key_gain,
    cosine,
    sine,
    group_size,
):
    seq_len, head_dim = cosine.shape
    heads = query_raw.shape[1] // head_dim
    block = math.gcd(256, seq_len)
    count, query, key, gain, table = attention_specs(seq_len, head_dim, group_size)
    pairs = heads * seq_len * (seq_len + block) // 2
    rows = pltpu.VMEM((seq_len, head_dim), jnp.float32)
    return pl.pallas_call(
        partial(attention_back_kernel, group_size, block),
        grid=(heads,),
        in_specs=[count, query, key, key, query, key, query, gain, gain, table, table],
        out_specs=[query, key, key, gain, gain],
        out_shape=[
            jax.ShapeDtypeStruct(queries.shape, jnp.bfloat16),
            jax.ShapeDtypeStruct(keys.shape, jnp.bfloat16),
            jax.ShapeDtypeStruct(keys.shape, jnp.bfloat16),
            jax.ShapeDtypeStruct((1, head_dim), jnp.float32),
            jax.ShapeDtypeStruct((1, head_dim), jnp.float32),
        ],
        scratch_shapes=[rows, rows, rows],
        compiler_params=pltpu.CompilerParams(vmem_limit_bytes=40 * 1024 * 1024),
        cost_estimate=pl.CostEstimate(
            flops=10 * pairs * head_dim, bytes_accessed=12 * query_raw.size, transcendentals=pairs
        ),
        name="attention_back",
    )(length, queries, keys, values, query_raw, key_raw, grads, query_gain, key_gain, cosine, sine)


def feed_kernel(branch_steps, own_width, first_half, *refs):
    rank_ref, heads_ref, token_ref, grad_ref, out_ref, gain_ref = refs[:6]
    gate_ref, up_ref, down_ref = refs[6:9]
    refs = refs[9:] if first_half else refs[15:]
    mixed_ref, product_ref, gate_grad_ref, up_grad_ref, own_ref, root_ref = refs[:6]
    mid_ref, mixed_grad_ref, hidden, total, squares, mid = refs[6:]
    step = pl.program_id(0)
    width = out_ref.shape[1]

    @pl.when(step == 0)
    def _():
        squares[...] = jnp.zeros_like(squares)

    @pl.when(step < branch_steps)
    def _():
        part = token_ref[...].astype(jnp.float32) + dot(heads_ref[...], out_ref[...], ((1,), (0,)))
        hidden[:, pl.ds(pl.multiple_of(step * width, width), width)] = part
        squares[...] += (part * part).sum(axis=1, keepdims=True)

    @pl.when(step == branch_steps)
    def _():
        root = lax.rsqrt(squares[...] / hidden.shape[1] + EPSILON)
        root_ref[...] = root
        mixed_ref[...] = (hidden[...] * root * gain_ref[...]).astype(jnp.bfloat16)
        own_start = pl.multiple_of(rank_ref[0] * own_width, own_width)
        own_ref[...] = hidden[:, pl.ds(own_start, own_width)]
        total[...] = jnp.zeros_like(total)
        mid[...] = jnp.zeros_like(mid)

    @pl.when(step >= branch_steps)
    def _():
        gate = dot(mixed_ref[...], gate_ref[...], ((1,), (0,)))
        up = dot(mixed_ref[...], up_ref[...], ((1,), (0,)))
        product_grad = dot(grad_ref[...], down_ref[...], ((1,), (1,)))
        sigmoid = jax.nn.sigmoid(gate)
        activated = gate * sigmoid
        product_ref[...] = (activated * up).astype(jnp.bfloat16)
        slope = sigmoid * (1.0 + gate * (1.0 - sigmoid))
        gate_grad = (product_grad * up * slope).astype(jnp.bfloat16)
        up_grad = (product_grad * activated).astype(jnp.bfloat16)
        gate_grad_ref[...] = gate_grad
        up_grad_ref[...] = up_grad
        terms = gate_grad.astype(jnp.float32) * gate + up_grad.astype(jnp.float32) * up
        mid[...] += terms.sum(axis=1, keepdims=True)
        total[...] += dot(gate_grad, gate_ref[...], ((1,), (1,)))
        total[...] += dot(up_grad, up_ref[...], ((1,), (1,)))

    @pl.when(step == pl.num_programs(0) - 1)
    def _():
        mixed_grad_ref[...] = total[...].astype(jnp.bfloat16)
        mid_ref[...] = mid[...]


def feed_forward(part, earlier, rank, heads, tokens, grads, out_full, gain, gate, up, down, own):
    seq_len, model_width = tokens.shape
    half, hidden_width = seq_len // 2, gate.shape[1]
    wide = math.gcd(512, model_width)
    tile = math.gcd(512, hidden_width)
    branch_steps = model_width // wide
    steps = branch_steps + hidden_width // tile

    def first(step):
        return jnp.minimum(step, branch_steps - 1)

    def second(step):
        return jnp.maximum(step - branch_steps, 0)

    once = pl.Buffered(1)
    f32, bf16 = jnp.float32, jnp.bfloat16
    in_specs = [
        pl.BlockSpec(memory_space=pltpu.SMEM),
        pl.BlockSpec((half, heads.shape[1]), lambda i: (0, 0), pipeline_mode=once),
        pl.BlockSpec((half, wide), lambda i: (part, first(i))),
        pl.BlockSpec((half, model_width), lambda i: (part, 0), pipeline_mode=once),
        pl.BlockSpec((out_full.shape[0], wide), lambda i: (0, first(i))),
        pl.BlockSpec((1, model_width), lambda i: (0, 0)),
        pl.BlockSpec((model_width, tile), lambda i: (0, second(i))),
        pl.BlockSpec((model_width, tile), lambda i: (0, second(i))),
        pl.BlockSpec((tile, model_width), lambda i: (second(i), 0)),
    ]
    in_specs += [pl.BlockSpec(memory_space=pl.ANY)] * len(earlier)
    inner = pl.BlockSpec((half, tile), lambda i: (part, second(i)))
    out_specs = [
        pl.BlockSpec((half, model_width), lambda i: (part, 0), pipeline_mode=once),
        inner,
        inner,
        inner,
        pl.BlockSpec((half, own), lambda i: (part, 0), pipeline_mode=once),
        pl.BlockSpec((half, 1), lambda i: (part, 0), pipeline_mode=once),
        pl.BlockSpec((half, 1), lambda i: (0, 0), pipeline_mode=once),
        pl.BlockSpec((half, model_width), lambda i: (0, 0), pipeline_mode=once),
    ]
    out_shape = [
        jax.ShapeDtypeStruct((seq_len, model_width), bf16),
        jax.ShapeDtypeStruct((seq_len, hidden_width), bf16),
        jax.ShapeDtypeStruct((seq_len, hidden_width), bf16),
        jax.ShapeDtypeStruct((seq_len, hidden_width), bf16),
        jax.ShapeDtypeStruct((seq_len, own), f32),
        jax.ShapeDtypeStruct((seq_len, 1), f32),
        jax.ShapeDtypeStruct((half, 1), f32),
        jax.ShapeDtypeStruct((half, model_width), bf16),
    ]
    return pl.pallas_call(
        partial(feed_kernel, branch_steps, own, not earlier),
        grid=(steps,),
        in_specs=in_specs,
        out_specs=out_specs,
        out_shape=out_shape,
        input_output_aliases={9 + i: i for i in range(len(earlier))},
        scratch_shapes=[
            pltpu.VMEM((half, model_width), f32),
            pltpu.VMEM((half, model_width), f32),
            pltpu.VMEM((half, 1), f32),
            pltpu.VMEM((half, 1), f32),
        ],
        compiler_params=pltpu.CompilerParams(vmem_limit_bytes=58 * 1024 * 1024),
        cost_estimate=pl.CostEstimate(
            flops=2 * half * model_width * (heads.shape[1] + 5 * hidden_width),
            bytes_accessed=2 * (out_full.size + gate.size + up.size + down.size),
            transcendentals=half * hidden_width,
        ),
        name="feed_forward",
    )(rank, heads, tokens, grads, out_full, gain, gate, up, down, *earlier)


def small_sum(values, axis, size):
    total = values
    for shift in range(1, size):
        pairs = [(i, (i + shift) % size) for i in range(size)]
        total = total + lax.ppermute(values, axis, pairs)
    return total


def after(value, *others):
    return lax.optimization_barrier((value, others))[0]


def pair_sum(left, right, core, pairs):
    half = left.shape[1] // 2

    def rows(which):
        part = lax.dynamic_slice_in_dim(left, which * half, half, 1)
        return dot(part, right, ((0,), (0,)))

    received = lax.ppermute(rows(1 - core).astype(jnp.bfloat16), "dp", pairs)
    return (rows(core) + received.astype(jnp.float32)).astype(jnp.bfloat16)


def both_halves(mine, core, pairs):
    other = lax.ppermute(mine, "dp", pairs)
    parts = (jnp.where(core == 0, mine, other), jnp.where(core == 0, other, mine))
    return jnp.concatenate(parts, axis=0).astype(jnp.float32)


def local(
    tensor_size,
    dp_size,
    tokens,
    lengths,
    cotangent,
    first_gain,
    query_weight,
    key_weight,
    value_weight,
    query_gain,
    key_gain,
    out_weight,
    second_gain,
    gate_weight,
    up_weight,
    down_weight,
):
    bf16 = jnp.bfloat16
    tensor_rank = lax.axis_index("tensor")
    dp_rank = lax.axis_index("dp")
    seq_len = tokens.shape[0]
    share_width = tokens.shape[1]
    model_width = first_gain.shape[0]
    head_dim = query_gain.shape[0]
    local_heads = query_weight.shape[1] // head_dim
    local_groups = key_weight.shape[1] // head_dim
    group_size = local_heads // local_groups
    length = lengths[0]
    valid_rows = (jnp.arange(seq_len, dtype=jnp.int32) < length).astype(jnp.float32)[:, None]
    own_start = tensor_rank * share_width
    first_own = lax.dynamic_slice_in_dim(first_gain, own_start, share_width, 0)
    second_own = lax.dynamic_slice_in_dim(second_gain, own_start, share_width, 0)
    full_tokens = lax.all_gather(tokens, "tensor", axis=1, tiled=True)
    out_cols = model_width // dp_size
    out_rows = out_weight.shape[0]
    out_part = lax.dynamic_slice_in_dim(out_weight, dp_rank * out_cols, out_cols, 1)
    pieces = [out_part]
    for shift in range(1, tensor_size):
        ring = [(i, (i + shift) % tensor_size) for i in range(tensor_size)]
        pieces.append(lax.ppermute(out_part, "tensor", ring))
    full_tokens = after(full_tokens, *pieces)
    full_cot = lax.all_gather(after(cotangent, full_tokens), "tensor", axis=1, tiled=True)
    out_block = jnp.zeros((out_rows * tensor_size, out_cols), bf16)
    for shift, piece in enumerate(pieces):
        source = lax.rem(tensor_rank + tensor_size - shift, tensor_size)
        out_block = lax.dynamic_update_slice_in_dim(out_block, piece, source * out_rows, 0)
    out_full = jnp.zeros((out_rows * tensor_size, model_width), bf16)
    out_full = lax.dynamic_update_slice_in_dim(out_full, out_block, dp_rank * out_cols, 1)
    rotated_order = [[(i + 1) % dp_size for i in range(dp_size)]]
    out_full = lax.psum(out_full, "dp", axis_index_groups=rotated_order)

    token_own = tokens.astype(jnp.float32)
    token_rows = full_tokens.astype(jnp.float32)
    first_root = lax.rsqrt(jnp.mean(token_rows * token_rows, axis=1, keepdims=True) + EPSILON)
    normed = (token_rows * first_root * first_gain).astype(bf16)
    query_raw = dot(normed, query_weight, ((1,), (0,)))
    key_raw = dot(normed, key_weight, ((1,), (0,)))
    value_rows = dot(normed, value_weight, ((1,), (0,))).astype(bf16)
    cosine, sine = rope_rows(seq_len, head_dim)
    head_gains = (query_gain[None, :], key_gain[None, :])
    attended, query_rows, key_rows = attention(
        lengths, query_raw, key_raw, value_rows, *head_gains, cosine, sine, group_size
    )

    out_full = after(out_full, attended)
    attended = after(attended, full_cot)
    grad_full = (full_cot.astype(jnp.float32) * valid_rows).astype(bf16)
    grad_own = cotangent.astype(jnp.float32) * valid_rows

    half = seq_len // 2
    heads_in = (attended[:half], after(attended[half:], out_full))
    heads_parts = [lax.all_gather(part, "tensor", axis=1, tiled=True) for part in heads_in]
    rank = tensor_rank.astype(jnp.int32)[None]
    grad_parts, mid_parts, kept = [], [], []
    for part, heads_full in enumerate(heads_parts):
        *kept, mid, mixed_grad = feed_forward(
            part,
            kept,
            rank,
            heads_full,
            full_tokens,
            grad_full,
            out_full,
            second_gain[None, :],
            gate_weight,
            up_weight,
            down_weight,
            share_width,
        )
        mid_parts.append(small_sum(mid[:, 0], "tensor", tensor_size)[:, None])
        grad_parts.append(lax.psum_scatter(mixed_grad, "tensor", scatter_dimension=1, tiled=True))
    mixed_rows, product, gate_grads, up_grads, hidden_own, second_root = kept
    core = lax.rem(dp_rank, 2)
    pairs = [(i, i ^ 1) for i in range(dp_size)]
    chips = [[i for i in range(dp_size) if i % 2 == side] for side in (0, 1)]
    early = (
        pair_sum(product, grad_full, core, pairs),
        pair_sum(mixed_rows, gate_grads, core, pairs),
        pair_sum(mixed_rows, up_grads, core, pairs),
    )
    down_part = dot(after(product, *early), down_weight, ((1,), (0,))).astype(bf16)
    grad_parts, mid_parts = after((grad_parts, mid_parts), *early)
    mixed_own_grad = jnp.concatenate(grad_parts, axis=0).astype(jnp.float32)
    mid_total = jnp.concatenate(mid_parts, axis=0)
    early = lax.psum(early, "dp", axis_index_groups=chips)

    second_gain_grad = jnp.sum(mixed_own_grad * hidden_own * second_root, axis=0)
    hidden_grad = (
        grad_own
        + mixed_own_grad * second_own * second_root
        - hidden_own * second_root**2 / model_width * mid_total
    )
    hidden_grad_rows = lax.all_gather(hidden_grad.astype(bf16), "tensor", axis=1, tiled=True)
    down_part, hidden_grad_rows = lax.optimization_barrier((down_part, hidden_grad_rows))
    down_own = lax.psum_scatter(down_part, "tensor", scatter_dimension=1, tiled=True)
    grad_out = pair_sum(attended, hidden_grad_rows, core, pairs)
    attended_grad = dot(hidden_grad_rows, out_weight, ((1,), (1,))).astype(bf16)
    query_raw_grad, key_raw_grad, value_raw_grad, query_gain_grad, key_gain_grad = attention_back(
        lengths,
        query_rows,
        key_rows,
        value_rows,
        query_raw,
        key_raw,
        attended_grad,
        *head_gains,
        cosine,
        sine,
        group_size,
    )
    query_gain_grad, key_gain_grad = query_gain_grad[0], key_gain_grad[0]
    normed_grad = (
        dot(query_raw_grad, query_weight, ((1,), (1,)))
        + dot(key_raw_grad, key_weight, ((1,), (1,)))
        + dot(value_raw_grad, value_weight, ((1,), (1,)))
    )
    normed_grad = normed_grad.astype(bf16)
    normed_own_grad = lax.psum_scatter(normed_grad, "tensor", scatter_dimension=1, tiled=True)
    late = (
        grad_out,
        pair_sum(normed, query_raw_grad, core, pairs),
        pair_sum(normed, key_raw_grad, core, pairs),
        pair_sum(normed, value_raw_grad, core, pairs),
    )
    early = after(early, *late)
    down_own = after(down_own, normed_grad, *late)
    layer_out = (hidden_own + down_own.astype(jnp.float32)).astype(bf16)
    normed_own_grad = after(normed_own_grad, layer_out, *early).astype(jnp.float32)
    backwards = [group[::-1] for group in chips]
    late = lax.psum(after(late, normed_grad, *early), "dp", axis_index_groups=backwards)
    grad_down, grad_gate, grad_up = (both_halves(part, core, pairs) for part in early)
    grad_out, grad_query, grad_key, grad_value = (both_halves(part, core, pairs) for part in late)
    first_term, query_gain_grad, key_gain_grad = lax.psum(
        (
            jnp.sum(normed_own_grad * first_own * token_own, axis=1, keepdims=True),
            query_gain_grad,
            key_gain_grad,
        ),
        "tensor",
    )
    first_gain_grad = jnp.sum(normed_own_grad * token_own * first_root, axis=0)
    token_grad = (
        hidden_grad
        + normed_own_grad * first_own * first_root
        - token_own * first_root**3 / model_width * first_term
    ).astype(bf16)
    gains = jnp.concatenate([first_gain_grad, second_gain_grad, query_gain_grad, key_gain_grad])
    gains = lax.psum(gains, "dp")
    first_gain_grad, second_gain_grad, query_gain_grad, key_gain_grad = (
        gains[:share_width],
        gains[share_width : 2 * share_width],
        gains[2 * share_width : 2 * share_width + head_dim],
        gains[2 * share_width + head_dim :],
    )
    return (
        layer_out,
        token_grad,
        first_gain_grad,
        grad_query,
        grad_key,
        grad_value,
        query_gain_grad,
        key_gain_grad,
        grad_out,
        second_gain_grad,
        grad_gate,
        grad_up,
        grad_down,
    )


def solution(mesh):
    in_specs = (
        P("dp", "tensor"),
        P("dp"),
        P("dp", "tensor"),
        P(),
        P(None, "tensor"),
        P(None, "tensor"),
        P(None, "tensor"),
        P(),
        P(),
        P("tensor", None),
        P(),
        P(None, "tensor"),
        P(None, "tensor"),
        P("tensor", None),
    )
    out_specs = (
        P("dp", "tensor"),
        P("dp", "tensor"),
        P("tensor"),
        P(None, "tensor"),
        P(None, "tensor"),
        P(None, "tensor"),
        P(),
        P(),
        P("tensor", None),
        P("tensor"),
        P(None, "tensor"),
        P(None, "tensor"),
        P("tensor", None),
    )
    return jax.shard_map(
        partial(local, mesh.shape["tensor"], mesh.shape["dp"]), mesh=mesh, in_specs=in_specs, out_specs=out_specs, check_vma=False)
```

time: 822 us -> 716 us (0.87)
  matrix products: 244 us -> 93.7 us
  Pallas kernels: 0 us -> 94.5 us
  waiting for transfers between devices: 319 us -> 372 us
  local copies, waits for them, and re-layouts: 64 us -> 16.6 us
  other arithmetic: 117 us -> 70.9 us
  loops' own time: 12.5 us -> 0 us
    pallas_call x0 -> x4, Pallas kernels: none -> 94.5 us  [the longest x2 67.7 us: feed_forward(): pl.pallas_call(partial(feed_kernel, branch_steps, own, not earlier), grid...]
    dot_general x34 -> x22, matrix products: 181 us -> 93.7 us  [dot(): lax.dot_general(left, right, (contract, ((), ())), preferred_element_type...]
    dot_general x14 -> x0, matrix products: 62.6 us -> none  [the longest x4 17.5 us: block_scores(): jnp.einsum('qcgd,kcd->cgqk', query_block, key_rows, preferred_element_typ...]
    psum x1, waiting for transfers between devices: 9.69 us -> 60.2 us  [local(): early = lax.psum(early, 'dp', axis_index_groups=chips)]
    all_gather x1, waiting for transfers between devices: 0.01 us -> 45.7 us  [local(): lax.all_gather(after(cotangent, full_tokens), 'tensor', axis=1, tiled=True)]
    convert_element_type x10 -> x0, other arithmetic: 24.8 us -> none  [the longest x2 7.42 us: attend_back(): score_grad = (weights * (weight_grad - centre)).astype(bf16)]
    all_gather x1, waiting for transfers between devices: 85.1 us -> 62.1 us  [local(): full_tokens = lax.all_gather(tokens, 'tensor', axis=1, tiled=True)]
    psum x1, waiting for transfers between devices: 63 us -> 50.3 us  [local(): out_full = lax.psum(out_full, 'dp', axis_index_groups=rotated_order)]
  transfers between devices with their start and end apart: 35 -> 35, of which waited for: 13 -> 17; matrix products, arithmetic and copies ran while one was open for 49% -> 24% of each run, Pallas kernels for 0% -> 13%
where the time goes in v2:
time: 716 us; the launch traced here: 707 us
  waiting for transfers between devices  372 us (52%)
  Pallas kernels  94.5 us (13%)
  matrix products  93.7 us (13%)
  other arithmetic  70.9 us (10%)
  blocking collectives  23.4 us (3%)
  starting transfers between devices  18.5 us (3%)
  between operations  17.2 us (2%)
  local copies, waits for them, and re-layouts  16.6 us (2%)
    dot_general x22, matrix products, dot(): lax.dot_general(left, right, (contract, ((), ())), preferred_element_type...  93.7 us
    all_gather x1, waiting for transfers between devices, local(): lax.all_gather(hidden_grad.astype(bf16), 'tensor', axis=1, tiled=True)  68.1 us
    pallas_call x2, Pallas kernels, feed_forward(): pl.pallas_call(partial(feed_kernel, branch_steps, own, not earlier), grid...  67.7 us
    all_gather x1, waiting for transfers between devices, local(): full_tokens = lax.all_gather(tokens, 'tensor', axis=1, tiled=True)  62.1 us
    psum x1, waiting for transfers between devices, local(): early = lax.psum(early, 'dp', axis_index_groups=chips)  60.2 us
    psum x1, waiting for transfers between devices, local(): out_full = lax.psum(out_full, 'dp', axis_index_groups=rotated_order)  50.3 us
    all_gather x1, waiting for transfers between devices, local(): lax.all_gather(after(cotangent, full_tokens), 'tensor', axis=1, tiled=True)  45.7 us
    psum x1, waiting for transfers between devices, local(): lax.psum(after(late, normed_grad, *early), 'dp', axis_index_groups=backwa...  37.8 us
  transfers between devices with their start and end apart: 35, of which 17 were waited for; matrix products, arithmetic and copies ran while one was open for 24% of the time, Pallas kernels for 13%

profile of v2, /device:TPU:0, one launch (start us, length us, event | category | flops | bytes accessed | tf_op | source)
XLA Modules:
  0.0 707.2 jit_solution(15202098447793758931)
XLA Ops:
  16.9 5.4 collective-permute-done
  22.3 21.8 %collective-permute-done.1 = bf16[512,256]{1,0:T(8,128)(2,1)} collective-permute-done((bf16[512,256]{1,0:T(8,128)(2,1)S(1)}, bf16[512,256]{1,0:T(8,128)(2,1)}, u32[]{:S(2)}, u32[]{:S(2)}) %collective-permute-start.1) | collective-permute-done | bytes 262176 | tf_op jit(solution)/shard_map/ppermute | solution.py:458
  44.1 62.1 %all-gather.6.cloned.1.call-done.refs_2_ = bf16[1024,2048]{1,0:T(8,128)(2,1)} async-done(((bf16[1024,512]{1,0:T(8,128)(2,1)}), bf16[1024,2048]{1,0:T(8,128)(2,1)}) %all-gather.6.cloned.1.call-update) | async-done | bytes 4194320 | tf_op jit(solution)/shard_map/all_gather | solution.py:451
  108.2 4.5 broadcast_in_dim.50
  128.4 10.8 %attention.1 = (bf16[1024,512]{1,0:T(8,128)(2,1)S(1)}, bf16[1024,512]{1,0:T(8,128)(2,1)S(1)}, bf16[1024,256]{1,0:T(8,128)(2,1)S(1)}) custom-call(s32[1]{0:T(128)} %copy.52.length_ref, f32[1024,512]{1,0:T(8,128)S(1)} %fusion.93.query_ref.query_raw_ref, f32[1024,256]{1,0:T(8,128)S(1)} %fusion.94.key_ref.key_raw_ref, ...), custom_call_target="tpu_custom_call" | custom-call | flops 1342177280 | bytes 4194304 | tf_op jit(solution)/shard_map/attention/pallas_call | solution.py:205
  142.2 45.7 %all-gather.8.cloned.1.call-done = bf16[1024,2048]{1,0:T(8,128)(2,1)} async-done(((bf16[1024,512]{1,0:T(8,128)(2,1)}), bf16[1024,2048]{1,0:T(8,128)(2,1)}) %all-gather.8.cloned.1.call-update) | async-done | bytes 4194320 | tf_op jit(solution)/shard_map/all_gather | solution.py:460
  189.0 50.3 %all-reduce.7.cloned.1.call-done.refs_4_ = bf16[2048,2048]{1,0:T(8,128)(2,1)} async-done(((bf16[2048,2048]{1,0:T(8,128)(2,1)}), bf16[2048,2048]{1,0:T(8,128)(2,1)}) %all-reduce.7.cloned.1.call-update) | async-done | bytes 8388624 | tf_op jit(solution)/shard_map/psum | solution.py:468
  239.9 4.9 multiply_convert_fusion.refs_3_
  244.9 34.0 %feed_forward.2 = (bf16[1024,2048]{1,0:T(8,128)(2,1)}, bf16[1024,1536]{1,0:T(8,128)(2,1)}, bf16[1024,1536]{1,0:T(8,128)(2,1)}, bf16[1024,1536]{1,0:T(8,128)(2,1)...) custom-call(s32[1]{0:T(128)} %bitcast.refs_0_, ...), custom_call_target="tpu_custom_call" | custom-call | flops 20401094656 | bytes 27262976 | tf_op jit(solution)/shard_map/feed_forward/pallas_call | solution.py:366
  279.1 6.4 all-gather.10.cloned.1.call-done.refs_1_
  285.5 33.7 %feed_forward.3 = (bf16[1024,2048]{1,0:T(8,128)(2,1)}, bf16[1024,1536]{1,0:T(8,128)(2,1)}, bf16[1024,1536]{1,0:T(8,128)(2,1)}, bf16[1024,1536]{1,0:T(8,128)(2,1)...) custom-call(s32[1]{0:T(128)} %bitcast.refs_0_, ...), custom_call_target="tpu_custom_call", output_to_operand_aliasing={{0}: (9, {}), {1}: (10, {}), {2}: (11, {}), {3}: (12, {}), ... | custom-call | flops 20401094656 | bytes 27262976 | tf_op jit(solution)/shard_map/feed_forward/pallas_call | solution.py:366
  319.3 7.8 %convolution_convert_fusion.2 = bf16[1024,1536]{1,0:T(8,128)(2,1)} fusion(bf16[1024,1536]{1,0:T(8,128)(2,1)} %get-tuple-element.73, bf16[1024,2048]{1,0:T(8,128)(2,1)} %get-tuple-element.72, s32[]{:T(128)S(6)} %select_n.139), kind=kOutput, calls=%fused_computation.15 | convolution fusion | flops 3222798336 | bytes 8388612 | tf_op jit(solution)/shard_map/dot_general | solution.py:38
  327.1 4.9 convolution_convert_fusion.1
  332.8 7.8 %convolution_convert_fusion.3 = bf16[768,2048]{1,0:T(8,128)(2,1)} fusion(bf16[1024,2048]{1,0:T(8,128)(2,1)} %multiply_convert_fusion.refs_3_, bf16[1024,1536]{1,0:T(8,128)(2,1)} %get-tuple-element.75, s32[]{:T(128)S(6)} %select_n.137), kind=kOutput, calls=%fused_computation.16 | convolution fusion | flops 3222798336 | bytes 8912900 | tf_op jit(solution)/shard_map/dot_general | solution.py:38
  356.0 8.8 %add_convert_fusion.2 = bf16[1024,1536]{1,0:T(8,128)(2,1)} fusion(bf16[1024,1536]{1,0:T(8,128)(2,1)} %collective-permute-done.4, bf16[1024,1536]{1,0:T(8,128)(2,1)} %get-tuple-element.73, bf16[1024,2048]{1,0:T(8,128)(2,1)} %get-tuple-element.72, s32[]{:T(128)S(6)} %select_n.138), kind=kOutput, calls=%fused_computation.11 | convolution fusion | flops 3225944064 | bytes 11534340 | tf_op jit(solution)/shard_map/dot_general | solution.py:38
  364.8 6.5 add_convert_fusion.1
  371.3 6.4 add_convert_fusion.3
  383.0 11.0 %convolution_convert_fusion = bf16[1024,2048]{1,0:T(8,128)(2,1)} fusion(bf16[1024,1536]{1,0:T(8,128)(2,1)} %get-tuple-element.75, bf16[1536,2048]{1,0:T(8,128)(2,1)} %refs_8_.3), kind=kOutput, calls=%fused_computation.13 | convolution fusion | flops 6444548096 | bytes 13631488 | tf_op jit(solution)/shard_map/dot_general | solution.py:38
  394.0 68.1 %all-gather.14.cloned.1.call-done = bf16[1024,2048]{1,0:T(8,128)(2,1)} async-done(((bf16[1024,512]{1,0:T(8,128)(2,1)}), bf16[1024,2048]{1,0:T(8,128)(2,1)}) %all-gather.14.cloned.1.call-update) | async-done | bytes 4194320 | tf_op jit(solution)/shard_map/all_gather | solution.py:531
  462.3 5.4 convolution_convert_fusion.5.grad_ref
  467.8 16.0 %attention_back.1 = (bf16[1024,512]{1,0:T(8,128)(2,1)S(1)}, bf16[1024,256]{1,0:T(8,128)(2,1)S(1)}, bf16[1024,256]{1,0:T(8,128)(2,1)S(1)}, f32[1,128]{1,0:T(1,128)S(1)}, f32[1,128]{1,0:T(1,128)S(1)}) custom-call(s32[1]{0:T(128)} %copy.52.length_ref, bf16[1024,512]{1,0:T(8,128)(2,1)S(1)} %copy-done.17, bf16[1024,256]{1,0:T(8,128)(2,1)S(1)} %copy-done.21, ...), custom_call_target="tpu_custom_call" | custom-call | flops 3355443200 | bytes 6291456 | tf_op jit(solution)/shard_map/attention_back/pallas_call | solution.py:243
  491.2 4.3 fusion.43
  515.9 60.2 %all-reduce.9.cloned.1.call-done = (bf16[768,2048]{1,0:T(8,128)(2,1)}, bf16[1024,1536]{1,0:T(8,128)(2,1)}, bf16[1024,1536]{1,0:T(8,128)(2,1)}) async-done(((bf16[768,2048]{1,0:T(8,128)(2,1)}, bf16[1024,1536]{1,0:T(8,128)(2,1)}, bf16[1024,1536]{1,0:T(8,128)(2,1)}), (bf16[768,2048]{1,0:T(8,128)(2,1)}, bf16[1024,1536]{1,0:T(8,128)(2,1)}, bf16[1024,1536]{1,0:T(8,128)(2,1)})) %all-reduce.9.cloned.1.call-update) | async-done | bytes 9437200 | tf_op jit(solution)/shard_map/psum | solution.py:523
  576.7 5.4 collective-permute-done.20
  585.4 6.6 maximum_convert_fusion
  592.0 5.0 broadcast_select_fusion.3
  597.0 5.1 broadcast_select_fusion.1
  602.4 6.6 maximum_convert_fusion.1
  608.9 8.7 %maximum_convert_fusion.2 = f32[1536,2048]{1,0:T(8,128)} fusion(bf16[768,2048]{1,0:T(8,128)(2,1)} %get-tuple-element.122, bf16[768,2048]{1,0:T(8,128)(2,1)S(1)} %get-tuple-element.121), kind=kLoop, calls=%fused_computation.9 | loop fusion | flops 12582912 | bytes 18874368 | tf_op jit(solution)/shard_map/convert_element_type | solution.py:415
  622.8 11.1 %all-reduce = (f32[1024,1]{0,1:T(1,128)S(1)}, f32[128]{0:T(128)S(1)}, f32[128]{0:T(128)S(1)}) all-reduce(f32[1024,1]{0,1:T(1,128)S(1)} %bitcast.49, f32[128]{0:T(128)S(1)} %bitcast.44, f32[128]{0:T(128)S(1)} %bitcast.43), channel_id=1, replica_groups=mesh['dp'=8,'tensor'=4] {'tensor'}, use_global_device_ids=true, to_apply=%region_10.11 | all-reduce | flops 1280 | bytes 10240 | tf_op jit(solution)/shard_map/psum | solution.py:571
  633.9 12.4 %psum.91 = f32[1280]{0:T(1024)S(1)} all-reduce(f32[1280]{0:T(1024)S(1)} %pad_maximum_fusion.2), channel_id=1, replica_groups=mesh['dp'=8,'tensor'=4] {'dp'}, use_global_device_ids=true, to_apply=%region_15.16 | all-reduce | flops 1280 | bytes 10240 | tf_op jit(solution)/shard_map/psum | solution.py:586
  646.9 37.8 %all-reduce.11.cloned.1.call-done = (bf16[1024,512]{1,0:T(8,128)(2,1)}, bf16[1024,256]{1,0:T(8,128)(2,1)}, bf16[1024,256]{1,0:T(8,128)(2,1)}, bf16[256,2048]{1,0:T(8,128)(2,1)}) async-done(((bf16[1024,512]{1,0:T(8,128)(2,1)}, bf16[1024,256]{1,0:T(8,128)(2,1)}, bf16[1024,256]{1,0:T(8,128)(2,1)}, bf16[256,2048]{1,0:T(8,128)(2,1)}), (bf16[1024,512]{1,0:T(8,128)(2,1)}, bf16[1024,256]{1,0:T(8,128)(2,1)}, ...) | async-done | bytes 3145744 | tf_op jit(solution)/shard_map/psum | solution.py:568
  (235 shorter events, 104.7 us)
Async XLA Ops:
  8.0 98.1 %all-gather.6.cloned.1.call-start = ((), (), s32[]{:S(2)}) async-start(), calls=%async_computation.4 | async-start | bytes 5242880 | tf_op jit(solution)/shard_map/all_gather | solution.py:451
  8.8 179.2 %all-gather.8.cloned.1.call-start = ((), (), s32[]{:S(2)}) async-start(), calls=%async_computation.5 | async-start | bytes 5242880 | tf_op jit(solution)/shard_map/all_gather | solution.py:460
  9.9 12.4 %collective-permute-start = (bf16[512,256]{1,0:T(8,128)(2,1)S(1)}, bf16[512,256]{1,0:T(8,128)(2,1)S(1)}, u32[]{:S(2)}, u32[]{:S(2)}) collective-permute-start(bf16[512,256]{1,0:T(8,128)(2,1)S(1)} %get-tuple-element.120), channel_id=1, source_target_pairs={{0,1},{1,2},{2,3},{3,0},{4,5},{5,6},{6,7},{7,4},{8,9},{9,10},{10,1... | collective-permute-start | bytes 786440 | tf_op jit(solution)/shard_map/ppermute | solution.py:458
  13.0 31.1 %collective-permute-start.1 = (bf16[512,256]{1,0:T(8,128)(2,1)S(1)}, bf16[512,256]{1,0:T(8,128)(2,1)}, u32[]{:S(2)}, u32[]{:S(2)}) collective-permute-start(bf16[512,256]{1,0:T(8,128)(2,1)S(1)} %get-tuple-element.120), channel_id=1, source_target_pairs={{0,2},{1,3},{2,0},{3,1},{4,6},{5,7},{6,4},{7,5},{8,10},{9,11},{10,... | collective-permute-start | bytes 786440 | tf_op jit(solution)/shard_map/ppermute | solution.py:458
  15.6 28.5 %collective-permute-start.2 = (bf16[512,256]{1,0:T(8,128)(2,1)S(1)}, bf16[512,256]{1,0:T(8,128)(2,1)}, u32[]{:S(2)}, u32[]{:S(2)}) collective-permute-start(bf16[512,256]{1,0:T(8,128)(2,1)S(1)} %get-tuple-element.120), channel_id=1, source_target_pairs={{0,3},{1,0},{2,1},{3,2},{4,7},{5,4},{6,5},{7,6},{8,11},{9,8},{10,9... | collective-permute-start | bytes 786440 | tf_op jit(solution)/shard_map/ppermute | solution.py:458
  106.1 133.2 %all-reduce.7.cloned.1.call-start = ((), (), s32[]{:S(2)}) async-start(), calls=%async_computation.6 | async-start | bytes 16777216 | tf_op jit(solution)/shard_map/psum | solution.py:468
  113.7 131.2 %all-gather.12.cloned.1.call-start = ((), (), s32[]{:S(2)}) async-start(), calls=%async_computation.8 | async-start | bytes 2621440 | tf_op jit(solution)/shard_map/all_gather | solution.py:490
  189.0 96.5 %all-gather.10.cloned.1.call-start = ((), (), s32[]{:S(2)}) async-start(), calls=%async_computation.7 | async-start | bytes 2621440 | tf_op jit(solution)/shard_map/all_gather | solution.py:490
  239.4 138.3 %reduce-scatter.5.cloned.1.call-start = ((), (), s32[]{:S(2)}) async-start(), calls=%async_computation.9 | async-start | bytes 2621440 | tf_op jit(solution)/shard_map/reduce_scatter | solution.py:509
  278.9 98.8 %reduce-scatter.7.cloned.1.call-start = ((), (), s32[]{:S(2)}) async-start(), calls=%async_computation.10 | async-start | bytes 2621440 | tf_op jit(solution)/shard_map/reduce_scatter | solution.py:509
  327.1 28.9 %collective-permute-start.4 = (bf16[1024,1536]{1,0:T(8,128)(2,1)}, bf16[1024,1536]{1,0:T(8,128)(2,1)}, u32[]{:S(2)}, u32[]{:S(2)}) collective-permute-start(bf16[1024,1536]{1,0:T(8,128)(2,1)} %convolution_convert_fusion.2), channel_id=1, source_target_pairs={{0,4},{4,0},{8,12},{12,8},{16,20},{20,16},{24,28},{28,24},{1,5},{5... | collective-permute-start | bytes 9437192 | tf_op jit(solution)/shard_map/ppermute | solution.py:408
  332.1 32.7 %collective-permute-start.5 = (bf16[1024,1536]{1,0:T(8,128)(2,1)}, bf16[1024,1536]{1,0:T(8,128)(2,1)}, u32[]{:S(2)}, u32[]{:S(2)}) collective-permute-start(bf16[1024,1536]{1,0:T(8,128)(2,1)} %convolution_convert_fusion.1), channel_id=1, source_target_pairs={{0,4},{4,0},{8,12},{12,8},{16,20},{20,16},{24,28},{28,24},{1,5},{5... | collective-permute-start | bytes 9437192 | tf_op jit(solution)/shard_map/ppermute | solution.py:408
  332.6 129.6 %all-gather.14.cloned.1.call-start = ((), (), s32[]{:S(2)}) async-start(), calls=%async_computation.11 | async-start | bytes 5242880 | tf_op jit(solution)/shard_map/all_gather | solution.py:531
  340.7 30.6 %collective-permute-start.3 = (bf16[768,2048]{1,0:T(8,128)(2,1)}, bf16[768,2048]{1,0:T(8,128)(2,1)}, u32[]{:S(2)}, u32[]{:S(2)}) collective-permute-start(bf16[768,2048]{1,0:T(8,128)(2,1)} %convolution_convert_fusion.3), channel_id=1, source_target_pairs={{0,4},{4,0},{8,12},{12,8},{16,20},{20,16},{24,28},{28,24},{1,5},{5... | collective-permute-start | bytes 9437192 | tf_op jit(solution)/shard_map/ppermute | solution.py:408
  341.9 4.8 collective-permute-start.7
  344.5 5.4 collective-permute-start.6
  349.9 5.8 collective-permute-start.10
  350.4 5.6 collective-permute-start.9
  381.9 194.2 %all-reduce.9.cloned.1.call-start = ((), (), s32[]{:S(2)}) async-start(), calls=%async_computation.14 | async-start | bytes 18874368 | tf_op jit(solution)/shard_map/psum | solution.py:523
  382.5 214.5 %reduce-scatter.9.cloned.1.call-start = ((), (), s32[]{:S(2)}) async-start(), calls=%async_computation.12 | async-start | bytes 5242880 | tf_op jit(solution)/shard_map/reduce_scatter | solution.py:533
  462.2 158.5 %reduce-scatter.11.cloned.1.call-start = ((), (), s32[]{:S(2)}) async-start(), calls=%async_computation.13 | async-start | bytes 5242880 | tf_op jit(solution)/shard_map/reduce_scatter | solution.py:556
  490.9 193.8 %all-reduce.11.cloned.1.call-start = ((), (), s32[]{:S(2)}) async-start(), calls=%async_computation.15 | async-start | bytes 6291456 | tf_op jit(solution)/shard_map/psum | solution.py:568
  495.4 13.3 %collective-permute-start.13 = (bf16[1024,512]{1,0:T(8,128)(2,1)}, bf16[1024,512]{1,0:T(8,128)(2,1)}, u32[]{:S(2)}, u32[]{:S(2)}) collective-permute-start(bf16[1024,512]{1,0:T(8,128)(2,1)} %fusion.43), channel_id=1, source_target_pairs={{0,4},{4,0},{8,12},{12,8},{16,20},{20,16},{24,28},{28,24},{1,5},{5... | collective-permute-start | bytes 3145736 | tf_op jit(solution)/shard_map/ppermute | solution.py:408
  497.1 5.3 collective-permute-start.14
  499.2 6.9 collective-permute-start.15
  502.1 10.4 %collective-permute-start.12 = (bf16[256,2048]{1,0:T(8,128)(2,1)}, bf16[256,2048]{1,0:T(8,128)(2,1)}, u32[]{:S(2)}, u32[]{:S(2)}) collective-permute-start(bf16[256,2048]{1,0:T(8,128)(2,1)} %convolution_convert_fusion.4), channel_id=1, source_target_pairs={{0,4},{4,0},{8,12},{12,8},{16,20},{20,16},{24,28},{28,24},{1,5},{5... | collective-permute-start | bytes 3145736 | tf_op jit(solution)/shard_map/ppermute | solution.py:408
  576.1 6.0 collective-permute-start.20
  576.1 15.9 %collective-permute-start.21 = (bf16[1024,1536]{1,0:T(8,128)(2,1)}, bf16[1024,1536]{1,0:T(8,128)(2,1)}, u32[]{:S(2)}, u32[]{:S(2)}) collective-permute-start(bf16[1024,1536]{1,0:T(8,128)(2,1)} %get-tuple-element.95), channel_id=1, source_target_pairs={{0,4},{4,0},{8,12},{12,8},{16,20},{20,16},{24,28},{28,24},{1,5},{5... | collective-permute-start | bytes 9437192 | tf_op jit(solution)/shard_map/ppermute | solution.py:413
  576.6 20.4 %collective-permute-start.22 = (bf16[768,2048]{1,0:T(8,128)(2,1)}, bf16[768,2048]{1,0:T(8,128)(2,1)}, u32[]{:S(2)}, u32[]{:S(2)}) collective-permute-start(bf16[768,2048]{1,0:T(8,128)(2,1)} %get-tuple-element.93), channel_id=1, source_target_pairs={{0,4},{4,0},{8,12},{12,8},{16,20},{20,16},{24,28},{28,24},{1,5},{5... | collective-permute-start | bytes 9437192 | tf_op jit(solution)/shard_map/ppermute | solution.py:413
  684.7 5.1 collective-permute-start.17
  689.1 5.0 collective-permute-start.16
  689.6 7.3 %collective-permute-start.19 = (bf16[256,2048]{1,0:T(8,128)(2,1)S(1)}, bf16[256,2048]{1,0:T(8,128)(2,1)S(1)}, u32[]{:S(2)}, u32[]{:S(2)}) collective-permute-start(bf16[256,2048]{1,0:T(8,128)(2,1)S(1)} %copy-done.38), channel_id=1, source_target_pairs={{0,4},{4,0},{8,12},{12,8},{16,20},{20,16},{24,28},{28,24},{1,5},{5... | collective-permute-start | bytes 3145736 | tf_op jit(solution)/shard_map/ppermute | solution.py:413
  (58 other events, 458.8 us)
Sparse Core Ops, SparseCore 0:
  10.4 95.6 all-gather.5
  107.7 80.2 all-gather.7
  190.1 44.4 all-gather.11
  239.5 45.9 all-gather.9
  288.3 42.5 reduce-scatter.4
  333.1 43.5 reduce-scatter.6
  382.0 80.1 all-gather.13
  465.1 75.2 reduce-scatter.8
  543.4 77.2 reduce-scatter.10
Sparse Core Ops, SparseCore 1:
  113.8 125.5 all-reduce.6
  387.3 188.7 all-reduce.8
  597.1 87.6 all-reduce.10

commit v3 on v2

--- a/solution.py
+++ b/solution.py
@@ -88,7 +88,7 @@
         for first, count, scores in parts:
             raised = jnp.exp(scores - highest)
             total = total + raised.sum(axis=1, keepdims=True)
-            values = value_ref[first : first + count, :]
+            values = value_ref[first : first + count, :].astype(jnp.bfloat16)
             result = result + dot(raised.astype(jnp.bfloat16), values, ((1,), (0,)))
         out_ref[start : start + block, :] = (result / total).astype(jnp.bfloat16)
 
@@ -99,9 +99,9 @@
     length_ref,
     query_ref,
     key_ref,
-    value_ref,
     query_raw_ref,
     key_raw_ref,
+    value_raw_ref,
     grad_ref,
     query_gain_ref,
     key_gain_ref,
@@ -112,6 +112,7 @@
     value_grad_ref,
     query_gain_grad_ref,
     key_gain_grad_ref,
+    row_ref,
     query_sum,
     key_sum,
     value_sum,
@@ -126,6 +127,7 @@
     def _():
         query_gain_grad_ref[...] = jnp.zeros_like(query_gain_grad_ref)
         key_gain_grad_ref[...] = jnp.zeros_like(key_gain_grad_ref)
+        row_ref[...] = jnp.zeros_like(row_ref)
 
     @pl.when(place_in_group == 0)
     def _():
@@ -157,7 +159,8 @@
         centre, weighted = 0.0, []
         for keys, raised in parts:
             weights = raised * inverse
-            weight_grad = dot(value_ref[keys, :], grads, ((1,), (1,)))
+            values = value_raw_ref[keys, :].astype(jnp.bfloat16)
+            weight_grad = dot(values, grads, ((1,), (1,)))
             centre = centre + (weights * weight_grad).sum(axis=0, keepdims=True)
             value_sum[keys, :] += dot(weights.astype(jnp.bfloat16), grads, ((1,), (0,)))
             weighted.append((keys, weights, weight_grad))
@@ -175,7 +178,9 @@
         gain_grad = (grad * raw * factor).sum(axis=0, keepdims=True)
         grad = grad * gain
         shift = (grad * raw).sum(axis=1, keepdims=True) * (factor * factor * factor / head_dim)
-        return (grad * factor - raw * shift).astype(jnp.bfloat16), gain_grad
+        grad = (grad * factor - raw * shift).astype(jnp.bfloat16)
+        row_ref[...] += (grad.astype(jnp.float32) * raw).sum(axis=1, keepdims=True)
+        return grad, gain_grad
 
     query_grad_ref[...], gain_grad = back(query_sum[...], query_raw_ref[...], query_gain_ref[...])
     query_gain_grad_ref[...] += gain_grad
@@ -184,81 +189,88 @@
     def _():
         key_grad_ref[...], gain_grad = back(key_sum[...], key_raw_ref[...], key_gain_ref[...])
         key_gain_grad_ref[...] += gain_grad
-        value_grad_ref[...] = value_sum[...].astype(jnp.bfloat16)
-
-
-def attention_specs(seq_len, head_dim, group_size):
-    query = pl.BlockSpec((seq_len, head_dim), lambda head: (0, head))
-    key = pl.BlockSpec((seq_len, head_dim), lambda head: (0, head // group_size))
+        value_grad = value_sum[...].astype(jnp.bfloat16)
+        value_grad_ref[...] = value_grad
+        terms = value_grad.astype(jnp.float32) * value_raw_ref[...]
+        row_ref[...] += terms.sum(axis=1, keepdims=True)
+
+
+def attention_specs(seq_len, head_dim, heads, groups):
+    size = heads // groups
+
+    def columns(place):
+        return pl.BlockSpec((seq_len, head_dim), lambda head: (0, place(head)))
+
+    raw = [
+        columns(lambda head: head),
+        columns(lambda head: heads + head // size),
+        columns(lambda head: heads + groups + head // size),
+    ]
+    key = columns(lambda head: head // size)
     gain = pl.BlockSpec((1, head_dim), lambda head: (0, 0))
-    table = pl.BlockSpec((seq_len, head_dim), lambda head: (0, 0))
     length = pl.BlockSpec(memory_space=pltpu.SMEM)
-    return length, query, key, gain, table
-
-
-def attention(length, query_raw, key_raw, values, query_gain, key_gain, cosine, sine, group_size):
+    return length, raw, key, gain, columns(lambda head: 0)
+
+
+def attention(length, raw, query_gain, key_gain, cosine, sine, heads, groups):
     seq_len, head_dim = cosine.shape
-    heads = query_raw.shape[1] // head_dim
     block = math.gcd(256, seq_len)
-    count, query, key, gain, table = attention_specs(seq_len, head_dim, group_size)
+    count, columns, key, gain, table = attention_specs(seq_len, head_dim, heads, groups)
     pairs = heads * seq_len * (seq_len + block) // 2
+    wide = jax.ShapeDtypeStruct((seq_len, heads * head_dim), jnp.bfloat16)
     return pl.pallas_call(
-        partial(attention_kernel, group_size, block),
+        partial(attention_kernel, heads // groups, block),
         grid=(heads,),
-        in_specs=[count, query, key, key, gain, gain, table, table],
-        out_specs=[query, query, key],
+        in_specs=[count, *columns, gain, gain, table, table],
+        out_specs=[columns[0], columns[0], key],
         out_shape=[
-            jax.ShapeDtypeStruct(query_raw.shape, jnp.bfloat16),
-            jax.ShapeDtypeStruct(query_raw.shape, jnp.bfloat16),
-            jax.ShapeDtypeStruct(key_raw.shape, jnp.bfloat16),
+            wide,
+            wide,
+            jax.ShapeDtypeStruct((seq_len, groups * head_dim), jnp.bfloat16),
         ],
         compiler_params=pltpu.CompilerParams(vmem_limit_bytes=40 * 1024 * 1024),
         cost_estimate=pl.CostEstimate(
-            flops=4 * pairs * head_dim, bytes_accessed=8 * query_raw.size, transcendentals=pairs
+            flops=4 * pairs * head_dim, bytes_accessed=6 * raw.size, transcendentals=pairs
         ),
         name="attention",
-    )(length, query_raw, key_raw, values, query_gain, key_gain, cosine, sine)
+    )(length, raw, raw, raw, query_gain, key_gain, cosine, sine)
 
 
 def attention_back(
-    length,
-    queries,
-    keys,
-    values,
-    query_raw,
-    key_raw,
-    grads,
-    query_gain,
-    key_gain,
-    cosine,
-    sine,
-    group_size,
+    length, queries, keys, raw, grads, query_gain, key_gain, cosine, sine, heads, groups
 ):
     seq_len, head_dim = cosine.shape
-    heads = query_raw.shape[1] // head_dim
     block = math.gcd(256, seq_len)
-    count, query, key, gain, table = attention_specs(seq_len, head_dim, group_size)
+    count, columns, key, gain, table = attention_specs(seq_len, head_dim, heads, groups)
     pairs = heads * seq_len * (seq_len + block) // 2
     rows = pltpu.VMEM((seq_len, head_dim), jnp.float32)
     return pl.pallas_call(
-        partial(attention_back_kernel, group_size, block),
+        partial(attention_back_kernel, heads // groups, block),
         grid=(heads,),
-        in_specs=[count, query, key, key, query, key, query, gain, gain, table, table],
-        out_specs=[query, key, key, gain, gain],
+        in_specs=[count, columns[0], key, *columns, columns[0], gain, gain, table, table],
+        out_specs=[
+            columns[0],
+            key,
+            key,
+            gain,
+            gain,
+            pl.BlockSpec((seq_len, 1), lambda head: (0, 0)),
+        ],
         out_shape=[
             jax.ShapeDtypeStruct(queries.shape, jnp.bfloat16),
             jax.ShapeDtypeStruct(keys.shape, jnp.bfloat16),
             jax.ShapeDtypeStruct(keys.shape, jnp.bfloat16),
             jax.ShapeDtypeStruct((1, head_dim), jnp.float32),
             jax.ShapeDtypeStruct((1, head_dim), jnp.float32),
+            jax.ShapeDtypeStruct((seq_len, 1), jnp.float32),
         ],
         scratch_shapes=[rows, rows, rows],
         compiler_params=pltpu.CompilerParams(vmem_limit_bytes=40 * 1024 * 1024),
         cost_estimate=pl.CostEstimate(
-            flops=10 * pairs * head_dim, bytes_accessed=12 * query_raw.size, transcendentals=pairs
+            flops=10 * pairs * head_dim, bytes_accessed=10 * raw.size, transcendentals=pairs
         ),
         name="attention_back",
-    )(length, queries, keys, values, query_raw, key_raw, grads, query_gain, key_gain, cosine, sine)
+    )(length, queries, keys, raw, raw, raw, grads, query_gain, key_gain, cosine, sine)
 
 
 def feed_kernel(branch_steps, own_width, first_half, *refs):
@@ -409,10 +421,76 @@
     return (rows(core) + received.astype(jnp.float32)).astype(jnp.bfloat16)
 
 
-def both_halves(mine, core, pairs):
+def halving_sum(value, bits, rank, size, gates):
+    for bit in bits:
+        half = value.shape[0] // 2
+        side = lax.rem(rank >> bit, 2)
+        pairs = [(i, i ^ (1 << bit)) for i in range(size)]
+        sent = lax.dynamic_slice_in_dim(value, (1 - side) * half, half, 0)
+        kept = lax.dynamic_slice_in_dim(value, side * half, half, 0).astype(jnp.float32)
+        value = (kept + lax.ppermute(sent, "dp", pairs).astype(jnp.float32)).astype(jnp.bfloat16)
+    for place, bit in enumerate(reversed(bits)):
+        value = after(value, gates[min(place, len(gates) - 1)])
+        side = lax.rem(rank >> bit, 2)
+        pairs = [(i, i ^ (1 << bit)) for i in range(size)]
+        other = lax.ppermute(value, "dp", pairs)
+        parts = (jnp.where(side == 0, value, other), jnp.where(side == 0, other, value))
+        value = jnp.concatenate(parts, axis=0)
+    return value
+
+
+def chip_sum(value, rank, size, gates):
+    bits = list(range(1, size.bit_length() - 1))
+    half = value.shape[0] // 2
+    parts = (
+        halving_sum(value[:half], bits, rank, size, gates),
+        halving_sum(value[half:], bits[::-1], rank, size, gates),
+    )
+    return jnp.concatenate(parts, axis=0)
+
+
+def join_kernel(steps, core_ref, mine_ref, other_ref, *out_refs):
+    own = (pl.program_id(0) < steps) == (core_ref[0] == 0)
+
+    def write(source_ref):
+        start = 0
+        for out_ref in out_refs:
+            width = out_ref.shape[1]
+            out_ref[...] = source_ref[:, start : start + width].astype(jnp.float32)
+            start += width
+
+    pl.when(own)(lambda: write(mine_ref))
+    pl.when(jnp.logical_not(own))(lambda: write(other_ref))
+
+
+def both_halves(mine, core, pairs, widths):
     other = lax.ppermute(mine, "dp", pairs)
-    parts = (jnp.where(core == 0, mine, other), jnp.where(core == 0, other, mine))
-    return jnp.concatenate(parts, axis=0).astype(jnp.float32)
+    half, width = mine.shape
+    block = math.gcd(256, half)
+    steps = half // block
+
+    def place(step, first):
+        return jnp.clip(step - jnp.where(first, 0, steps), 0, steps - 1)
+
+    grid_spec = pltpu.PrefetchScalarGridSpec(
+        num_scalar_prefetch=1,
+        grid=(2 * steps,),
+        in_specs=[
+            pl.BlockSpec((block, width), lambda i, core_ref: (place(i, core_ref[0] == 0), 0)),
+            pl.BlockSpec((block, width), lambda i, core_ref: (place(i, core_ref[0] != 0), 0)),
+        ],
+        out_specs=[pl.BlockSpec((block, each), lambda i, core_ref: (i, 0)) for each in widths],
+    )
+    return pl.pallas_call(
+        partial(join_kernel, steps),
+        grid_spec=grid_spec,
+        out_shape=[jax.ShapeDtypeStruct((2 * half, each), jnp.float32) for each in widths],
+        compiler_params=pltpu.CompilerParams(vmem_limit_bytes=32 * 1024 * 1024),
+        cost_estimate=pl.CostEstimate(
+            flops=mine.size, bytes_accessed=12 * mine.size, transcendentals=0
+        ),
+        name="join",
+    )(core.astype(jnp.int32)[None], mine, other)
 
 
 def local(
@@ -442,7 +520,6 @@
     head_dim = query_gain.shape[0]
     local_heads = query_weight.shape[1] // head_dim
     local_groups = key_weight.shape[1] // head_dim
-    group_size = local_heads // local_groups
     length = lengths[0]
     valid_rows = (jnp.arange(seq_len, dtype=jnp.int32) < length).astype(jnp.float32)[:, None]
     own_start = tensor_rank * share_width
@@ -471,19 +548,18 @@
     token_rows = full_tokens.astype(jnp.float32)
     first_root = lax.rsqrt(jnp.mean(token_rows * token_rows, axis=1, keepdims=True) + EPSILON)
     normed = (token_rows * first_root * first_gain).astype(bf16)
-    query_raw = dot(normed, query_weight, ((1,), (0,)))
-    key_raw = dot(normed, key_weight, ((1,), (0,)))
-    value_rows = dot(normed, value_weight, ((1,), (0,))).astype(bf16)
+    heads_weight = jnp.concatenate([query_weight, key_weight, value_weight], axis=1)
+    raw = dot(normed, heads_weight, ((1,), (0,)))
     cosine, sine = rope_rows(seq_len, head_dim)
     head_gains = (query_gain[None, :], key_gain[None, :])
-    attended, query_rows, key_rows = attention(
-        lengths, query_raw, key_raw, value_rows, *head_gains, cosine, sine, group_size
-    )
+    counts = (local_heads, local_groups)
+    attended, query_rows, key_rows = attention(lengths, raw, *head_gains, cosine, sine, *counts)
 
     out_full = after(out_full, attended)
     attended = after(attended, full_cot)
     grad_full = (full_cot.astype(jnp.float32) * valid_rows).astype(bf16)
     grad_own = cotangent.astype(jnp.float32) * valid_rows
+    out_full = after(out_full, grad_full)
 
     half = seq_len // 2
     heads_in = (attended[:half], after(attended[half:], out_full))
@@ -506,6 +582,8 @@
             share_width,
         )
         mid_parts.append(small_sum(mid[:, 0], "tensor", tensor_size)[:, None])
+        if grad_parts:
+            mixed_grad = after(mixed_grad, grad_parts[-1])
         grad_parts.append(lax.psum_scatter(mixed_grad, "tensor", scatter_dimension=1, tiled=True))
     mixed_rows, product, gate_grads, up_grads, hidden_own, second_root = kept
     core = lax.rem(dp_rank, 2)
@@ -531,65 +609,55 @@
     hidden_grad_rows = lax.all_gather(hidden_grad.astype(bf16), "tensor", axis=1, tiled=True)
     down_part, hidden_grad_rows = lax.optimization_barrier((down_part, hidden_grad_rows))
     down_own = lax.psum_scatter(down_part, "tensor", scatter_dimension=1, tiled=True)
+    attended_grad = dot(hidden_grad_rows, out_weight, ((1,), (1,))).astype(bf16)
+    *raw_grads, query_gain_grad, key_gain_grad, row_sum = attention_back(
+        lengths, query_rows, key_rows, raw, attended_grad, *head_gains, cosine, sine, *counts
+    )
+    raw_grad = jnp.concatenate(raw_grads, axis=1)
+    row_sum = small_sum(row_sum[:, 0], "tensor", tensor_size)[:, None]
+    normed_grad = dot(raw_grad, heads_weight, ((1,), (1,))).astype(bf16)
+    normed_own_grad = lax.psum_scatter(normed_grad, "tensor", scatter_dimension=1, tiled=True)
+    first_gain_part = jnp.sum(
+        normed_grad.astype(jnp.float32) * (full_tokens.astype(jnp.float32) * first_root), axis=0
+    )
+    second_gain_part = lax.dynamic_update_slice_in_dim(
+        jnp.zeros((model_width,), jnp.float32), second_gain_grad, own_start, 0
+    )
+    gains = [first_gain_part, second_gain_part, query_gain_grad[0], key_gain_grad[0]]
+    gains = small_sum(jnp.concatenate(gains), "tensor", tensor_size)
+    for bit in range(dp_size.bit_length() - 1):
+        gains = gains + lax.ppermute(gains, "dp", [(i, i ^ (1 << bit)) for i in range(dp_size)])
     grad_out = pair_sum(attended, hidden_grad_rows, core, pairs)
-    attended_grad = dot(hidden_grad_rows, out_weight, ((1,), (1,))).astype(bf16)
-    query_raw_grad, key_raw_grad, value_raw_grad, query_gain_grad, key_gain_grad = attention_back(
-        lengths,
-        query_rows,
-        key_rows,
-        value_rows,
-        query_raw,
-        key_raw,
-        attended_grad,
-        *head_gains,
-        cosine,
-        sine,
-        group_size,
-    )
-    query_gain_grad, key_gain_grad = query_gain_grad[0], key_gain_grad[0]
-    normed_grad = (
-        dot(query_raw_grad, query_weight, ((1,), (1,)))
-        + dot(key_raw_grad, key_weight, ((1,), (1,)))
-        + dot(value_raw_grad, value_weight, ((1,), (1,)))
-    )
-    normed_grad = normed_grad.astype(bf16)
-    normed_own_grad = lax.psum_scatter(normed_grad, "tensor", scatter_dimension=1, tiled=True)
-    late = (
-        grad_out,
-        pair_sum(normed, query_raw_grad, core, pairs),
-        pair_sum(normed, key_raw_grad, core, pairs),
-        pair_sum(normed, value_raw_grad, core, pairs),
-    )
-    early = after(early, *late)
-    down_own = after(down_own, normed_grad, *late)
+    grad_heads = pair_sum(normed, raw_grad, core, pairs)
+    early = after(early, grad_out, grad_heads, gains, row_sum)
+    down_own = after(down_own, normed_grad, grad_out, grad_heads)
+    (grad_down,), (grad_gate,), (grad_up,) = (
+        both_halves(part, core, pairs, (part.shape[1],)) for part in early
+    )
+    gates = (early, grad_down)
+    grad_out, grad_heads = (
+        chip_sum(after(part, normed_grad), dp_rank, dp_size, gates)
+        for part in (grad_out, grad_heads)
+    )
     layer_out = (hidden_own + down_own.astype(jnp.float32)).astype(bf16)
-    normed_own_grad = after(normed_own_grad, layer_out, *early).astype(jnp.float32)
-    backwards = [group[::-1] for group in chips]
-    late = lax.psum(after(late, normed_grad, *early), "dp", axis_index_groups=backwards)
-    grad_down, grad_gate, grad_up = (both_halves(part, core, pairs) for part in early)
-    grad_out, grad_query, grad_key, grad_value = (both_halves(part, core, pairs) for part in late)
-    first_term, query_gain_grad, key_gain_grad = lax.psum(
-        (
-            jnp.sum(normed_own_grad * first_own * token_own, axis=1, keepdims=True),
-            query_gain_grad,
-            key_gain_grad,
-        ),
-        "tensor",
-    )
-    first_gain_grad = jnp.sum(normed_own_grad * token_own * first_root, axis=0)
+    normed_own_grad = after(normed_own_grad, layer_out, gains, *early).astype(jnp.float32)
     token_grad = (
         hidden_grad
         + normed_own_grad * first_own * first_root
-        - token_own * first_root**3 / model_width * first_term
+        - token_own * first_root**2 / model_width * row_sum
     ).astype(bf16)
-    gains = jnp.concatenate([first_gain_grad, second_gain_grad, query_gain_grad, key_gain_grad])
-    gains = lax.psum(gains, "dp")
-    first_gain_grad, second_gain_grad, query_gain_grad, key_gain_grad = (
-        gains[:share_width],
-        gains[share_width : 2 * share_width],
-        gains[2 * share_width : 2 * share_width + head_dim],
-        gains[2 * share_width + head_dim :],
-    )
+    grad_out, grad_heads = after(
+        (grad_out, grad_heads), grad_gate, grad_up, layer_out, token_grad
+    )
+    (grad_out,) = both_halves(grad_out, core, pairs, (model_width,))
+    query_width, key_width = query_weight.shape[1], key_weight.shape[1]
+    grad_query, grad_key, grad_value = both_halves(
+        grad_heads, core, pairs, (query_width, key_width, key_width)
+    )
+    first_gain_grad = lax.dynamic_slice_in_dim(gains, own_start, share_width, 0)
+    second_gain_grad = lax.dynamic_slice_in_dim(gains, model_width + own_start, share_width, 0)
+    query_gain_grad = gains[2 * model_width : 2 * model_width + head_dim]
+    key_gain_grad = gains[2 * model_width + head_dim :]
     return (
         layer_out,
         token_grad,

time: 716 us -> 687 us (0.959)
  other arithmetic: 70.9 us -> 26.6 us
  Pallas kernels: 94.5 us -> 122 us
  starting transfers between devices: 18.5 us -> 44.4 us
  blocking collectives: 23.4 us -> 0 us
  waiting for transfers between devices: 372 us -> 361 us
  matrix products: 93.7 us -> 84 us
    psum x1 -> x0, waiting for transfers between devices: 37.8 us -> none  [local(): lax.psum(after(late, normed_grad, *early), 'dp', axis_index_groups=backwa...]
    ppermute x0 -> x19, waiting for transfers between devices: none -> 29.9 us  [the longest x8 19 us: halving_sum(): lax.ppermute(sent, 'dp', pairs).astype(jnp.float32)]
    convert_element_type x7 -> x8, other arithmetic: 30 us -> 1.64 us  [halving_sum(): (kept + lax.ppermute(sent, 'dp', pairs).astype(jnp.float32)).astype(jnp.b...]
    pallas_call x2 -> x7, Pallas kernels: 26.8 us -> 54.7 us  [the longest x5 26.4 us: both_halves(): pl.pallas_call(partial(join_kernel, steps), grid_spec=grid_spec, out_shap...]
    psum x2 -> x0, blocking collectives: 23.4 us -> none  [the longest x1 12.4 us: local(): gains = lax.psum(gains, 'dp')]
    ppermute x0 -> x19, starting transfers between devices: none -> 18.8 us  [the longest x8 9.46 us: halving_sum(): other = lax.ppermute(value, 'dp', pairs)]
    psum x1, waiting for transfers between devices: 60.2 us -> 46.6 us  [local(): early = lax.psum(early, 'dp', axis_index_groups=chips)]
    select_n x7 -> x8, other arithmetic: 13.9 us -> 0.35 us  [halving_sum(): jnp.where(side == 0, value, other)]
  transfers between devices with their start and end apart: 35 -> 55, of which waited for: 17 -> 23; matrix products, arithmetic and copies ran while one was open for 24% -> 17% of each run, Pallas kernels for 13% -> 17%
where the time goes in v3:
time: 687 us; the launch traced here: 678 us
  waiting for transfers between devices  361 us (53%)
  Pallas kernels  122 us (18%)
  matrix products  84 us (12%)
  starting transfers between devices  44.4 us (6%)
  other arithmetic  26.6 us (4%)
  local copies, waits for them, and re-layouts  23.4 us (3%)
  between operations  17 us (2%)
    dot_general x14, matrix products, dot(): lax.dot_general(left, right, (contract, ((), ())), preferred_element_type...  84 us
    all_gather x1, waiting for transfers between devices, local(): lax.all_gather(hidden_grad.astype(bf16), 'tensor', axis=1, tiled=True)  69.4 us
    pallas_call x2, Pallas kernels, feed_forward(): pl.pallas_call(partial(feed_kernel, branch_steps, own, not earlier), grid...  67.1 us
    all_gather x1, waiting for transfers between devices, local(): full_tokens = lax.all_gather(tokens, 'tensor', axis=1, tiled=True)  62.2 us
    all_gather x1, waiting for transfers between devices, local(): lax.all_gather(after(cotangent, full_tokens), 'tensor', axis=1, tiled=True)  49.1 us
    psum x1, waiting for transfers between devices, local(): out_full = lax.psum(out_full, 'dp', axis_index_groups=rotated_order)  49 us
    psum x1, waiting for transfers between devices, local(): early = lax.psum(early, 'dp', axis_index_groups=chips)  46.6 us
    ppermute x3, waiting for transfers between devices, local(): pieces.append(lax.ppermute(out_part, 'tensor', ring))  27 us
  transfers between devices with their start and end apart: 55, of which 23 were waited for; matrix products, arithmetic and copies ran while one was open for 17% of the time, Pallas kernels for 17%

profile of v3, /device:TPU:0, one launch (start us, length us, event | category | flops | bytes accessed | tf_op | source)
XLA Modules:
  0.0 677.8 jit_solution(1073323265587600059)
XLA Ops:
  16.9 5.4 collective-permute-done
  22.3 21.7 %collective-permute-done.1 = bf16[512,256]{1,0:T(8,128)(2,1)S(1)} collective-permute-done((bf16[512,256]{1,0:T(8,128)(2,1)S(1)}, bf16[512,256]{1,0:T(8,128)(2,1)S(1)}, u32[]{:S(2)}, u32[]{:S(2)}) %collective-permute-start.1) | collective-permute-done | bytes 262176 | tf_op jit(solution)/shard_map/ppermute | solution.py:535
  43.9 62.2 %all-gather.6.cloned.1.call-done.refs_2_ = bf16[1024,2048]{1,0:T(8,128)(2,1)} async-done(((bf16[1024,512]{1,0:T(8,128)(2,1)}), bf16[1024,2048]{1,0:T(8,128)(2,1)}) %all-gather.6.cloned.1.call-update) | async-done | bytes 4194320 | tf_op jit(solution)/shard_map/all_gather | solution.py:528
  106.9 4.5 broadcast_in_dim.57
  120.5 4.5 fusion.60.query_ref.key_ref.value_ref.query_raw_ref.key_raw_ref.value_raw_ref
  125.0 11.0 %attention.1 = (bf16[1024,512]{1,0:T(8,128)(2,1)S(1)}, bf16[1024,512]{1,0:T(8,128)(2,1)S(1)}, bf16[1024,256]{1,0:T(8,128)(2,1)S(1)}) custom-call(s32[1]{0:T(128)} %copy.53.length_ref, f32[1024,1024]{1,0:T(8,128)S(1)} %fusion.60.query_ref.key_ref.value_ref.query_raw_ref.key_raw_ref.value_raw_ref, ...), custom_call_target="tpu_custom_call" | custom-call | flops 1342177280 | bytes 6291456 | tf_op jit(solution)/shard_map/attention/pallas_call | solution.py:221
  138.8 49.1 %all-gather.8.cloned.1.call-done = bf16[1024,2048]{1,0:T(8,128)(2,1)} async-done(((bf16[1024,512]{1,0:T(8,128)(2,1)}), bf16[1024,2048]{1,0:T(8,128)(2,1)}) %all-gather.8.cloned.1.call-update) | async-done | bytes 4194320 | tf_op jit(solution)/shard_map/all_gather | solution.py:537
  189.0 49.0 %all-reduce.4.cloned.1.call-done.refs_4_ = bf16[2048,2048]{1,0:T(8,128)(2,1)} async-done(((bf16[2048,2048]{1,0:T(8,128)(2,1)}), bf16[2048,2048]{1,0:T(8,128)(2,1)}) %all-reduce.4.cloned.1.call-update) | async-done | bytes 8388624 | tf_op jit(solution)/shard_map/psum | solution.py:545
  238.1 4.9 multiply_convert_fusion.refs_3_
  243.5 33.5 %feed_forward.2 = (bf16[1024,2048]{1,0:T(8,128)(2,1)}, bf16[1024,1536]{1,0:T(8,128)(2,1)}, bf16[1024,1536]{1,0:T(8,128)(2,1)}, bf16[1024,1536]{1,0:T(8,128)(2,1)...) custom-call(s32[1]{0:T(128)} %bitcast.refs_0_, ...), custom_call_target="tpu_custom_call" | custom-call | flops 20401094656 | bytes 27262976 | tf_op jit(solution)/shard_map/feed_forward/pallas_call | solution.py:378
  277.1 12.1 %all-gather.10.cloned.1.call-done.refs_1_ = bf16[512,2048]{1,0:T(8,128)(2,1)} async-done(((bf16[512,512]{1,0:T(8,128)(2,1)}), bf16[512,2048]{1,0:T(8,128)(2,1)}) %all-gather.10.cloned.1.call-update) | async-done | bytes 2097168 | tf_op jit(solution)/shard_map/all_gather | solution.py:566
  289.1 33.6 %feed_forward.3 = (bf16[1024,2048]{1,0:T(8,128)(2,1)}, bf16[1024,1536]{1,0:T(8,128)(2,1)}, bf16[1024,1536]{1,0:T(8,128)(2,1)}, bf16[1024,1536]{1,0:T(8,128)(2,1)...) custom-call(s32[1]{0:T(128)} %bitcast.refs_0_, ...), custom_call_target="tpu_custom_call", output_to_operand_aliasing={{0}: (9, {}), {1}: (10, {}), {2}: (11, {}), {3}: (12, {}), ... | custom-call | flops 20401094656 | bytes 27262976 | tf_op jit(solution)/shard_map/feed_forward/pallas_call | solution.py:378
  322.8 7.8 %convolution_convert_fusion.1 = bf16[1024,1536]{1,0:T(8,128)(2,1)} fusion(bf16[1024,1536]{1,0:T(8,128)(2,1)} %get-tuple-element.89, bf16[1024,2048]{1,0:T(8,128)(2,1)} %get-tuple-element.87, s32[]{:T(128)S(6)} %select_n.202), kind=kOutput, calls=%fused_computation.13 | convolution fusion | flops 3222798336 | bytes 8388612 | tf_op jit(solution)/shard_map/dot_general | solution.py:38
  330.6 4.9 convolution_convert_fusion.2
  336.2 7.9 %convolution_convert_fusion.4 = bf16[768,2048]{1,0:T(8,128)(2,1)} fusion(bf16[1024,2048]{1,0:T(8,128)(2,1)} %multiply_convert_fusion.refs_3_, bf16[1024,1536]{1,0:T(8,128)(2,1)} %get-tuple-element.90, s32[]{:T(128)S(6)} %select_n.200), kind=kOutput, calls=%fused_computation.16 | convolution fusion | flops 3222798336 | bytes 8912900 | tf_op jit(solution)/shard_map/dot_general | solution.py:38
  360.8 8.9 %add_convert_fusion = bf16[1024,1536]{1,0:T(8,128)(2,1)} fusion(bf16[1024,1536]{1,0:T(8,128)(2,1)} %collective-permute-done.5, bf16[1024,1536]{1,0:T(8,128)(2,1)} %get-tuple-element.89, bf16[1024,2048]{1,0:T(8,128)(2,1)} %get-tuple-element.87, s32[]{:T(128)S(6)} %select_n.201), kind=kOutput, calls=%fused_computation.8 | convolution fusion | flops 3225944064 | bytes 11534340 | tf_op jit(solution)/shard_map/dot_general | solution.py:38
  369.7 6.5 add_convert_fusion.1
  376.1 6.4 add_convert_fusion.2
  387.8 11.0 %convolution_convert_fusion = bf16[1024,2048]{1,0:T(8,128)(2,1)} fusion(bf16[1024,1536]{1,0:T(8,128)(2,1)} %get-tuple-element.90, bf16[1536,2048]{1,0:T(8,128)(2,1)} %refs_8_.3), kind=kOutput, calls=%fused_computation.12 | convolution fusion | flops 6444548096 | bytes 13631488 | tf_op jit(solution)/shard_map/dot_general | solution.py:38
  398.8 69.4 %all-gather.14.cloned.1.call-done = bf16[1024,2048]{1,0:T(8,128)(2,1)} async-done(((bf16[1024,512]{1,0:T(8,128)(2,1)}), bf16[1024,2048]{1,0:T(8,128)(2,1)}) %all-gather.14.cloned.1.call-update) | async-done | bytes 4194320 | tf_op jit(solution)/shard_map/all_gather | solution.py:609
  468.6 4.6 convolution_convert_fusion.5
  476.0 17.4 %attention_back.1 = (bf16[1024,512]{1,0:T(8,128)(2,1)S(1)}, bf16[1024,256]{1,0:T(8,128)(2,1)S(1)}, bf16[1024,256]{1,0:T(8,128)(2,1)S(1)}, f32[1,128]{1,0:T(1,128...) custom-call(s32[1]{0:T(128)} %copy.53.length_ref, bf16[1024,512]{1,0:T(8,128)(2,1)S(1)} %get-tuple-element.102.query_ref, ...), custom_call_target="tpu_custom_call" | custom-call | flops 3355443200 | bytes 10485760 | tf_op jit(solution)/shard_map/attention_back/pallas_call | solution.py:247
  496.2 6.2 fusion.3
  512.9 5.9 fusion.14
  526.3 4.6 add_convert_fusion.5
  532.3 13.4 %collective-permute-done.23 = bf16[64,2048]{1,0:T(8,128)(2,1)S(1)} collective-permute-done((bf16[64,2048]{1,0:T(8,128)(2,1)S(1)}, bf16[64,2048]{1,0:T(8,128)(2,1)S(1)}, u32[]{:S(2)}, u32[]{:S(2)}) %collective-permute-start.23) | collective-permute-done | bytes 262176 | tf_op jit(solution)/shard_map/ppermute | solution.py:431
  555.0 46.6 %all-reduce.6.cloned.1.call-done = (bf16[768,2048]{1,0:T(8,128)(2,1)}, bf16[1024,1536]{1,0:T(8,128)(2,1)}, bf16[1024,1536]{1,0:T(8,128)(2,1)}) async-done(((bf16[768,2048]{1,0:T(8,128)(2,1)}, bf16[1024,1536]{1,0:T(8,128)(2,1)}, bf16[1024,1536]{1,0:T(8,128)(2,1)}), (bf16[768,2048]{1,0:T(8,128)(2,1)}, bf16[1024,1536]{1,0:T(8,128)(2,1)}, bf16[1024,1536]{1,0:T(8,128)(2,1)})) %all-reduce.6.cloned.1.call-update) | async-done | bytes 9437200 | tf_op jit(solution)/shard_map/psum | solution.py:601
  606.0 4.6 collective-permute-done.33
  623.9 5.1 join.5
  633.3 5.5 join.7
  638.8 5.5 join.6
  663.6 6.9 %join.8 = (f32[2048,512]{1,0:T(8,128)}, f32[2048,256]{1,0:T(8,128)}, f32[2048,256]{1,0:T(8,128)}) custom-call(s32[1]{0:T(128)} %bitcast.10.core_ref, bf16[1024,1024]{1,0:T(8,128)(2,1)S(1)} %pad_maximum_fusion.mine_ref, bf16[1024,1024]{1,0:T(8,128)(2,1)} %collective-permute-done.42.other_ref), custom_call_target="tpu_custom_call" | custom-call | flops 1048576 | bytes 12582912 | tf_op jit(solution)/shard_map/join/pallas_call | solution.py:484
  (255 shorter events, 120.3 us)
Async XLA Ops:
  8.0 98.1 %all-gather.6.cloned.1.call-start = ((), (), s32[]{:S(2)}) async-start(), calls=%async_computation.4 | async-start | bytes 5242880 | tf_op jit(solution)/shard_map/all_gather | solution.py:528
  8.7 179.2 %all-gather.8.cloned.1.call-start = ((), (), s32[]{:S(2)}) async-start(), calls=%async_computation.5 | async-start | bytes 5242880 | tf_op jit(solution)/shard_map/all_gather | solution.py:537
  9.9 12.4 %collective-permute-start = (bf16[512,256]{1,0:T(8,128)(2,1)S(1)}, bf16[512,256]{1,0:T(8,128)(2,1)S(1)}, u32[]{:S(2)}, u32[]{:S(2)}) collective-permute-start(bf16[512,256]{1,0:T(8,128)(2,1)S(1)} %get-tuple-element.139), channel_id=1, source_target_pairs={{0,1},{1,2},{2,3},{3,0},{4,5},{5,6},{6,7},{7,4},{8,9},{9,10},{10,1... | collective-permute-start | bytes 786440 | tf_op jit(solution)/shard_map/ppermute | solution.py:535
  13.0 31.0 %collective-permute-start.1 = (bf16[512,256]{1,0:T(8,128)(2,1)S(1)}, bf16[512,256]{1,0:T(8,128)(2,1)S(1)}, u32[]{:S(2)}, u32[]{:S(2)}) collective-permute-start(bf16[512,256]{1,0:T(8,128)(2,1)S(1)} %get-tuple-element.139), channel_id=1, source_target_pairs={{0,2},{1,3},{2,0},{3,1},{4,6},{5,7},{6,4},{7,5},{8,10},{9,11},{10,... | collective-permute-start | bytes 786440 | tf_op jit(solution)/shard_map/ppermute | solution.py:535
  15.5 28.4 %collective-permute-start.2 = (bf16[512,256]{1,0:T(8,128)(2,1)S(1)}, bf16[512,256]{1,0:T(8,128)(2,1)S(1)}, u32[]{:S(2)}, u32[]{:S(2)}) collective-permute-start(bf16[512,256]{1,0:T(8,128)(2,1)S(1)} %get-tuple-element.139), channel_id=1, source_target_pairs={{0,3},{1,0},{2,1},{3,2},{4,7},{5,4},{6,5},{7,6},{8,11},{9,8},{10,9... | collective-permute-start | bytes 786440 | tf_op jit(solution)/shard_map/ppermute | solution.py:535
  106.1 131.9 %all-reduce.4.cloned.1.call-start = ((), (), s32[]{:S(2)}) async-start(), calls=%async_computation.6 | async-start | bytes 16777216 | tf_op jit(solution)/shard_map/psum | solution.py:545
  112.5 131.0 %all-gather.12.cloned.1.call-start = ((), (), s32[]{:S(2)}) async-start(), calls=%async_computation.8 | async-start | bytes 2621440 | tf_op jit(solution)/shard_map/all_gather | solution.py:566
  189.0 100.2 %all-gather.10.cloned.1.call-start = ((), (), s32[]{:S(2)}) async-start(), calls=%async_computation.7 | async-start | bytes 2621440 | tf_op jit(solution)/shard_map/all_gather | solution.py:566
  243.0 92.9 %reduce-scatter.5.cloned.1.call-start = ((), (), s32[]{:S(2)}) async-start(), calls=%async_computation.9 | async-start | bytes 2621440 | tf_op jit(solution)/shard_map/reduce_scatter | solution.py:587
  277.0 105.5 %reduce-scatter.7.cloned.1.call-start = ((), (), s32[]{:S(2)}) async-start(), calls=%async_computation.10 | async-start | bytes 2621440 | tf_op jit(solution)/shard_map/reduce_scatter | solution.py:587
  330.6 30.2 %collective-permute-start.5 = (bf16[1024,1536]{1,0:T(8,128)(2,1)}, bf16[1024,1536]{1,0:T(8,128)(2,1)}, u32[]{:S(2)}, u32[]{:S(2)}) collective-permute-start(bf16[1024,1536]{1,0:T(8,128)(2,1)} %convolution_convert_fusion.1), channel_id=1, source_target_pairs={{0,4},{4,0},{8,12},{12,8},{16,20},{20,16},{24,28},{28,24},{1,5},{5... | collective-permute-start | bytes 9437192 | tf_op jit(solution)/shard_map/ppermute | solution.py:420
  335.5 34.2 %collective-permute-start.4 = (bf16[1024,1536]{1,0:T(8,128)(2,1)}, bf16[1024,1536]{1,0:T(8,128)(2,1)}, u32[]{:S(2)}, u32[]{:S(2)}) collective-permute-start(bf16[1024,1536]{1,0:T(8,128)(2,1)} %convolution_convert_fusion.2), channel_id=1, source_target_pairs={{0,4},{4,0},{8,12},{12,8},{16,20},{20,16},{24,28},{28,24},{1,5},{5... | collective-permute-start | bytes 9437192 | tf_op jit(solution)/shard_map/ppermute | solution.py:420
  336.0 132.2 %all-gather.14.cloned.1.call-start = ((), (), s32[]{:S(2)}) async-start(), calls=%async_computation.11 | async-start | bytes 5242880 | tf_op jit(solution)/shard_map/all_gather | solution.py:609
  344.2 32.0 %collective-permute-start.3 = (bf16[768,2048]{1,0:T(8,128)(2,1)}, bf16[768,2048]{1,0:T(8,128)(2,1)}, u32[]{:S(2)}, u32[]{:S(2)}) collective-permute-start(bf16[768,2048]{1,0:T(8,128)(2,1)} %convolution_convert_fusion.4), channel_id=1, source_target_pairs={{0,4},{4,0},{8,12},{12,8},{16,20},{20,16},{24,28},{28,24},{1,5},{5... | collective-permute-start | bytes 9437192 | tf_op jit(solution)/shard_map/ppermute | solution.py:420
  386.7 214.9 %all-reduce.6.cloned.1.call-start = ((), (), s32[]{:S(2)}) async-start(), calls=%async_computation.14 | async-start | bytes 18874368 | tf_op jit(solution)/shard_map/psum | solution.py:601
  387.3 260.2 %reduce-scatter.9.cloned.1.call-start = ((), (), s32[]{:S(2)}) async-start(), calls=%async_computation.12 | async-start | bytes 5242880 | tf_op jit(solution)/shard_map/reduce_scatter | solution.py:611
  468.2 182.4 %reduce-scatter.11.cloned.1.call-start = ((), (), s32[]{:S(2)}) async-start(), calls=%async_computation.13 | async-start | bytes 5242880 | tf_op jit(solution)/shard_map/reduce_scatter | solution.py:619
  473.2 51.6 %collective-permute-start.12 = (bf16[256,2048]{1,0:T(8,128)(2,1)}, bf16[256,2048]{1,0:T(8,128)(2,1)}, u32[]{:S(2)}, u32[]{:S(2)}) collective-permute-start(bf16[256,2048]{1,0:T(8,128)(2,1)} %convolution_convert_fusion.5), channel_id=1, source_target_pairs={{0,4},{4,0},{8,12},{12,8},{16,20},{20,16},{24,28},{28,24},{1,5},{5... | collective-permute-start | bytes 3145736 | tf_op jit(solution)/shard_map/ppermute | solution.py:420
  511.6 13.1 %collective-permute-start.18 = (f32[4352]{0:T(1024)S(1)}, f32[4352]{0:T(1024)S(1)}, u32[]{:S(2)}, u32[]{:S(2)}) collective-permute-start(f32[4352]{0:T(1024)S(1)} %add.269), channel_id=1, source_target_pairs={{0,8},{4,12},{8,0},{12,4},{16,24},{20,28},{24,16},{28,20},{1,9},{5... | collective-permute-start | bytes 52232 | tf_op jit(solution)/shard_map/ppermute | solution.py:629
  524.7 24.4 %collective-permute-start.13 = (bf16[1024,1024]{1,0:T(8,128)(2,1)}, bf16[1024,1024]{1,0:T(8,128)(2,1)S(1)}, u32[]{:S(2)}, u32[]{:S(2)}) collective-permute-start(bf16[1024,1024]{1,0:T(8,128)(2,1)} %fusion.14), channel_id=1, source_target_pairs={{0,4},{4,0},{8,12},{12,8},{16,20},{20,16},{24,28},{28,24},{1,5},{5... | collective-permute-start | bytes 6291464 | tf_op jit(solution)/shard_map/ppermute | solution.py:420
  531.1 14.6 %collective-permute-start.23 = (bf16[64,2048]{1,0:T(8,128)(2,1)S(1)}, bf16[64,2048]{1,0:T(8,128)(2,1)S(1)}, u32[]{:S(2)}, u32[]{:S(2)}) collective-permute-start(bf16[64,2048]{1,0:T(8,128)(2,1)S(1)} %constant_dynamic-slice_fusion.7), channel_id=1, source_target_pairs={{0,8},{4,12},{8,0},{12,4},{16,24},{20,28},{24,16},{28,20},{1,9},{5... | collective-permute-start | bytes 786440 | tf_op jit(solution)/shard_map/ppermute | solution.py:431
  531.9 14.6 %collective-permute-start.28 = (bf16[64,2048]{1,0:T(8,128)(2,1)S(1)}, bf16[64,2048]{1,0:T(8,128)(2,1)S(1)}, u32[]{:S(2)}, u32[]{:S(2)}) collective-permute-start(bf16[64,2048]{1,0:T(8,128)(2,1)S(1)} %constant_dynamic-slice_fusion.5), channel_id=1, source_target_pairs={{0,16},{4,20},{8,24},{12,28},{16,0},{20,4},{24,8},{28,12},{1,17},{... | collective-permute-start | bytes 786440 | tf_op jit(solution)/shard_map/ppermute | solution.py:431
  547.2 56.8 %collective-permute-start.29 = (bf16[32,2048]{1,0:T(8,128)(2,1)}, bf16[32,2048]{1,0:T(8,128)(2,1)}, u32[]{:S(2)}, u32[]{:S(2)}) collective-permute-start(bf16[32,2048]{1,0:T(8,128)(2,1)} %constant_dynamic-slice_fusion.4), channel_id=1, source_target_pairs={{0,8},{4,12},{8,0},{12,4},{16,24},{20,28},{24,16},{28,20},{1,9},{5... | collective-permute-start | bytes 393224 | tf_op jit(solution)/shard_map/ppermute | solution.py:431
  552.6 49.0 %collective-permute-start.32 = (bf16[256,1024]{1,0:T(8,128)(2,1)}, bf16[256,1024]{1,0:T(8,128)(2,1)S(1)}, u32[]{:S(2)}, u32[]{:S(2)}) collective-permute-start(bf16[256,1024]{1,0:T(8,128)(2,1)} %constant_dynamic-slice_fusion.3), channel_id=1, source_target_pairs={{0,8},{4,12},{8,0},{12,4},{16,24},{20,28},{24,16},{28,20},{1,9},{5... | collective-permute-start | bytes 1572872 | tf_op jit(solution)/shard_map/ppermute | solution.py:431
  553.6 49.6 %collective-permute-start.36 = (bf16[256,1024]{1,0:T(8,128)(2,1)}, bf16[256,1024]{1,0:T(8,128)(2,1)S(1)}, u32[]{:S(2)}, u32[]{:S(2)}) collective-permute-start(bf16[256,1024]{1,0:T(8,128)(2,1)} %constant_dynamic-slice_fusion.1), channel_id=1, source_target_pairs={{0,16},{4,20},{8,24},{12,28},{16,0},{20,4},{24,8},{28,12},{1,17},{... | collective-permute-start | bytes 1572872 | tf_op jit(solution)/shard_map/ppermute | solution.py:431
  601.6 22.3 %collective-permute-start.26 = (bf16[768,2048]{1,0:T(8,128)(2,1)}, bf16[768,2048]{1,0:T(8,128)(2,1)S(1)}, u32[]{:S(2)}, u32[]{:S(2)}) collective-permute-start(bf16[768,2048]{1,0:T(8,128)(2,1)} %get-tuple-element.111.mine_ref), channel_id=1, source_target_pairs={{0,4},{4,0},{8,12},{12,8},{16,20},{20,16},{24,28},{28,24},{1,5},{5... | collective-permute-start | bytes 9437192 | tf_op jit(solution)/shard_map/ppermute | solution.py:467
  603.4 28.3 %collective-permute-start.41 = (bf16[1024,1536]{1,0:T(8,128)(2,1)}, bf16[1024,1536]{1,0:T(8,128)(2,1)S(1)}, u32[]{:S(2)}, u32[]{:S(2)}) collective-permute-start(bf16[1024,1536]{1,0:T(8,128)(2,1)} %get-tuple-element.113.mine_ref), channel_id=1, source_target_pairs={{0,4},{4,0},{8,12},{12,8},{16,20},{20,16},{24,28},{28,24},{1,5},{5... | collective-permute-start | bytes 9437192 | tf_op jit(solution)/shard_map/ppermute | solution.py:467
  603.7 35.1 %collective-permute-start.40 = (bf16[1024,1536]{1,0:T(8,128)(2,1)S(1)}, bf16[1024,1536]{1,0:T(8,128)(2,1)S(1)}, u32[]{:S(2)}, u32[]{:S(2)}) collective-permute-start(bf16[1024,1536]{1,0:T(8,128)(2,1)S(1)} %copy-done.2), channel_id=1, source_target_pairs={{0,4},{4,0},{8,12},{12,8},{16,20},{20,16},{24,28},{28,24},{1,5},{5... | collective-permute-start | bytes 9437192 | tf_op jit(solution)/shard_map/ppermute | solution.py:467
  629.0 15.3 %collective-permute-start.27 = (bf16[64,2048]{1,0:T(8,128)(2,1)S(1)}, bf16[64,2048]{1,0:T(8,128)(2,1)S(1)}, u32[]{:S(2)}, u32[]{:S(2)}) collective-permute-start(bf16[64,2048]{1,0:T(8,128)(2,1)S(1)} %pad_maximum_fusion.6), channel_id=1, source_target_pairs={{0,8},{4,12},{8,0},{12,4},{16,24},{20,28},{24,16},{28,20},{1,9},{5... | collective-permute-start | bytes 786440 | tf_op jit(solution)/shard_map/ppermute | solution.py:436
  629.8 17.3 %collective-permute-start.35 = (bf16[256,1024]{1,0:T(8,128)(2,1)S(1)}, bf16[256,1024]{1,0:T(8,128)(2,1)S(1)}, u32[]{:S(2)}, u32[]{:S(2)}) collective-permute-start(bf16[256,1024]{1,0:T(8,128)(2,1)S(1)} %pad_maximum_fusion.4), channel_id=1, source_target_pairs={{0,8},{4,12},{8,0},{12,4},{16,24},{20,28},{24,16},{28,20},{1,9},{5... | collective-permute-start | bytes 1572872 | tf_op jit(solution)/shard_map/ppermute | solution.py:436
  631.3 15.9 %collective-permute-start.39 = (bf16[256,1024]{1,0:T(8,128)(2,1)S(1)}, bf16[256,1024]{1,0:T(8,128)(2,1)S(1)}, u32[]{:S(2)}, u32[]{:S(2)}) collective-permute-start(bf16[256,1024]{1,0:T(8,128)(2,1)S(1)} %pad_maximum_fusion.5), channel_id=1, source_target_pairs={{0,16},{4,20},{8,24},{12,28},{16,0},{20,4},{24,8},{28,12},{1,17},{... | collective-permute-start | bytes 1572872 | tf_op jit(solution)/shard_map/ppermute | solution.py:436
  631.7 15.2 %collective-permute-start.31 = (bf16[64,2048]{1,0:T(8,128)(2,1)S(1)}, bf16[64,2048]{1,0:T(8,128)(2,1)S(1)}, u32[]{:S(2)}, u32[]{:S(2)}) collective-permute-start(bf16[64,2048]{1,0:T(8,128)(2,1)S(1)} %pad_maximum_fusion.7), channel_id=1, source_target_pairs={{0,16},{4,20},{8,24},{12,28},{16,0},{20,4},{24,8},{28,12},{1,17},{... | collective-permute-start | bytes 786440 | tf_op jit(solution)/shard_map/ppermute | solution.py:436
  (56 other events, 379.2 us)
Sparse Core Ops, SparseCore 0:
  10.4 95.6 all-gather.5
  107.7 80.2 all-gather.7
  190.1 44.4 all-gather.11
  243.2 45.9 all-gather.9
  292.0 42.6 reduce-scatter.4
  336.8 43.4 reduce-scatter.6
  386.9 81.3 all-gather.13
  471.2 76.8 reduce-scatter.8
  551.0 77.2 reduce-scatter.10
Sparse Core Ops, SparseCore 1:
  112.6 125.5 all-reduce.3
  391.6 209.9 all-reduce.5

commit v4 on v3

--- a/solution.py
+++ b/solution.py
@@ -562,7 +562,7 @@
     out_full = after(out_full, grad_full)
 
     half = seq_len // 2
-    heads_in = (attended[:half], after(attended[half:], out_full))
+    heads_in = (attended[:half], after(attended[half:], grad_full))
     heads_parts = [lax.all_gather(part, "tensor", axis=1, tiled=True) for part in heads_in]
     rank = tensor_rank.astype(jnp.int32)[None]
     grad_parts, mid_parts, kept = [], [], []
@@ -581,7 +581,7 @@
             down_weight,
             share_width,
         )
-        mid_parts.append(small_sum(mid[:, 0], "tensor", tensor_size)[:, None])
+        mid_parts.append(mid[:, 0])
         if grad_parts:
             mixed_grad = after(mixed_grad, grad_parts[-1])
         grad_parts.append(lax.psum_scatter(mixed_grad, "tensor", scatter_dimension=1, tiled=True))
@@ -595,9 +595,9 @@
         pair_sum(mixed_rows, up_grads, core, pairs),
     )
     down_part = dot(after(product, *early), down_weight, ((1,), (0,))).astype(bf16)
-    grad_parts, mid_parts = after((grad_parts, mid_parts), *early)
+    mid_total = small_sum(jnp.concatenate(mid_parts), "tensor", tensor_size)[:, None]
+    grad_parts, mid_total = after((grad_parts, mid_total), *early)
     mixed_own_grad = jnp.concatenate(grad_parts, axis=0).astype(jnp.float32)
-    mid_total = jnp.concatenate(mid_parts, axis=0)
     early = lax.psum(early, "dp", axis_index_groups=chips)
 
     second_gain_grad = jnp.sum(mixed_own_grad * hidden_own * second_root, axis=0)

time: 687 us -> 676 us (0.984)
  waiting for transfers between devices: 361 us -> 353 us
    ppermute x12 -> x9, starting transfers between devices: 15.5 us -> 11.4 us  [small_sum(): total = total + lax.ppermute(values, axis, pairs)]
  transfers between devices with their start and end apart: 55 -> 52, of which waited for: 23 -> 22; matrix products, arithmetic and copies ran while one was open for 17% -> 18% of each run, Pallas kernels for 17% -> 17%
where the time goes in v4:
time: 676 us; the launch traced here: 666 us
  waiting for transfers between devices  353 us (52%)
  Pallas kernels  122 us (18%)
  matrix products  84.1 us (12%)
  starting transfers between devices  40.3 us (6%)
  other arithmetic  26.6 us (4%)
  local copies, waits for them, and re-layouts  23.4 us (3%)
  between operations  17 us (3%)
    dot_general x14, matrix products, dot(): lax.dot_general(left, right, (contract, ((), ())), preferred_element_type...  84.1 us
    all_gather x1, waiting for transfers between devices, local(): lax.all_gather(hidden_grad.astype(bf16), 'tensor', axis=1, tiled=True)  68.2 us
    pallas_call x2, Pallas kernels, feed_forward(): pl.pallas_call(partial(feed_kernel, branch_steps, own, not earlier), grid...  67.4 us
    all_gather x1, waiting for transfers between devices, local(): full_tokens = lax.all_gather(tokens, 'tensor', axis=1, tiled=True)  62.2 us
    all_gather x1, waiting for transfers between devices, local(): lax.all_gather(after(cotangent, full_tokens), 'tensor', axis=1, tiled=True)  49.1 us
    psum x1, waiting for transfers between devices, local(): early = lax.psum(early, 'dp', axis_index_groups=chips)  46.6 us
    psum x1, waiting for transfers between devices, local(): out_full = lax.psum(out_full, 'dp', axis_index_groups=rotated_order)  43.7 us
    ppermute x3, waiting for transfers between devices, local(): pieces.append(lax.ppermute(out_part, 'tensor', ring))  27 us
  transfers between devices with their start and end apart: 52, of which 22 were waited for; matrix products, arithmetic and copies ran while one was open for 18% of the time, Pallas kernels for 17%

profile of v4, /device:TPU:0, one launch (start us, length us, event | category | flops | bytes accessed | tf_op | source)
XLA Modules:
  0.0 666.4 jit_solution(11826229925050306913)
XLA Ops:
  16.9 5.4 collective-permute-done
  22.3 21.7 %collective-permute-done.1 = bf16[512,256]{1,0:T(8,128)(2,1)S(1)} collective-permute-done((bf16[512,256]{1,0:T(8,128)(2,1)S(1)}, bf16[512,256]{1,0:T(8,128)(2,1)S(1)}, u32[]{:S(2)}, u32[]{:S(2)}) %collective-permute-start.1) | collective-permute-done | bytes 262176 | tf_op jit(solution)/shard_map/ppermute | solution.py:535
  43.9 62.2 %all-gather.6.cloned.1.call-done.refs_2_ = bf16[1024,2048]{1,0:T(8,128)(2,1)} async-done(((bf16[1024,512]{1,0:T(8,128)(2,1)}), bf16[1024,2048]{1,0:T(8,128)(2,1)}) %all-gather.6.cloned.1.call-update) | async-done | bytes 4194320 | tf_op jit(solution)/shard_map/all_gather | solution.py:528
  106.9 4.5 broadcast_in_dim.54
  120.5 4.5 fusion.60.query_ref.key_ref.value_ref.query_raw_ref.key_raw_ref.value_raw_ref
  125.0 11.0 %attention.1 = (bf16[1024,512]{1,0:T(8,128)(2,1)S(1)}, bf16[1024,512]{1,0:T(8,128)(2,1)S(1)}, bf16[1024,256]{1,0:T(8,128)(2,1)S(1)}) custom-call(s32[1]{0:T(128)} %copy.53.length_ref, f32[1024,1024]{1,0:T(8,128)S(1)} %fusion.60.query_ref.key_ref.value_ref.query_raw_ref.key_raw_ref.value_raw_ref, ...), custom_call_target="tpu_custom_call" | custom-call | flops 1342177280 | bytes 6291456 | tf_op jit(solution)/shard_map/attention/pallas_call | solution.py:221
  138.8 49.1 %all-gather.8.cloned.1.call-done = bf16[1024,2048]{1,0:T(8,128)(2,1)} async-done(((bf16[1024,512]{1,0:T(8,128)(2,1)}), bf16[1024,2048]{1,0:T(8,128)(2,1)}) %all-gather.8.cloned.1.call-update) | async-done | bytes 4194320 | tf_op jit(solution)/shard_map/all_gather | solution.py:537
  189.0 4.9 multiply_convert_fusion.refs_3_
  194.4 43.7 %all-reduce.4.cloned.1.call-done.refs_4_ = bf16[2048,2048]{1,0:T(8,128)(2,1)} async-done(((bf16[2048,2048]{1,0:T(8,128)(2,1)}), bf16[2048,2048]{1,0:T(8,128)(2,1)}) %all-reduce.4.cloned.1.call-update) | async-done | bytes 8388624 | tf_op jit(solution)/shard_map/psum | solution.py:545
  238.1 33.8 %feed_forward.2 = (bf16[1024,2048]{1,0:T(8,128)(2,1)}, bf16[1024,1536]{1,0:T(8,128)(2,1)}, bf16[1024,1536]{1,0:T(8,128)(2,1)}, bf16[1024,1536]{1,0:T(8,128)(2,1)...) custom-call(s32[1]{0:T(128)} %bitcast.refs_0_, ...), custom_call_target="tpu_custom_call" | custom-call | flops 20401094656 | bytes 27262976 | tf_op jit(solution)/shard_map/feed_forward/pallas_call | solution.py:378
  272.0 9.2 %all-gather.10.cloned.1.call-done.refs_1_ = bf16[512,2048]{1,0:T(8,128)(2,1)} async-done(((bf16[512,512]{1,0:T(8,128)(2,1)}), bf16[512,2048]{1,0:T(8,128)(2,1)}) %all-gather.10.cloned.1.call-update) | async-done | bytes 2097168 | tf_op jit(solution)/shard_map/all_gather | solution.py:566
  281.2 33.6 %feed_forward.3 = (bf16[1024,2048]{1,0:T(8,128)(2,1)}, bf16[1024,1536]{1,0:T(8,128)(2,1)}, bf16[1024,1536]{1,0:T(8,128)(2,1)}, bf16[1024,1536]{1,0:T(8,128)(2,1)...) custom-call(s32[1]{0:T(128)} %bitcast.refs_0_, ...), custom_call_target="tpu_custom_call", output_to_operand_aliasing={{0}: (9, {}), {1}: (10, {}), {2}: (11, {}), {3}: (12, {}), ... | custom-call | flops 20401094656 | bytes 27262976 | tf_op jit(solution)/shard_map/feed_forward/pallas_call | solution.py:378
  314.9 7.8 %convolution_convert_fusion.1 = bf16[1024,1536]{1,0:T(8,128)(2,1)} fusion(bf16[1024,1536]{1,0:T(8,128)(2,1)} %get-tuple-element.88, bf16[1024,2048]{1,0:T(8,128)(2,1)} %get-tuple-element.86, s32[]{:T(128)S(6)} %select_n.202), kind=kOutput, calls=%fused_computation.13 | convolution fusion | flops 3222798336 | bytes 8388612 | tf_op jit(solution)/shard_map/dot_general | solution.py:38
  322.7 4.9 convolution_convert_fusion.2
  328.3 7.9 %convolution_convert_fusion.4 = bf16[768,2048]{1,0:T(8,128)(2,1)} fusion(bf16[1024,2048]{1,0:T(8,128)(2,1)} %multiply_convert_fusion.refs_3_, bf16[1024,1536]{1,0:T(8,128)(2,1)} %get-tuple-element.89, s32[]{:T(128)S(6)} %select_n.200), kind=kOutput, calls=%fused_computation.16 | convolution fusion | flops 3222798336 | bytes 8912900 | tf_op jit(solution)/shard_map/dot_general | solution.py:38
  347.3 8.8 %add_convert_fusion = bf16[1024,1536]{1,0:T(8,128)(2,1)} fusion(bf16[1024,1536]{1,0:T(8,128)(2,1)} %collective-permute-done.5, bf16[1024,1536]{1,0:T(8,128)(2,1)} %get-tuple-element.88, bf16[1024,2048]{1,0:T(8,128)(2,1)} %get-tuple-element.86, s32[]{:T(128)S(6)} %select_n.201), kind=kOutput, calls=%fused_computation.8 | convolution fusion | flops 3225944064 | bytes 11534340 | tf_op jit(solution)/shard_map/dot_general | solution.py:38
  356.2 6.5 add_convert_fusion.1
  362.6 6.4 add_convert_fusion.2
  377.6 11.0 %convolution_convert_fusion = bf16[1024,2048]{1,0:T(8,128)(2,1)} fusion(bf16[1024,1536]{1,0:T(8,128)(2,1)} %get-tuple-element.89, bf16[1536,2048]{1,0:T(8,128)(2,1)} %refs_8_.3), kind=kOutput, calls=%fused_computation.12 | convolution fusion | flops 6444548096 | bytes 13631488 | tf_op jit(solution)/shard_map/dot_general | solution.py:38
  388.6 68.2 %all-gather.14.cloned.1.call-done = bf16[1024,2048]{1,0:T(8,128)(2,1)} async-done(((bf16[1024,512]{1,0:T(8,128)(2,1)}), bf16[1024,2048]{1,0:T(8,128)(2,1)}) %all-gather.14.cloned.1.call-update) | async-done | bytes 4194320 | tf_op jit(solution)/shard_map/all_gather | solution.py:609
  457.2 4.6 convolution_convert_fusion.5
  464.5 17.4 %attention_back.1 = (bf16[1024,512]{1,0:T(8,128)(2,1)S(1)}, bf16[1024,256]{1,0:T(8,128)(2,1)S(1)}, bf16[1024,256]{1,0:T(8,128)(2,1)S(1)}, f32[1,128]{1,0:T(1,128...) custom-call(s32[1]{0:T(128)} %copy.53.length_ref, bf16[1024,512]{1,0:T(8,128)(2,1)S(1)} %get-tuple-element.100.query_ref, ...), custom_call_target="tpu_custom_call" | custom-call | flops 3355443200 | bytes 10485760 | tf_op jit(solution)/shard_map/attention_back/pallas_call | solution.py:247
  484.8 6.2 fusion.3
  501.4 5.9 fusion.14
  514.9 4.6 add_convert_fusion.5
  520.9 13.4 %collective-permute-done.20 = bf16[64,2048]{1,0:T(8,128)(2,1)S(1)} collective-permute-done((bf16[64,2048]{1,0:T(8,128)(2,1)S(1)}, bf16[64,2048]{1,0:T(8,128)(2,1)S(1)}, u32[]{:S(2)}, u32[]{:S(2)}) %collective-permute-start.20) | collective-permute-done | bytes 262176 | tf_op jit(solution)/shard_map/ppermute | solution.py:431
  543.6 46.6 %all-reduce.6.cloned.1.call-done = (bf16[768,2048]{1,0:T(8,128)(2,1)}, bf16[1024,1536]{1,0:T(8,128)(2,1)}, bf16[1024,1536]{1,0:T(8,128)(2,1)}) async-done(((bf16[768,2048]{1,0:T(8,128)(2,1)}, bf16[1024,1536]{1,0:T(8,128)(2,1)}, bf16[1024,1536]{1,0:T(8,128)(2,1)}), (bf16[768,2048]{1,0:T(8,128)(2,1)}, bf16[1024,1536]{1,0:T(8,128)(2,1)}, bf16[1024,1536]{1,0:T(8,128)(2,1)})) %all-reduce.6.cloned.1.call-update) | async-done | bytes 9437200 | tf_op jit(solution)/shard_map/psum | solution.py:601
  594.6 4.6 collective-permute-done.30
  612.5 5.1 join.5
  621.9 5.5 join.7
  627.4 5.5 join.6
  652.2 6.9 %join.8 = (f32[2048,512]{1,0:T(8,128)}, f32[2048,256]{1,0:T(8,128)}, f32[2048,256]{1,0:T(8,128)}) custom-call(s32[1]{0:T(128)} %bitcast.9.core_ref, bf16[1024,1024]{1,0:T(8,128)(2,1)S(1)} %pad_maximum_fusion.mine_ref, bf16[1024,1024]{1,0:T(8,128)(2,1)} %collective-permute-done.39.other_ref), custom_call_target="tpu_custom_call" | custom-call | flops 1048576 | bytes 12582912 | tf_op jit(solution)/shard_map/join/pallas_call | solution.py:484
  (249 shorter events, 118.0 us)
Async XLA Ops:
  8.0 98.1 %all-gather.6.cloned.1.call-start = ((), (), s32[]{:S(2)}) async-start(), calls=%async_computation.4 | async-start | bytes 5242880 | tf_op jit(solution)/shard_map/all_gather | solution.py:528
  8.7 179.2 %all-gather.8.cloned.1.call-start = ((), (), s32[]{:S(2)}) async-start(), calls=%async_computation.5 | async-start | bytes 5242880 | tf_op jit(solution)/shard_map/all_gather | solution.py:537
  9.9 12.4 %collective-permute-start = (bf16[512,256]{1,0:T(8,128)(2,1)S(1)}, bf16[512,256]{1,0:T(8,128)(2,1)S(1)}, u32[]{:S(2)}, u32[]{:S(2)}) collective-permute-start(bf16[512,256]{1,0:T(8,128)(2,1)S(1)} %get-tuple-element.137), channel_id=1, source_target_pairs={{0,1},{1,2},{2,3},{3,0},{4,5},{5,6},{6,7},{7,4},{8,9},{9,10},{10,1... | collective-permute-start | bytes 786440 | tf_op jit(solution)/shard_map/ppermute | solution.py:535
  13.0 31.0 %collective-permute-start.1 = (bf16[512,256]{1,0:T(8,128)(2,1)S(1)}, bf16[512,256]{1,0:T(8,128)(2,1)S(1)}, u32[]{:S(2)}, u32[]{:S(2)}) collective-permute-start(bf16[512,256]{1,0:T(8,128)(2,1)S(1)} %get-tuple-element.137), channel_id=1, source_target_pairs={{0,2},{1,3},{2,0},{3,1},{4,6},{5,7},{6,4},{7,5},{8,10},{9,11},{10,... | collective-permute-start | bytes 786440 | tf_op jit(solution)/shard_map/ppermute | solution.py:535
  15.5 28.4 %collective-permute-start.2 = (bf16[512,256]{1,0:T(8,128)(2,1)S(1)}, bf16[512,256]{1,0:T(8,128)(2,1)S(1)}, u32[]{:S(2)}, u32[]{:S(2)}) collective-permute-start(bf16[512,256]{1,0:T(8,128)(2,1)S(1)} %get-tuple-element.137), channel_id=1, source_target_pairs={{0,3},{1,0},{2,1},{3,2},{4,7},{5,4},{6,5},{7,6},{8,11},{9,8},{10,9... | collective-permute-start | bytes 786440 | tf_op jit(solution)/shard_map/ppermute | solution.py:535
  106.1 131.9 %all-reduce.4.cloned.1.call-start = ((), (), s32[]{:S(2)}) async-start(), calls=%async_computation.7 | async-start | bytes 16777216 | tf_op jit(solution)/shard_map/psum | solution.py:545
  112.5 125.6 %all-gather.12.cloned.1.call-start = ((), (), s32[]{:S(2)}) async-start(), calls=%async_computation.8 | async-start | bytes 2621440 | tf_op jit(solution)/shard_map/all_gather | solution.py:566
  189.0 92.3 %all-gather.10.cloned.1.call-start = ((), (), s32[]{:S(2)}) async-start(), calls=%async_computation.6 | async-start | bytes 2621440 | tf_op jit(solution)/shard_map/all_gather | solution.py:566
  194.0 134.1 %reduce-scatter.5.cloned.1.call-start = ((), (), s32[]{:S(2)}) async-start(), calls=%async_computation.9 | async-start | bytes 2621440 | tf_op jit(solution)/shard_map/reduce_scatter | solution.py:587
  271.9 100.4 %reduce-scatter.7.cloned.1.call-start = ((), (), s32[]{:S(2)}) async-start(), calls=%async_computation.10 | async-start | bytes 2621440 | tf_op jit(solution)/shard_map/reduce_scatter | solution.py:587
  322.7 24.6 %collective-permute-start.5 = (bf16[1024,1536]{1,0:T(8,128)(2,1)}, bf16[1024,1536]{1,0:T(8,128)(2,1)}, u32[]{:S(2)}, u32[]{:S(2)}) collective-permute-start(bf16[1024,1536]{1,0:T(8,128)(2,1)} %convolution_convert_fusion.1), channel_id=1, source_target_pairs={{0,4},{4,0},{8,12},{12,8},{16,20},{20,16},{24,28},{28,24},{1,5},{5... | collective-permute-start | bytes 9437192 | tf_op jit(solution)/shard_map/ppermute | solution.py:420
  327.6 28.6 %collective-permute-start.4 = (bf16[1024,1536]{1,0:T(8,128)(2,1)}, bf16[1024,1536]{1,0:T(8,128)(2,1)}, u32[]{:S(2)}, u32[]{:S(2)}) collective-permute-start(bf16[1024,1536]{1,0:T(8,128)(2,1)} %convolution_convert_fusion.2), channel_id=1, source_target_pairs={{0,4},{4,0},{8,12},{12,8},{16,20},{20,16},{24,28},{28,24},{1,5},{5... | collective-permute-start | bytes 9437192 | tf_op jit(solution)/shard_map/ppermute | solution.py:420
  328.1 128.7 %all-gather.14.cloned.1.call-start = ((), (), s32[]{:S(2)}) async-start(), calls=%async_computation.11 | async-start | bytes 5242880 | tf_op jit(solution)/shard_map/all_gather | solution.py:609
  336.3 26.3 %collective-permute-start.3 = (bf16[768,2048]{1,0:T(8,128)(2,1)}, bf16[768,2048]{1,0:T(8,128)(2,1)}, u32[]{:S(2)}, u32[]{:S(2)}) collective-permute-start(bf16[768,2048]{1,0:T(8,128)(2,1)} %convolution_convert_fusion.4), channel_id=1, source_target_pairs={{0,4},{4,0},{8,12},{12,8},{16,20},{20,16},{24,28},{28,24},{1,5},{5... | collective-permute-start | bytes 9437192 | tf_op jit(solution)/shard_map/ppermute | solution.py:420
  376.5 213.6 %all-reduce.6.cloned.1.call-start = ((), (), s32[]{:S(2)}) async-start(), calls=%async_computation.14 | async-start | bytes 18874368 | tf_op jit(solution)/shard_map/psum | solution.py:601
  377.1 258.9 %reduce-scatter.9.cloned.1.call-start = ((), (), s32[]{:S(2)}) async-start(), calls=%async_computation.12 | async-start | bytes 5242880 | tf_op jit(solution)/shard_map/reduce_scatter | solution.py:611
  456.8 182.4 %reduce-scatter.11.cloned.1.call-start = ((), (), s32[]{:S(2)}) async-start(), calls=%async_computation.13 | async-start | bytes 5242880 | tf_op jit(solution)/shard_map/reduce_scatter | solution.py:619
  461.8 51.6 %collective-permute-start.9 = (bf16[256,2048]{1,0:T(8,128)(2,1)}, bf16[256,2048]{1,0:T(8,128)(2,1)}, u32[]{:S(2)}, u32[]{:S(2)}) collective-permute-start(bf16[256,2048]{1,0:T(8,128)(2,1)} %convolution_convert_fusion.5), channel_id=1, source_target_pairs={{0,4},{4,0},{8,12},{12,8},{16,20},{20,16},{24,28},{28,24},{1,5},{5... | collective-permute-start | bytes 3145736 | tf_op jit(solution)/shard_map/ppermute | solution.py:420
  500.1 13.1 %collective-permute-start.15 = (f32[4352]{0:T(1024)S(1)}, f32[4352]{0:T(1024)S(1)}, u32[]{:S(2)}, u32[]{:S(2)}) collective-permute-start(f32[4352]{0:T(1024)S(1)} %add.257), channel_id=1, source_target_pairs={{0,8},{4,12},{8,0},{12,4},{16,24},{20,28},{24,16},{28,20},{1,9},{5... | collective-permute-start | bytes 52232 | tf_op jit(solution)/shard_map/ppermute | solution.py:629
  513.3 24.4 %collective-permute-start.10 = (bf16[1024,1024]{1,0:T(8,128)(2,1)}, bf16[1024,1024]{1,0:T(8,128)(2,1)S(1)}, u32[]{:S(2)}, u32[]{:S(2)}) collective-permute-start(bf16[1024,1024]{1,0:T(8,128)(2,1)} %fusion.14), channel_id=1, source_target_pairs={{0,4},{4,0},{8,12},{12,8},{16,20},{20,16},{24,28},{28,24},{1,5},{5... | collective-permute-start | bytes 6291464 | tf_op jit(solution)/shard_map/ppermute | solution.py:420
  519.7 14.6 %collective-permute-start.20 = (bf16[64,2048]{1,0:T(8,128)(2,1)S(1)}, bf16[64,2048]{1,0:T(8,128)(2,1)S(1)}, u32[]{:S(2)}, u32[]{:S(2)}) collective-permute-start(bf16[64,2048]{1,0:T(8,128)(2,1)S(1)} %constant_dynamic-slice_fusion.7), channel_id=1, source_target_pairs={{0,8},{4,12},{8,0},{12,4},{16,24},{20,28},{24,16},{28,20},{1,9},{5... | collective-permute-start | bytes 786440 | tf_op jit(solution)/shard_map/ppermute | solution.py:431
  520.4 14.6 %collective-permute-start.25 = (bf16[64,2048]{1,0:T(8,128)(2,1)S(1)}, bf16[64,2048]{1,0:T(8,128)(2,1)S(1)}, u32[]{:S(2)}, u32[]{:S(2)}) collective-permute-start(bf16[64,2048]{1,0:T(8,128)(2,1)S(1)} %constant_dynamic-slice_fusion.5), channel_id=1, source_target_pairs={{0,16},{4,20},{8,24},{12,28},{16,0},{20,4},{24,8},{28,12},{1,17},{... | collective-permute-start | bytes 786440 | tf_op jit(solution)/shard_map/ppermute | solution.py:431
  535.7 56.9 %collective-permute-start.26 = (bf16[32,2048]{1,0:T(8,128)(2,1)}, bf16[32,2048]{1,0:T(8,128)(2,1)}, u32[]{:S(2)}, u32[]{:S(2)}) collective-permute-start(bf16[32,2048]{1,0:T(8,128)(2,1)} %constant_dynamic-slice_fusion.4), channel_id=1, source_target_pairs={{0,8},{4,12},{8,0},{12,4},{16,24},{20,28},{24,16},{28,20},{1,9},{5... | collective-permute-start | bytes 393224 | tf_op jit(solution)/shard_map/ppermute | solution.py:431
  541.2 49.0 %collective-permute-start.29 = (bf16[256,1024]{1,0:T(8,128)(2,1)}, bf16[256,1024]{1,0:T(8,128)(2,1)S(1)}, u32[]{:S(2)}, u32[]{:S(2)}) collective-permute-start(bf16[256,1024]{1,0:T(8,128)(2,1)} %constant_dynamic-slice_fusion.3), channel_id=1, source_target_pairs={{0,8},{4,12},{8,0},{12,4},{16,24},{20,28},{24,16},{28,20},{1,9},{5... | collective-permute-start | bytes 1572872 | tf_op jit(solution)/shard_map/ppermute | solution.py:431
  542.1 49.6 %collective-permute-start.33 = (bf16[256,1024]{1,0:T(8,128)(2,1)}, bf16[256,1024]{1,0:T(8,128)(2,1)S(1)}, u32[]{:S(2)}, u32[]{:S(2)}) collective-permute-start(bf16[256,1024]{1,0:T(8,128)(2,1)} %constant_dynamic-slice_fusion.1), channel_id=1, source_target_pairs={{0,16},{4,20},{8,24},{12,28},{16,0},{20,4},{24,8},{28,12},{1,17},{... | collective-permute-start | bytes 1572872 | tf_op jit(solution)/shard_map/ppermute | solution.py:431
  590.2 22.3 %collective-permute-start.23 = (bf16[768,2048]{1,0:T(8,128)(2,1)}, bf16[768,2048]{1,0:T(8,128)(2,1)S(1)}, u32[]{:S(2)}, u32[]{:S(2)}) collective-permute-start(bf16[768,2048]{1,0:T(8,128)(2,1)} %get-tuple-element.109.mine_ref), channel_id=1, source_target_pairs={{0,4},{4,0},{8,12},{12,8},{16,20},{20,16},{24,28},{28,24},{1,5},{5... | collective-permute-start | bytes 9437192 | tf_op jit(solution)/shard_map/ppermute | solution.py:467
  592.0 28.3 %collective-permute-start.38 = (bf16[1024,1536]{1,0:T(8,128)(2,1)}, bf16[1024,1536]{1,0:T(8,128)(2,1)S(1)}, u32[]{:S(2)}, u32[]{:S(2)}) collective-permute-start(bf16[1024,1536]{1,0:T(8,128)(2,1)} %get-tuple-element.111.mine_ref), channel_id=1, source_target_pairs={{0,4},{4,0},{8,12},{12,8},{16,20},{20,16},{24,28},{28,24},{1,5},{5... | collective-permute-start | bytes 9437192 | tf_op jit(solution)/shard_map/ppermute | solution.py:467
  592.3 35.1 %collective-permute-start.37 = (bf16[1024,1536]{1,0:T(8,128)(2,1)S(1)}, bf16[1024,1536]{1,0:T(8,128)(2,1)S(1)}, u32[]{:S(2)}, u32[]{:S(2)}) collective-permute-start(bf16[1024,1536]{1,0:T(8,128)(2,1)S(1)} %copy-done.2), channel_id=1, source_target_pairs={{0,4},{4,0},{8,12},{12,8},{16,20},{20,16},{24,28},{28,24},{1,5},{5... | collective-permute-start | bytes 9437192 | tf_op jit(solution)/shard_map/ppermute | solution.py:467
  617.6 15.3 %collective-permute-start.24 = (bf16[64,2048]{1,0:T(8,128)(2,1)S(1)}, bf16[64,2048]{1,0:T(8,128)(2,1)S(1)}, u32[]{:S(2)}, u32[]{:S(2)}) collective-permute-start(bf16[64,2048]{1,0:T(8,128)(2,1)S(1)} %pad_maximum_fusion.6), channel_id=1, source_target_pairs={{0,8},{4,12},{8,0},{12,4},{16,24},{20,28},{24,16},{28,20},{1,9},{5... | collective-permute-start | bytes 786440 | tf_op jit(solution)/shard_map/ppermute | solution.py:436
  618.3 17.3 %collective-permute-start.32 = (bf16[256,1024]{1,0:T(8,128)(2,1)S(1)}, bf16[256,1024]{1,0:T(8,128)(2,1)S(1)}, u32[]{:S(2)}, u32[]{:S(2)}) collective-permute-start(bf16[256,1024]{1,0:T(8,128)(2,1)S(1)} %pad_maximum_fusion.4), channel_id=1, source_target_pairs={{0,8},{4,12},{8,0},{12,4},{16,24},{20,28},{24,16},{28,20},{1,9},{5... | collective-permute-start | bytes 1572872 | tf_op jit(solution)/shard_map/ppermute | solution.py:436
  619.8 15.9 %collective-permute-start.36 = (bf16[256,1024]{1,0:T(8,128)(2,1)S(1)}, bf16[256,1024]{1,0:T(8,128)(2,1)S(1)}, u32[]{:S(2)}, u32[]{:S(2)}) collective-permute-start(bf16[256,1024]{1,0:T(8,128)(2,1)S(1)} %pad_maximum_fusion.5), channel_id=1, source_target_pairs={{0,16},{4,20},{8,24},{12,28},{16,0},{20,4},{24,8},{28,12},{1,17},{... | collective-permute-start | bytes 1572872 | tf_op jit(solution)/shard_map/ppermute | solution.py:436
  620.3 15.2 %collective-permute-start.28 = (bf16[64,2048]{1,0:T(8,128)(2,1)S(1)}, bf16[64,2048]{1,0:T(8,128)(2,1)S(1)}, u32[]{:S(2)}, u32[]{:S(2)}) collective-permute-start(bf16[64,2048]{1,0:T(8,128)(2,1)S(1)} %pad_maximum_fusion.7), channel_id=1, source_target_pairs={{0,16},{4,20},{8,24},{12,28},{16,0},{20,4},{24,8},{28,12},{1,17},{... | collective-permute-start | bytes 786440 | tf_op jit(solution)/shard_map/ppermute | solution.py:436
  (53 other events, 362.0 us)
Sparse Core Ops, SparseCore 0:
  10.4 95.6 all-gather.5
  107.7 80.2 all-gather.7
  190.1 44.4 all-gather.11
  236.5 44.6 all-gather.9
  284.0 42.6 reduce-scatter.4
  328.8 43.4 reduce-scatter.6
  376.7 80.0 all-gather.13
  459.8 76.8 reduce-scatter.8
  539.5 77.2 reduce-scatter.10
Sparse Core Ops, SparseCore 1:
  112.6 125.5 all-reduce.3
  381.4 208.7 all-reduce.5

commit v5 on v4

--- a/solution.py
+++ b/solution.py
@@ -228,7 +228,7 @@
             wide,
             jax.ShapeDtypeStruct((seq_len, groups * head_dim), jnp.bfloat16),
         ],
-        compiler_params=pltpu.CompilerParams(vmem_limit_bytes=40 * 1024 * 1024),
+        compiler_params=pltpu.CompilerParams(vmem_limit_bytes=24 * 1024 * 1024),
         cost_estimate=pl.CostEstimate(
             flops=4 * pairs * head_dim, bytes_accessed=6 * raw.size, transcendentals=pairs
         ),
@@ -265,7 +265,7 @@
             jax.ShapeDtypeStruct((seq_len, 1), jnp.float32),
         ],
         scratch_shapes=[rows, rows, rows],
-        compiler_params=pltpu.CompilerParams(vmem_limit_bytes=40 * 1024 * 1024),
+        compiler_params=pltpu.CompilerParams(vmem_limit_bytes=24 * 1024 * 1024),
         cost_estimate=pl.CostEstimate(
             flops=10 * pairs * head_dim, bytes_accessed=10 * raw.size, transcendentals=pairs
         ),

time: 676 us -> 676 us (level)
  no operation moved by 1% of the time
where the time goes in v5:
time: 676 us; the launch traced here: 666 us
  waiting for transfers between devices  353 us (52%)
  Pallas kernels  122 us (18%)
  matrix products  84.1 us (12%)
  starting transfers between devices  40.3 us (6%)
  other arithmetic  26.6 us (4%)
  local copies, waits for them, and re-layouts  23.4 us (3%)
  between operations  17 us (3%)
    dot_general x14, matrix products, dot(): lax.dot_general(left, right, (contract, ((), ())), preferred_element_type...  84.1 us
    all_gather x1, waiting for transfers between devices, local(): lax.all_gather(hidden_grad.astype(bf16), 'tensor', axis=1, tiled=True)  68.2 us
    pallas_call x2, Pallas kernels, feed_forward(): pl.pallas_call(partial(feed_kernel, branch_steps, own, not earlier), grid...  67.4 us
    all_gather x1, waiting for transfers between devices, local(): full_tokens = lax.all_gather(tokens, 'tensor', axis=1, tiled=True)  62.2 us
    all_gather x1, waiting for transfers between devices, local(): lax.all_gather(after(cotangent, full_tokens), 'tensor', axis=1, tiled=True)  49.1 us
    psum x1, waiting for transfers between devices, local(): early = lax.psum(early, 'dp', axis_index_groups=chips)  46.6 us
    psum x1, waiting for transfers between devices, local(): out_full = lax.psum(out_full, 'dp', axis_index_groups=rotated_order)  43.7 us
    ppermute x3, waiting for transfers between devices, local(): pieces.append(lax.ppermute(out_part, 'tensor', ring))  27 us
  transfers between devices with their start and end apart: 52, of which 22 were waited for; matrix products, arithmetic and copies ran while one was open for 18% of the time, Pallas kernels for 17%

profile of v5, /device:TPU:0, one launch (start us, length us, event | category | flops | bytes accessed | tf_op | source)
XLA Modules:
  0.0 666.3 jit_solution(18288262495030396590)
XLA Ops:
  16.9 5.4 collective-permute-done
  22.3 21.7 %collective-permute-done.1 = bf16[512,256]{1,0:T(8,128)(2,1)S(1)} collective-permute-done((bf16[512,256]{1,0:T(8,128)(2,1)S(1)}, bf16[512,256]{1,0:T(8,128)(2,1)S(1)}, u32[]{:S(2)}, u32[]{:S(2)}) %collective-permute-start.1) | collective-permute-done | bytes 262176 | tf_op jit(solution)/shard_map/ppermute | solution.py:535
  43.9 62.2 %all-gather.6.cloned.1.call-done.refs_2_ = bf16[1024,2048]{1,0:T(8,128)(2,1)} async-done(((bf16[1024,512]{1,0:T(8,128)(2,1)}), bf16[1024,2048]{1,0:T(8,128)(2,1)}) %all-gather.6.cloned.1.call-update) | async-done | bytes 4194320 | tf_op jit(solution)/shard_map/all_gather | solution.py:528
  106.9 4.5 broadcast_in_dim.54
  120.5 4.5 fusion.60.query_ref.key_ref.value_ref.query_raw_ref.key_raw_ref.value_raw_ref
  125.0 11.0 %attention.1 = (bf16[1024,512]{1,0:T(8,128)(2,1)S(1)}, bf16[1024,512]{1,0:T(8,128)(2,1)S(1)}, bf16[1024,256]{1,0:T(8,128)(2,1)S(1)}) custom-call(s32[1]{0:T(128)} %copy.53.length_ref, f32[1024,1024]{1,0:T(8,128)S(1)} %fusion.60.query_ref.key_ref.value_ref.query_raw_ref.key_raw_ref.value_raw_ref, ...), custom_call_target="tpu_custom_call" | custom-call | flops 1342177280 | bytes 6291456 | tf_op jit(solution)/shard_map/attention/pallas_call | solution.py:221
  138.8 49.1 %all-gather.8.cloned.1.call-done = bf16[1024,2048]{1,0:T(8,128)(2,1)} async-done(((bf16[1024,512]{1,0:T(8,128)(2,1)}), bf16[1024,2048]{1,0:T(8,128)(2,1)}) %all-gather.8.cloned.1.call-update) | async-done | bytes 4194320 | tf_op jit(solution)/shard_map/all_gather | solution.py:537
  189.0 4.9 multiply_convert_fusion.refs_3_
  194.4 43.7 %all-reduce.4.cloned.1.call-done.refs_4_ = bf16[2048,2048]{1,0:T(8,128)(2,1)} async-done(((bf16[2048,2048]{1,0:T(8,128)(2,1)}), bf16[2048,2048]{1,0:T(8,128)(2,1)}) %all-reduce.4.cloned.1.call-update) | async-done | bytes 8388624 | tf_op jit(solution)/shard_map/psum | solution.py:545
  238.1 33.8 %feed_forward.2 = (bf16[1024,2048]{1,0:T(8,128)(2,1)}, bf16[1024,1536]{1,0:T(8,128)(2,1)}, bf16[1024,1536]{1,0:T(8,128)(2,1)}, bf16[1024,1536]{1,0:T(8,128)(2,1)...) custom-call(s32[1]{0:T(128)} %bitcast.refs_0_, ...), custom_call_target="tpu_custom_call" | custom-call | flops 20401094656 | bytes 27262976 | tf_op jit(solution)/shard_map/feed_forward/pallas_call | solution.py:378
  272.0 9.3 %all-gather.10.cloned.1.call-done.refs_1_ = bf16[512,2048]{1,0:T(8,128)(2,1)} async-done(((bf16[512,512]{1,0:T(8,128)(2,1)}), bf16[512,2048]{1,0:T(8,128)(2,1)}) %all-gather.10.cloned.1.call-update) | async-done | bytes 2097168 | tf_op jit(solution)/shard_map/all_gather | solution.py:566
  281.3 33.6 %feed_forward.3 = (bf16[1024,2048]{1,0:T(8,128)(2,1)}, bf16[1024,1536]{1,0:T(8,128)(2,1)}, bf16[1024,1536]{1,0:T(8,128)(2,1)}, bf16[1024,1536]{1,0:T(8,128)(2,1)...) custom-call(s32[1]{0:T(128)} %bitcast.refs_0_, ...), custom_call_target="tpu_custom_call", output_to_operand_aliasing={{0}: (9, {}), {1}: (10, {}), {2}: (11, {}), {3}: (12, {}), ... | custom-call | flops 20401094656 | bytes 27262976 | tf_op jit(solution)/shard_map/feed_forward/pallas_call | solution.py:378
  314.9 7.8 %convolution_convert_fusion.1 = bf16[1024,1536]{1,0:T(8,128)(2,1)} fusion(bf16[1024,1536]{1,0:T(8,128)(2,1)} %get-tuple-element.88, bf16[1024,2048]{1,0:T(8,128)(2,1)} %get-tuple-element.86, s32[]{:T(128)S(6)} %select_n.202), kind=kOutput, calls=%fused_computation.13 | convolution fusion | flops 3222798336 | bytes 8388612 | tf_op jit(solution)/shard_map/dot_general | solution.py:38
  322.7 4.9 convolution_convert_fusion.2
  328.3 7.9 %convolution_convert_fusion.4 = bf16[768,2048]{1,0:T(8,128)(2,1)} fusion(bf16[1024,2048]{1,0:T(8,128)(2,1)} %multiply_convert_fusion.refs_3_, bf16[1024,1536]{1,0:T(8,128)(2,1)} %get-tuple-element.89, s32[]{:T(128)S(6)} %select_n.200), kind=kOutput, calls=%fused_computation.16 | convolution fusion | flops 3222798336 | bytes 8912900 | tf_op jit(solution)/shard_map/dot_general | solution.py:38
  347.5 8.8 %add_convert_fusion = bf16[1024,1536]{1,0:T(8,128)(2,1)} fusion(bf16[1024,1536]{1,0:T(8,128)(2,1)} %collective-permute-done.5, bf16[1024,1536]{1,0:T(8,128)(2,1)} %get-tuple-element.88, bf16[1024,2048]{1,0:T(8,128)(2,1)} %get-tuple-element.86, s32[]{:T(128)S(6)} %select_n.201), kind=kOutput, calls=%fused_computation.8 | convolution fusion | flops 3225944064 | bytes 11534340 | tf_op jit(solution)/shard_map/dot_general | solution.py:38
  356.3 6.5 add_convert_fusion.1
  362.8 6.4 add_convert_fusion.2
  377.5 11.0 %convolution_convert_fusion = bf16[1024,2048]{1,0:T(8,128)(2,1)} fusion(bf16[1024,1536]{1,0:T(8,128)(2,1)} %get-tuple-element.89, bf16[1536,2048]{1,0:T(8,128)(2,1)} %refs_8_.3), kind=kOutput, calls=%fused_computation.12 | convolution fusion | flops 6444548096 | bytes 13631488 | tf_op jit(solution)/shard_map/dot_general | solution.py:38
  388.5 68.2 %all-gather.14.cloned.1.call-done = bf16[1024,2048]{1,0:T(8,128)(2,1)} async-done(((bf16[1024,512]{1,0:T(8,128)(2,1)}), bf16[1024,2048]{1,0:T(8,128)(2,1)}) %all-gather.14.cloned.1.call-update) | async-done | bytes 4194320 | tf_op jit(solution)/shard_map/all_gather | solution.py:609
  457.1 4.6 convolution_convert_fusion.5
  464.5 17.4 %attention_back.1 = (bf16[1024,512]{1,0:T(8,128)(2,1)S(1)}, bf16[1024,256]{1,0:T(8,128)(2,1)S(1)}, bf16[1024,256]{1,0:T(8,128)(2,1)S(1)}, f32[1,128]{1,0:T(1,128...) custom-call(s32[1]{0:T(128)} %copy.53.length_ref, bf16[1024,512]{1,0:T(8,128)(2,1)S(1)} %get-tuple-element.100.query_ref, ...), custom_call_target="tpu_custom_call" | custom-call | flops 3355443200 | bytes 10485760 | tf_op jit(solution)/shard_map/attention_back/pallas_call | solution.py:247
  484.7 6.2 fusion.3
  501.4 5.9 fusion.14
  514.8 4.6 add_convert_fusion.5
  520.8 13.4 %collective-permute-done.20 = bf16[64,2048]{1,0:T(8,128)(2,1)S(1)} collective-permute-done((bf16[64,2048]{1,0:T(8,128)(2,1)S(1)}, bf16[64,2048]{1,0:T(8,128)(2,1)S(1)}, u32[]{:S(2)}, u32[]{:S(2)}) %collective-permute-start.20) | collective-permute-done | bytes 262176 | tf_op jit(solution)/shard_map/ppermute | solution.py:431
  543.5 46.6 %all-reduce.6.cloned.1.call-done = (bf16[768,2048]{1,0:T(8,128)(2,1)}, bf16[1024,1536]{1,0:T(8,128)(2,1)}, bf16[1024,1536]{1,0:T(8,128)(2,1)}) async-done(((bf16[768,2048]{1,0:T(8,128)(2,1)}, bf16[1024,1536]{1,0:T(8,128)(2,1)}, bf16[1024,1536]{1,0:T(8,128)(2,1)}), (bf16[768,2048]{1,0:T(8,128)(2,1)}, bf16[1024,1536]{1,0:T(8,128)(2,1)}, bf16[1024,1536]{1,0:T(8,128)(2,1)})) %all-reduce.6.cloned.1.call-update) | async-done | bytes 9437200 | tf_op jit(solution)/shard_map/psum | solution.py:601
  594.5 4.6 collective-permute-done.30
  612.4 5.1 join.5
  621.8 5.5 join.7
  627.3 5.5 join.6
  652.1 6.9 %join.8 = (f32[2048,512]{1,0:T(8,128)}, f32[2048,256]{1,0:T(8,128)}, f32[2048,256]{1,0:T(8,128)}) custom-call(s32[1]{0:T(128)} %bitcast.9.core_ref, bf16[1024,1024]{1,0:T(8,128)(2,1)S(1)} %pad_maximum_fusion.mine_ref, bf16[1024,1024]{1,0:T(8,128)(2,1)} %collective-permute-done.39.other_ref), custom_call_target="tpu_custom_call" | custom-call | flops 1048576 | bytes 12582912 | tf_op jit(solution)/shard_map/join/pallas_call | solution.py:484
  (249 shorter events, 117.9 us)
Async XLA Ops:
  8.0 98.1 %all-gather.6.cloned.1.call-start = ((), (), s32[]{:S(2)}) async-start(), calls=%async_computation.4 | async-start | bytes 5242880 | tf_op jit(solution)/shard_map/all_gather | solution.py:528
  8.7 179.2 %all-gather.8.cloned.1.call-start = ((), (), s32[]{:S(2)}) async-start(), calls=%async_computation.5 | async-start | bytes 5242880 | tf_op jit(solution)/shard_map/all_gather | solution.py:537
  9.9 12.4 %collective-permute-start = (bf16[512,256]{1,0:T(8,128)(2,1)S(1)}, bf16[512,256]{1,0:T(8,128)(2,1)S(1)}, u32[]{:S(2)}, u32[]{:S(2)}) collective-permute-start(bf16[512,256]{1,0:T(8,128)(2,1)S(1)} %get-tuple-element.137), channel_id=1, source_target_pairs={{0,1},{1,2},{2,3},{3,0},{4,5},{5,6},{6,7},{7,4},{8,9},{9,10},{10,1... | collective-permute-start | bytes 786440 | tf_op jit(solution)/shard_map/ppermute | solution.py:535
  13.0 31.0 %collective-permute-start.1 = (bf16[512,256]{1,0:T(8,128)(2,1)S(1)}, bf16[512,256]{1,0:T(8,128)(2,1)S(1)}, u32[]{:S(2)}, u32[]{:S(2)}) collective-permute-start(bf16[512,256]{1,0:T(8,128)(2,1)S(1)} %get-tuple-element.137), channel_id=1, source_target_pairs={{0,2},{1,3},{2,0},{3,1},{4,6},{5,7},{6,4},{7,5},{8,10},{9,11},{10,... | collective-permute-start | bytes 786440 | tf_op jit(solution)/shard_map/ppermute | solution.py:535
  15.5 28.4 %collective-permute-start.2 = (bf16[512,256]{1,0:T(8,128)(2,1)S(1)}, bf16[512,256]{1,0:T(8,128)(2,1)S(1)}, u32[]{:S(2)}, u32[]{:S(2)}) collective-permute-start(bf16[512,256]{1,0:T(8,128)(2,1)S(1)} %get-tuple-element.137), channel_id=1, source_target_pairs={{0,3},{1,0},{2,1},{3,2},{4,7},{5,4},{6,5},{7,6},{8,11},{9,8},{10,9... | collective-permute-start | bytes 786440 | tf_op jit(solution)/shard_map/ppermute | solution.py:535
  106.1 131.9 %all-reduce.4.cloned.1.call-start = ((), (), s32[]{:S(2)}) async-start(), calls=%async_computation.7 | async-start | bytes 16777216 | tf_op jit(solution)/shard_map/psum | solution.py:545
  112.5 125.6 %all-gather.12.cloned.1.call-start = ((), (), s32[]{:S(2)}) async-start(), calls=%async_computation.8 | async-start | bytes 2621440 | tf_op jit(solution)/shard_map/all_gather | solution.py:566
  189.0 92.3 %all-gather.10.cloned.1.call-start = ((), (), s32[]{:S(2)}) async-start(), calls=%async_computation.6 | async-start | bytes 2621440 | tf_op jit(solution)/shard_map/all_gather | solution.py:566
  194.0 134.0 %reduce-scatter.5.cloned.1.call-start = ((), (), s32[]{:S(2)}) async-start(), calls=%async_computation.9 | async-start | bytes 2621440 | tf_op jit(solution)/shard_map/reduce_scatter | solution.py:587
  271.9 100.3 %reduce-scatter.7.cloned.1.call-start = ((), (), s32[]{:S(2)}) async-start(), calls=%async_computation.10 | async-start | bytes 2621440 | tf_op jit(solution)/shard_map/reduce_scatter | solution.py:587
  322.7 24.8 %collective-permute-start.5 = (bf16[1024,1536]{1,0:T(8,128)(2,1)}, bf16[1024,1536]{1,0:T(8,128)(2,1)}, u32[]{:S(2)}, u32[]{:S(2)}) collective-permute-start(bf16[1024,1536]{1,0:T(8,128)(2,1)} %convolution_convert_fusion.1), channel_id=1, source_target_pairs={{0,4},{4,0},{8,12},{12,8},{16,20},{20,16},{24,28},{28,24},{1,5},{5... | collective-permute-start | bytes 9437192 | tf_op jit(solution)/shard_map/ppermute | solution.py:420
  327.6 28.7 %collective-permute-start.4 = (bf16[1024,1536]{1,0:T(8,128)(2,1)}, bf16[1024,1536]{1,0:T(8,128)(2,1)}, u32[]{:S(2)}, u32[]{:S(2)}) collective-permute-start(bf16[1024,1536]{1,0:T(8,128)(2,1)} %convolution_convert_fusion.2), channel_id=1, source_target_pairs={{0,4},{4,0},{8,12},{12,8},{16,20},{20,16},{24,28},{28,24},{1,5},{5... | collective-permute-start | bytes 9437192 | tf_op jit(solution)/shard_map/ppermute | solution.py:420
  328.1 128.6 %all-gather.14.cloned.1.call-start = ((), (), s32[]{:S(2)}) async-start(), calls=%async_computation.11 | async-start | bytes 5242880 | tf_op jit(solution)/shard_map/all_gather | solution.py:609
  336.3 26.5 %collective-permute-start.3 = (bf16[768,2048]{1,0:T(8,128)(2,1)}, bf16[768,2048]{1,0:T(8,128)(2,1)}, u32[]{:S(2)}, u32[]{:S(2)}) collective-permute-start(bf16[768,2048]{1,0:T(8,128)(2,1)} %convolution_convert_fusion.4), channel_id=1, source_target_pairs={{0,4},{4,0},{8,12},{12,8},{16,20},{20,16},{24,28},{28,24},{1,5},{5... | collective-permute-start | bytes 9437192 | tf_op jit(solution)/shard_map/ppermute | solution.py:420
  376.5 213.7 %all-reduce.6.cloned.1.call-start = ((), (), s32[]{:S(2)}) async-start(), calls=%async_computation.14 | async-start | bytes 18874368 | tf_op jit(solution)/shard_map/psum | solution.py:601
  377.0 259.0 %reduce-scatter.9.cloned.1.call-start = ((), (), s32[]{:S(2)}) async-start(), calls=%async_computation.12 | async-start | bytes 5242880 | tf_op jit(solution)/shard_map/reduce_scatter | solution.py:611
  456.7 182.5 %reduce-scatter.11.cloned.1.call-start = ((), (), s32[]{:S(2)}) async-start(), calls=%async_computation.13 | async-start | bytes 5242880 | tf_op jit(solution)/shard_map/reduce_scatter | solution.py:619
  461.7 51.6 %collective-permute-start.9 = (bf16[256,2048]{1,0:T(8,128)(2,1)}, bf16[256,2048]{1,0:T(8,128)(2,1)}, u32[]{:S(2)}, u32[]{:S(2)}) collective-permute-start(bf16[256,2048]{1,0:T(8,128)(2,1)} %convolution_convert_fusion.5), channel_id=1, source_target_pairs={{0,4},{4,0},{8,12},{12,8},{16,20},{20,16},{24,28},{28,24},{1,5},{5... | collective-permute-start | bytes 3145736 | tf_op jit(solution)/shard_map/ppermute | solution.py:420
  500.0 13.1 %collective-permute-start.15 = (f32[4352]{0:T(1024)S(1)}, f32[4352]{0:T(1024)S(1)}, u32[]{:S(2)}, u32[]{:S(2)}) collective-permute-start(f32[4352]{0:T(1024)S(1)} %add.257), channel_id=1, source_target_pairs={{0,8},{4,12},{8,0},{12,4},{16,24},{20,28},{24,16},{28,20},{1,9},{5... | collective-permute-start | bytes 52232 | tf_op jit(solution)/shard_map/ppermute | solution.py:629
  513.2 24.4 %collective-permute-start.10 = (bf16[1024,1024]{1,0:T(8,128)(2,1)}, bf16[1024,1024]{1,0:T(8,128)(2,1)S(1)}, u32[]{:S(2)}, u32[]{:S(2)}) collective-permute-start(bf16[1024,1024]{1,0:T(8,128)(2,1)} %fusion.14), channel_id=1, source_target_pairs={{0,4},{4,0},{8,12},{12,8},{16,20},{20,16},{24,28},{28,24},{1,5},{5... | collective-permute-start | bytes 6291464 | tf_op jit(solution)/shard_map/ppermute | solution.py:420
  519.6 14.6 %collective-permute-start.20 = (bf16[64,2048]{1,0:T(8,128)(2,1)S(1)}, bf16[64,2048]{1,0:T(8,128)(2,1)S(1)}, u32[]{:S(2)}, u32[]{:S(2)}) collective-permute-start(bf16[64,2048]{1,0:T(8,128)(2,1)S(1)} %constant_dynamic-slice_fusion.7), channel_id=1, source_target_pairs={{0,8},{4,12},{8,0},{12,4},{16,24},{20,28},{24,16},{28,20},{1,9},{5... | collective-permute-start | bytes 786440 | tf_op jit(solution)/shard_map/ppermute | solution.py:431
  520.4 14.6 %collective-permute-start.25 = (bf16[64,2048]{1,0:T(8,128)(2,1)S(1)}, bf16[64,2048]{1,0:T(8,128)(2,1)S(1)}, u32[]{:S(2)}, u32[]{:S(2)}) collective-permute-start(bf16[64,2048]{1,0:T(8,128)(2,1)S(1)} %constant_dynamic-slice_fusion.5), channel_id=1, source_target_pairs={{0,16},{4,20},{8,24},{12,28},{16,0},{20,4},{24,8},{28,12},{1,17},{... | collective-permute-start | bytes 786440 | tf_op jit(solution)/shard_map/ppermute | solution.py:431
  535.7 56.9 %collective-permute-start.26 = (bf16[32,2048]{1,0:T(8,128)(2,1)}, bf16[32,2048]{1,0:T(8,128)(2,1)}, u32[]{:S(2)}, u32[]{:S(2)}) collective-permute-start(bf16[32,2048]{1,0:T(8,128)(2,1)} %constant_dynamic-slice_fusion.4), channel_id=1, source_target_pairs={{0,8},{4,12},{8,0},{12,4},{16,24},{20,28},{24,16},{28,20},{1,9},{5... | collective-permute-start | bytes 393224 | tf_op jit(solution)/shard_map/ppermute | solution.py:431
  541.1 49.0 %collective-permute-start.29 = (bf16[256,1024]{1,0:T(8,128)(2,1)}, bf16[256,1024]{1,0:T(8,128)(2,1)S(1)}, u32[]{:S(2)}, u32[]{:S(2)}) collective-permute-start(bf16[256,1024]{1,0:T(8,128)(2,1)} %constant_dynamic-slice_fusion.3), channel_id=1, source_target_pairs={{0,8},{4,12},{8,0},{12,4},{16,24},{20,28},{24,16},{28,20},{1,9},{5... | collective-permute-start | bytes 1572872 | tf_op jit(solution)/shard_map/ppermute | solution.py:431
  542.0 49.7 %collective-permute-start.33 = (bf16[256,1024]{1,0:T(8,128)(2,1)}, bf16[256,1024]{1,0:T(8,128)(2,1)S(1)}, u32[]{:S(2)}, u32[]{:S(2)}) collective-permute-start(bf16[256,1024]{1,0:T(8,128)(2,1)} %constant_dynamic-slice_fusion.1), channel_id=1, source_target_pairs={{0,16},{4,20},{8,24},{12,28},{16,0},{20,4},{24,8},{28,12},{1,17},{... | collective-permute-start | bytes 1572872 | tf_op jit(solution)/shard_map/ppermute | solution.py:431
  590.1 22.3 %collective-permute-start.23 = (bf16[768,2048]{1,0:T(8,128)(2,1)}, bf16[768,2048]{1,0:T(8,128)(2,1)S(1)}, u32[]{:S(2)}, u32[]{:S(2)}) collective-permute-start(bf16[768,2048]{1,0:T(8,128)(2,1)} %get-tuple-element.109.mine_ref), channel_id=1, source_target_pairs={{0,4},{4,0},{8,12},{12,8},{16,20},{20,16},{24,28},{28,24},{1,5},{5... | collective-permute-start | bytes 9437192 | tf_op jit(solution)/shard_map/ppermute | solution.py:467
  591.9 28.3 %collective-permute-start.38 = (bf16[1024,1536]{1,0:T(8,128)(2,1)}, bf16[1024,1536]{1,0:T(8,128)(2,1)S(1)}, u32[]{:S(2)}, u32[]{:S(2)}) collective-permute-start(bf16[1024,1536]{1,0:T(8,128)(2,1)} %get-tuple-element.111.mine_ref), channel_id=1, source_target_pairs={{0,4},{4,0},{8,12},{12,8},{16,20},{20,16},{24,28},{28,24},{1,5},{5... | collective-permute-start | bytes 9437192 | tf_op jit(solution)/shard_map/ppermute | solution.py:467
  592.2 35.1 %collective-permute-start.37 = (bf16[1024,1536]{1,0:T(8,128)(2,1)S(1)}, bf16[1024,1536]{1,0:T(8,128)(2,1)S(1)}, u32[]{:S(2)}, u32[]{:S(2)}) collective-permute-start(bf16[1024,1536]{1,0:T(8,128)(2,1)S(1)} %copy-done.2), channel_id=1, source_target_pairs={{0,4},{4,0},{8,12},{12,8},{16,20},{20,16},{24,28},{28,24},{1,5},{5... | collective-permute-start | bytes 9437192 | tf_op jit(solution)/shard_map/ppermute | solution.py:467
  617.5 15.3 %collective-permute-start.24 = (bf16[64,2048]{1,0:T(8,128)(2,1)S(1)}, bf16[64,2048]{1,0:T(8,128)(2,1)S(1)}, u32[]{:S(2)}, u32[]{:S(2)}) collective-permute-start(bf16[64,2048]{1,0:T(8,128)(2,1)S(1)} %pad_maximum_fusion.6), channel_id=1, source_target_pairs={{0,8},{4,12},{8,0},{12,4},{16,24},{20,28},{24,16},{28,20},{1,9},{5... | collective-permute-start | bytes 786440 | tf_op jit(solution)/shard_map/ppermute | solution.py:436
  618.3 17.3 %collective-permute-start.32 = (bf16[256,1024]{1,0:T(8,128)(2,1)S(1)}, bf16[256,1024]{1,0:T(8,128)(2,1)S(1)}, u32[]{:S(2)}, u32[]{:S(2)}) collective-permute-start(bf16[256,1024]{1,0:T(8,128)(2,1)S(1)} %pad_maximum_fusion.4), channel_id=1, source_target_pairs={{0,8},{4,12},{8,0},{12,4},{16,24},{20,28},{24,16},{28,20},{1,9},{5... | collective-permute-start | bytes 1572872 | tf_op jit(solution)/shard_map/ppermute | solution.py:436
  619.8 15.9 %collective-permute-start.36 = (bf16[256,1024]{1,0:T(8,128)(2,1)S(1)}, bf16[256,1024]{1,0:T(8,128)(2,1)S(1)}, u32[]{:S(2)}, u32[]{:S(2)}) collective-permute-start(bf16[256,1024]{1,0:T(8,128)(2,1)S(1)} %pad_maximum_fusion.5), channel_id=1, source_target_pairs={{0,16},{4,20},{8,24},{12,28},{16,0},{20,4},{24,8},{28,12},{1,17},{... | collective-permute-start | bytes 1572872 | tf_op jit(solution)/shard_map/ppermute | solution.py:436
  620.2 15.2 %collective-permute-start.28 = (bf16[64,2048]{1,0:T(8,128)(2,1)S(1)}, bf16[64,2048]{1,0:T(8,128)(2,1)S(1)}, u32[]{:S(2)}, u32[]{:S(2)}) collective-permute-start(bf16[64,2048]{1,0:T(8,128)(2,1)S(1)} %pad_maximum_fusion.7), channel_id=1, source_target_pairs={{0,16},{4,20},{8,24},{12,28},{16,0},{20,4},{24,8},{28,12},{1,17},{... | collective-permute-start | bytes 786440 | tf_op jit(solution)/shard_map/ppermute | solution.py:436
  (53 other events, 354.5 us)
Sparse Core Ops, SparseCore 0:
  10.4 95.6 all-gather.5
  107.7 80.2 all-gather.7
  190.1 44.4 all-gather.11
  236.5 44.6 all-gather.9
  284.1 42.5 reduce-scatter.4
  328.8 43.4 reduce-scatter.6
  376.6 80.0 all-gather.13
  459.7 76.8 reduce-scatter.8
  539.4 77.2 reduce-scatter.10
Sparse Core Ops, SparseCore 1:
  112.6 125.5 all-reduce.3
  381.3 208.7 all-reduce.5
